TPU v7x, 32 devices: a whole 2x2x4 slice. The times are simulated.
32 devices in a mesh: section: 2 (over z_hi), dp: 8 (over y, x, core), tensor: 2 (over z_lo).
Axes of the slice: x: 2, y: 2, z: 4 (z_hi: 2, z_lo: 2; z = z_hi * 2 + z_lo), core: 2. Of those that a mesh axis runs over, the one named last changes fastest.
Arguments:
- block_input: bfloat16 [2, 1536, 2048], P(None, ('dp', 'tensor')), may hold values from -6 to 6
- segment_ids: int32 [2, 1536], P(None, 'dp'), may hold values from 0 to 2, as said below
- out_cotangent: bfloat16 [2, 1536, 2048], P(None, ('dp', 'tensor')), may hold values from -6 to 6
- attn_norm: float32 [2, 2048], P('section'), may hold values from 0.5 to 1.5
- q_weight: bfloat16 [2, 2048, 2048], P('section', 'dp', 'tensor'), may hold values from -0.125 to 0.125
- k_weight: bfloat16 [2, 2048, 1024], P('section', 'dp', 'tensor'), may hold values from -0.125 to 0.125
- v_weight: bfloat16 [2, 2048, 1024], P('section', 'dp', 'tensor'), may hold values from -0.125 to 0.125
- o_weight: bfloat16 [2, 2048, 2048], P('section', 'tensor', 'dp'), may hold values from -1 to 1
- q_norm: float32 [2, 128], P('section'), may hold values from 0.5 to 1.5
- k_norm: float32 [2, 128], P('section'), may hold values from 0.5 to 1.5
- ffn_norm: float32 [2, 2048], P('section'), may hold values from 0.5 to 1.5
- gate_weight: bfloat16 [2, 2048, 6144], P('section', 'dp', 'tensor'), may hold values from -0.125 to 0.125
- up_weight: bfloat16 [2, 2048, 6144], P('section', 'dp', 'tensor'), may hold values from -0.125 to 0.125
- down_weight: bfloat16 [2, 6144, 2048], P('section', 'tensor', 'dp'), may hold values from -0.078125 to 0.078125
Outputs:
- section_outputs: bfloat16 [2, 2, 1536, 2048], P('section', None, ('dp', 'tensor'))
- section_input_grads: bfloat16 [2, 2, 1536, 2048], P('section', None, ('dp', 'tensor'))
- attn_norm_grad: float32 [2, 2048], P('section')
- q_weight_grad: float32 [2, 2048, 2048], P('section', 'dp', 'tensor')
- k_weight_grad: float32 [2, 2048, 1024], P('section', 'dp', 'tensor')
- v_weight_grad: float32 [2, 2048, 1024], P('section', 'dp', 'tensor')
- o_weight_grad: float32 [2, 2048, 2048], P('section', 'tensor', 'dp')
- q_norm_grad: float32 [2, 128], P('section')
- k_norm_grad: float32 [2, 128], P('section')
- ffn_norm_grad: float32 [2, 2048], P('section')
- gate_weight_grad: float32 [2, 2048, 6144], P('section', 'dp', 'tensor')
- up_weight_grad: float32 [2, 2048, 6144], P('section', 'dp', 'tensor')
- down_weight_grad: float32 [2, 6144, 2048], P('section', 'tensor', 'dp')
Inputs may be any that keep to these rules, and one draw needn't show every extreme that they name: `segment_ids`: each sequence of 192 tokens holds three documents numbered 0, 1, 2 in order; document 1 starts at a position from 24 to 47, and document 2 starts at a position from 144 to 167.
All inputs are finite; a program needn't handle non-finite values.
Results may differ from a plain program's by a relative error of at most 0.03.
Values may be sent and summed in bfloat16 or wider, within the bound.
A program may use at most 384 MiB of HBM per device.

v0:
```python
import jax
import jax.numpy as jnp
from jax import lax
from jax.sharding import PartitionSpec as P

norm_eps = 1e-06
rope_base = 1000000.0
masked_score = -1e30


def from_behind(block, axis, distance):
    devices = range(lax.axis_size(axis))
    route = [(i - distance, i) for i in devices if i - distance in devices]
    return lax.ppermute(block, axis, route)


def inverse_rms(values):
    return lax.rsqrt(jnp.mean(values * values, axis=-1, keepdims=True) + norm_eps)


def rope_tables(length, head_width):
    exponent = jnp.arange(0, head_width, 2).astype(jnp.float32) / head_width
    inverse = rope_base ** (-exponent)
    angles = jnp.arange(length).astype(jnp.float32)[:, None] * inverse[None, :]
    cosine = jnp.cos(angles)
    sine_table = jnp.sin(angles)
    return (
        jnp.concatenate([cosine, cosine], axis=-1),
        jnp.concatenate([sine_table, sine_table], axis=-1),
    )


def rotate_half(values):
    half_width = values.shape[-1] // 2
    return jnp.concatenate([-values[..., half_width:], values[..., :half_width]], axis=-1)


def rotate_back(values):
    half_width = values.shape[-1] // 2
    return jnp.concatenate([values[..., half_width:], -values[..., :half_width]], axis=-1)


def apply_rope(values, cosine, sine_table):
    return values * cosine[:, None, :] + rotate_half(values) * sine_table[:, None, :]


def undo_rope(grad_out, cosine, sine_table):
    return grad_out * cosine[:, None, :] + rotate_back(grad_out * sine_table[:, None, :])


def norm_back(grad_out, values, inverse, gain_vec):
    scaled = grad_out * gain_vec
    return inverse * (
        scaled - values * inverse * inverse * jnp.mean(scaled * values, axis=-1, keepdims=True)
    )


def matmul(left_side, right_side):
    return jnp.dot(left_side, right_side, preferred_element_type=jnp.float32)


def contract_last(left_side, right_side):
    return lax.dot_general(
        left_side, right_side, (((1,), (1,)), ((), ())), preferred_element_type=jnp.float32
    )


def contract_first(left_side, right_side):
    return lax.dot_general(
        left_side, right_side, (((0,), (0,)), ((), ())), preferred_element_type=jnp.float32
    )


def seq_gather(values):
    return lax.all_gather(values, "tensor", axis=0, tiled=True)


def seq_scatter(values):
    return lax.psum_scatter(
        values.astype(jnp.bfloat16), "tensor", scatter_dimension=0, tiled=True
    ).astype(jnp.float32)


def block_mask(segments):
    position = jnp.arange(segments.shape[0])
    return (position[:, None] >= position[None, :]) & (segments[:, None] == segments[None, :])


def attention_forward(query_rot, key_rot, values, segments):
    score_scale = query_rot.shape[-1] ** (-0.5)
    scores = (
        jnp.einsum("qkgd,skd->kgqs", query_rot, key_rot, preferred_element_type=jnp.float32)
        * score_scale
    )
    scores = jnp.where(block_mask(segments), scores, masked_score)
    row_top = jnp.max(scores, axis=-1, keepdims=True)
    exponent = jnp.exp(scores - row_top)
    row_total = jnp.sum(exponent, axis=-1, keepdims=True)
    soft_weights = (exponent / row_total).astype(jnp.bfloat16)
    outputs = jnp.einsum("kgqs,skd->qkgd", soft_weights, values, preferred_element_type=jnp.float32)
    log_parts = row_top + jnp.log(row_total)
    return (outputs.astype(jnp.bfloat16), log_parts)


def attention_backward(query_rot, key_rot, values, segments, log_total, grad_out):
    score_scale = query_rot.shape[-1] ** (-0.5)
    scores = (
        jnp.einsum("qkgd,skd->kgqs", query_rot, key_rot, preferred_element_type=jnp.float32)
        * score_scale
    )
    scores = jnp.where(block_mask(segments), scores, masked_score)
    soft_weights = jnp.exp(scores - log_total)
    grad_soft = jnp.einsum("qkgd,skd->kgqs", grad_out, values, preferred_element_type=jnp.float32)
    row_delta = jnp.sum(soft_weights * grad_soft, axis=-1, keepdims=True)
    grad_scores = (soft_weights * (grad_soft - row_delta)).astype(jnp.bfloat16)
    query_grads = score_scale * jnp.einsum(
        "kgqs,skd->qkgd", grad_scores, key_rot, preferred_element_type=jnp.float32
    )
    key_grad = score_scale * jnp.einsum(
        "kgqs,qkgd->skd", grad_scores, query_rot, preferred_element_type=jnp.float32
    )
    value_grad = jnp.einsum(
        "kgqs,qkgd->skd",
        soft_weights.astype(jnp.bfloat16),
        grad_out,
        preferred_element_type=jnp.float32,
    )
    return (query_grads, key_grad, value_grad)


def layer_forward(hidden_in, segments, gain_set, fetch_attn, fetch_ffn):
    attn_gain, query_gain, key_gain, ffn_gain = gain_set
    hidden = hidden_in.astype(jnp.float32)
    inverse_in = inverse_rms(hidden)
    normed = seq_gather((hidden * inverse_in * attn_gain).astype(jnp.bfloat16))
    w_query, w_key, w_value, w_output = fetch_attn()
    length = normed.shape[0]
    head_width = query_gain.shape[0]
    queries = matmul(normed, w_query).reshape(length, -1, head_width)
    key_raw = matmul(normed, w_key).reshape(length, -1, head_width)
    values = matmul(normed, w_value).astype(jnp.bfloat16).reshape(length, -1, head_width)
    kv_local = key_raw.shape[1]
    group_size = queries.shape[1] // kv_local
    inverse_query = inverse_rms(queries)
    inverse_key = inverse_rms(key_raw)
    cosine, sine_table = rope_tables(length, head_width)
    query_rot = apply_rope(queries * inverse_query * query_gain, cosine, sine_table).astype(
        jnp.bfloat16
    )
    query_rot = query_rot.reshape(length, kv_local, group_size, head_width)
    key_rot = apply_rope(key_raw * inverse_key * key_gain, cosine, sine_table).astype(jnp.bfloat16)
    attended, log_total = attention_forward(query_rot, key_rot, values, segments)
    attended = attended.reshape(length, -1)
    mixed_rows = hidden + seq_scatter(matmul(attended, w_output))
    inverse_mid = inverse_rms(mixed_rows)
    normed_ffn = seq_gather((mixed_rows * inverse_mid * ffn_gain).astype(jnp.bfloat16))
    w_gate, w_up, w_down = fetch_ffn()
    gate_pre = matmul(normed_ffn, w_gate)
    upward = matmul(normed_ffn, w_up)
    activated = (gate_pre * jax.nn.sigmoid(gate_pre) * upward).astype(jnp.bfloat16)
    result = (mixed_rows + seq_scatter(matmul(activated, w_down))).astype(jnp.bfloat16)
    kept_step = (
        hidden_in,
        inverse_in,
        normed,
        queries,
        key_raw,
        inverse_query,
        inverse_key,
        query_rot,
        key_rot,
        values,
        log_total,
        attended,
        mixed_rows,
        inverse_mid,
        normed_ffn,
        gate_pre,
        upward,
        activated,
    )
    return (result, kept_step)


def layer_backward(grad_in, kept_step, segments, gain_set, fetch_attn, fetch_ffn):
    (
        hidden_in,
        inverse_in,
        normed,
        queries,
        key_raw,
        inverse_query,
        inverse_key,
        query_rot,
        key_rot,
        values,
        log_total,
        attended,
        mixed_rows,
        inverse_mid,
        normed_ffn,
        gate_pre,
        upward,
        activated,
    ) = kept_step
    attn_gain, query_gain, key_gain, ffn_gain = gain_set
    w_gate, w_up, w_down = fetch_ffn()
    grad_down = seq_gather(grad_in)
    grad_act = contract_last(grad_down, w_down)
    sigmoid_gate = jax.nn.sigmoid(gate_pre)
    grad_gate = (grad_act * upward * sigmoid_gate * (1.0 + gate_pre * (1.0 - sigmoid_gate))).astype(
        jnp.bfloat16
    )
    grad_upward = (grad_act * gate_pre * sigmoid_gate).astype(jnp.bfloat16)
    grad_normed_ffn = seq_scatter(
        contract_last(grad_gate, w_gate) + contract_last(grad_upward, w_up)
    )
    ffn_gain_grad = jnp.sum(grad_normed_ffn * mixed_rows * inverse_mid, axis=0)
    grad_mixed = grad_in.astype(jnp.float32) + norm_back(
        grad_normed_ffn, mixed_rows, inverse_mid, ffn_gain
    )
    w_query, w_key, w_value, w_output = fetch_attn()
    grad_proj = seq_gather(grad_mixed.astype(jnp.bfloat16))
    grad_attended = contract_last(grad_proj, w_output).astype(jnp.bfloat16)
    length, kv_local, group_size, head_width = query_rot.shape
    grad_query_rot, grad_key_rot, grad_value_sum = attention_backward(
        query_rot,
        key_rot,
        values,
        segments,
        log_total,
        grad_attended.reshape(length, kv_local, group_size, head_width),
    )
    cosine, sine_table = rope_tables(length, head_width)
    grad_query_norm = undo_rope(grad_query_rot.reshape(length, -1, head_width), cosine, sine_table)
    grad_key_norm = undo_rope(grad_key_rot, cosine, sine_table)
    query_gain_grad = jnp.sum(grad_query_norm * queries * inverse_query, axis=(0, 1))
    key_gain_grad = jnp.sum(grad_key_norm * key_raw * inverse_key, axis=(0, 1))
    grad_queries = (
        norm_back(grad_query_norm, queries, inverse_query, query_gain)
        .astype(jnp.bfloat16)
        .reshape(length, -1)
    )
    grad_keys = (
        norm_back(grad_key_norm, key_raw, inverse_key, key_gain)
        .astype(jnp.bfloat16)
        .reshape(length, -1)
    )
    grad_values = grad_value_sum.astype(jnp.bfloat16).reshape(length, -1)
    grad_normed = seq_scatter(
        contract_last(grad_queries, w_query)
        + contract_last(grad_keys, w_key)
        + contract_last(grad_values, w_value)
    )
    hidden = hidden_in.astype(jnp.float32)
    attn_gain_grad = jnp.sum(grad_normed * hidden * inverse_in, axis=0)
    grad_hidden = (grad_mixed + norm_back(grad_normed, hidden, inverse_in, attn_gain)).astype(
        jnp.bfloat16
    )
    saved_step = (
        normed,
        grad_queries,
        grad_keys,
        grad_values,
        attended,
        grad_proj,
        normed_ffn,
        grad_gate,
        grad_upward,
        activated,
        grad_down,
    )
    return (
        grad_hidden,
        saved_step,
        (attn_gain_grad, ffn_gain_grad, query_gain_grad, key_gain_grad),
    )


def per_device(
    block_input,
    segment_ids,
    out_cotangent,
    attn_norm,
    q_weight,
    k_weight,
    v_weight,
    o_weight,
    q_norm,
    k_norm,
    ffn_norm,
    gate_weight,
    up_weight,
    down_weight,
):
    section_index = lax.axis_index("section")
    micro_count = block_input.shape[0]
    step_count = micro_count + 1
    gain_set = (attn_norm[0], q_norm[0], k_norm[0], ffn_norm[0])

    def fetch_attn():
        return (
            lax.all_gather(q_weight[0], "dp", axis=0, tiled=True),
            lax.all_gather(k_weight[0], "dp", axis=0, tiled=True),
            lax.all_gather(v_weight[0], "dp", axis=0, tiled=True),
            lax.all_gather(o_weight[0], "dp", axis=1, tiled=True),
        )

    def fetch_ffn():
        return (
            lax.all_gather(gate_weight[0], "dp", axis=0, tiled=True),
            lax.all_gather(up_weight[0], "dp", axis=0, tiled=True),
            lax.all_gather(down_weight[0], "dp", axis=1, tiled=True),
        )

    zero_rows = jnp.zeros_like(block_input[0])
    received = zero_rows
    results = []
    kept_steps = []
    for step_index in range(step_count):
        own_rows = block_input[step_index] if step_index < micro_count else zero_rows
        hidden_in = jnp.where(section_index == 0, own_rows, received)
        micro_index = jnp.clip(step_index - section_index, 0, micro_count - 1)
        segments = lax.dynamic_index_in_dim(segment_ids, micro_index, 0, keepdims=False)
        result, kept_step = layer_forward(hidden_in, segments, gain_set, fetch_attn, fetch_ffn)
        results.append(result)
        kept_steps.append(kept_step)
        if step_index + 1 < step_count:
            received = from_behind(result, "section", 1)
    kept_all = jax.tree.map(lambda *pieces: jnp.stack(pieces), *kept_steps)
    grad_received = zero_rows
    grads_out = []
    saved_steps = []
    gain_total = None
    for step_index in range(step_count):
        own_rows = out_cotangent[step_index] if step_index < micro_count else zero_rows
        grad_in = jnp.where(section_index == 1, own_rows, grad_received)
        slot_index = jnp.clip(step_index - 1 + 2 * section_index, 0, micro_count)
        kept_step = jax.tree.map(
            lambda stacked: lax.dynamic_index_in_dim(stacked, slot_index, 0, keepdims=False),
            kept_all,
        )
        micro_index = jnp.clip(step_index - 1 + section_index, 0, micro_count - 1)
        segments = lax.dynamic_index_in_dim(segment_ids, micro_index, 0, keepdims=False)
        grad_hidden, saved_step, gain_grads = layer_backward(
            grad_in, kept_step, segments, gain_set, fetch_attn, fetch_ffn
        )
        grads_out.append(grad_hidden)
        saved_steps.append(saved_step)
        gain_total = (
            gain_grads if gain_total is None else jax.tree.map(jnp.add, gain_total, gain_grads)
        )
        if step_index + 1 < step_count:
            grad_received = from_behind(grad_hidden, "section", -1)
    result_stack = jnp.stack(results)
    grad_stack = jnp.stack(grads_out)
    section_outputs = jnp.where(section_index == 0, result_stack[:micro_count], result_stack[1:])[
        None
    ]
    section_input_grads = jnp.where(section_index == 1, grad_stack[:micro_count], grad_stack[1:])[
        None
    ]
    saved_all = tuple((jnp.concatenate(pieces, axis=0) for pieces in zip(*saved_steps)))
    (
        normed_all,
        grad_queries,
        grad_keys,
        grad_values,
        attended_all,
        grad_proj_all,
        normed_ffn_all,
        grad_gate_all,
        grad_up_all,
        activated_all,
        grad_down_all,
    ) = saved_all
    query_side = jnp.concatenate([grad_queries, grad_keys, grad_values], axis=1)
    ffn_side = jnp.concatenate([grad_gate_all, grad_up_all], axis=1)
    reduced = lax.psum_scatter(
        jnp.concatenate(
            [
                contract_first(normed_all, query_side),
                contract_first(normed_ffn_all, ffn_side),
                contract_first(grad_proj_all, attended_all),
                contract_first(grad_down_all, activated_all),
            ],
            axis=1,
        ).astype(jnp.bfloat16),
        "dp",
        scatter_dimension=0,
        tiled=True,
    ).astype(jnp.float32)
    query_width = q_weight.shape[2]
    key_width = k_weight.shape[2]
    unit_width = gate_weight.shape[2]
    widths = [query_width, key_width, key_width, unit_width, unit_width, query_width, unit_width]
    offsets = [0]
    for width_item in widths:
        offsets.append(offsets[-1] + width_item)
    pieces_out = [
        reduced[:, offsets[number] : offsets[number + 1]] for number in range(len(widths))
    ]
    summed = lax.psum(
        (gain_total[0], gain_total[1], gain_total[2], gain_total[3]), ("dp", "tensor")
    )
    return (
        section_outputs,
        section_input_grads,
        summed[0][None],
        pieces_out[0][None],
        pieces_out[1][None],
        pieces_out[2][None],
        pieces_out[5].T[None],
        summed[2][None],
        summed[3][None],
        summed[1][None],
        pieces_out[3][None],
        pieces_out[4][None],
        pieces_out[6].T[None],
    )


def solution(mesh):
    return jax.shard_map(
        per_device,
        mesh=mesh,
        in_specs=(
            P(None, ("dp", "tensor"), None),
            P(None, "dp"),
            P(None, ("dp", "tensor"), None),
            P("section", None),
            P("section", "dp", "tensor"),
            P("section", "dp", "tensor"),
            P("section", "dp", "tensor"),
            P("section", "tensor", "dp"),
            P("section", None),
            P("section", None),
            P("section", None),
            P("section", "dp", "tensor"),
            P("section", "dp", "tensor"),
            P("section", "tensor", "dp"),
        ),
        out_specs=(
            P("section", None, ("dp", "tensor"), None),
            P("section", None, ("dp", "tensor"), None),
            P("section", None),
            P("section", "dp", "tensor"),
            P("section", "dp", "tensor"),
            P("section", "dp", "tensor"),
            P("section", "tensor", "dp"),
            P("section", None),
            P("section", None),
            P("section", None),
            P("section", "dp", "tensor"),
            P("section", "dp", "tensor"),
            P("section", "tensor", "dp"),
        ),
        check_vma=False,
    )
```

profile of v0, /device:TPU:0, one launch (start us, length us, event | category | flops | bytes accessed | tf_op | source)
XLA Modules:
  0.0 1518.7 jit_solution(17317991533811760899)
XLA Ops:
  13.8 12.8 all_gather.38
  26.7 13.9 all-gather.16.cloned.1.call-done
  43.5 26.9 %all-gather.18.cloned.1.call-done = bf16[1,2048,512]{2,1,0:T(8,128)(2,1)} async-done(((bf16[1,256,512]{2,1,0:T(8,128)(2,1)}), bf16[1,2048,512]{2,1,0:T(8,128)(2,1)}) %all-gather.18.cloned.1.call-update) | async-done | bytes 2097168 | tf_op jit(solution)/shard_map/all_gather | solution.py:304
  75.2 33.9 %all-gather.20.cloned.1.call-done = bf16[1,2048,1024]{2,1,0:T(8,128)(2,1)} async-done(((bf16[1,256,1024]{2,1,0:T(8,128)(2,1)}), bf16[1,2048,1024]{2,1,0:T(8,128)(2,1)}) %all-gather.20.cloned.1.call-update) | async-done | bytes 4194320 | tf_op jit(solution)/shard_map/all_gather | solution.py:303
  120.1 28.1 %all-gather.22.cloned.1.call-done = bf16[1,1024,2048]{2,1,0:T(8,128)(2,1)} async-done(((bf16[1,1024,256]{2,1,0:T(8,128)(2,1)}), bf16[1,1024,2048]{2,1,0:T(8,128)(2,1)}) %all-gather.22.cloned.1.call-update) | async-done | bytes 4194320 | tf_op jit(solution)/shard_map/all_gather | solution.py:306
  154.4 15.5 %reduce-scatter.16.cloned.1.call-done = bf16[96,2048]{1,0:T(8,128)(2,1)} async-done(((bf16[192,2048]{1,0:T(8,128)(2,1)}), bf16[96,2048]{1,0:T(8,128)(2,1)}) %reduce-scatter.16.cloned.1.call-update) | async-done | bytes 393232 | tf_op jit(solution)/shard_map/reduce_scatter | solution.py:79
  173.7 11.7 all_gather.43
  185.4 58.5 %all-gather.24.cloned.1.call-done = bf16[1,2048,3072]{2,1,0:T(8,128)(2,1)} async-done(((bf16[1,256,3072]{2,1,0:T(8,128)(2,1)}), bf16[1,2048,3072]{2,1,0:T(8,128)(2,1)}) %all-gather.24.cloned.1.call-update) | async-done | bytes 12582928 | tf_op jit(solution)/shard_map/all_gather | solution.py:311
  252.5 65.6 %all-gather.26.cloned.1.call-done = bf16[1,2048,3072]{2,1,0:T(8,128)(2,1)} async-done(((bf16[1,256,3072]{2,1,0:T(8,128)(2,1)}), bf16[1,2048,3072]{2,1,0:T(8,128)(2,1)}) %all-gather.26.cloned.1.call-update) | async-done | bytes 12582928 | tf_op jit(solution)/shard_map/all_gather | solution.py:312
  327.7 67.1 %all-gather.28.cloned.1.call-done = bf16[1,3072,2048]{2,1,0:T(8,128)(2,1)} async-done(((bf16[1,3072,256]{2,1,0:T(8,128)(2,1)}), bf16[1,3072,2048]{2,1,0:T(8,128)(2,1)}) %all-gather.28.cloned.1.call-update) | async-done | bytes 12582928 | tf_op jit(solution)/shard_map/all_gather | solution.py:313
  403.0 17.6 %reduce-scatter.18.cloned.1.call-done = bf16[96,2048]{1,0:T(8,128)(2,1)} async-done(((bf16[192,2048]{1,0:T(8,128)(2,1)}), bf16[96,2048]{1,0:T(8,128)(2,1)}) %reduce-scatter.18.cloned.1.call-update) | async-done | bytes 393232 | tf_op jit(solution)/shard_map/reduce_scatter | solution.py:79
  435.7 18.2 %all_gather.47 = bf16[192,2048]{1,0:T(8,128)(2,1)S(1)} all-gather(bf16[96,2048]{1,0:T(8,128)(2,1)S(1)} %fusion.294), channel_id=1, replica_groups=mesh['section'=2,'dp'=8,'tensor'=2] {'tensor'}, dimensions={0}, use_global_device_ids=true | all-gather | bytes 1179648 | tf_op jit(solution)/shard_map/all_gather | solution.py:75
  486.9 17.9 %reduce-scatter.20.cloned.1.call-done = bf16[96,2048]{1,0:T(8,128)(2,1)} async-done(((bf16[192,2048]{1,0:T(8,128)(2,1)}), bf16[96,2048]{1,0:T(8,128)(2,1)}) %reduce-scatter.20.cloned.1.call-update) | async-done | bytes 393232 | tf_op jit(solution)/shard_map/reduce_scatter | solution.py:79
  508.6 12.0 all_gather.48
  541.7 15.3 %all-gather.7 = bf16[1,192,2048]{2,1,0:T(8,128)(2,1)} all-gather(bf16[1,96,2048]{2,1,0:T(8,128)(2,1)S(1)} %copy-done.115), channel_id=9, replica_groups=mesh['section'=2,'dp'=8,'tensor'=2] {'tensor'}, dimensions={1}, use_global_device_ids=true | all-gather | bytes 1179648 | tf_op jit(solution)/shard_map/all_gather | solution.py:75
  680.1 11.7 all_gather.50
  763.1 11.7 all_gather.52
  805.3 15.5 %reduce-scatter.30.cloned.1.call-done = bf16[96,2048]{1,0:T(8,128)(2,1)} async-done(((bf16[192,2048]{1,0:T(8,128)(2,1)}), bf16[96,2048]{1,0:T(8,128)(2,1)}) %reduce-scatter.30.cloned.1.call-update) | async-done | bytes 393232 | tf_op jit(solution)/shard_map/reduce_scatter | solution.py:79
  826.2 20.7 %collective-permute-done.2 = bf16[96,2048]{1,0:T(8,128)(2,1)S(1)} collective-permute-done((bf16[96,2048]{1,0:T(8,128)(2,1)S(1)}, bf16[96,2048]{1,0:T(8,128)(2,1)S(1)}, u32[]{:S(2)}, u32[]{:S(2)}) %collective-permute-start.2) | collective-permute-done | bytes 393248 | tf_op jit(solution)/shard_map/ppermute | solution.py:14
  846.9 11.7 all_gather.53
  858.6 11.0 fusion.175
  888.5 14.9 reduce-scatter.32.cloned.1.call-done
  907.1 11.9 all_gather.108
  972.6 17.8 %collective-permute-done.3 = bf16[96,2048]{1,0:T(8,128)(2,1)S(1)} collective-permute-done((bf16[96,2048]{1,0:T(8,128)(2,1)S(1)}, bf16[96,2048]{1,0:T(8,128)(2,1)S(1)}, u32[]{:S(2)}, u32[]{:S(2)}) %collective-permute-start.3) | collective-permute-done | bytes 393248 | tf_op jit(solution)/shard_map/ppermute | solution.py:14
  990.5 11.7 all_gather.109
  1052.0 27.4 %convolution_convert_fusion = bf16[2048,6144]{1,0:T(8,128)(2,1)} fusion(bf16[192,3072]{1,0:T(8,128)(2,1)} %copy-done.221, bf16[192,3072]{1,0:T(8,128)(2,1)} %copy-done.220, bf16[192,3072]{1,0:T(8,128)(2,1)} %copy-done.219, bf16[192,3072]{1,0:T(8,128)(2,1)} %copy-done.218, bf16[192,3072]{1,0:T(8,128)(2,1)} %copy-done.217, bf16[192,3072]{1,0:T(8,128)(2,1)} %copy-done.216, ...), kind=kOutput, calls=%fused_computation.1 | convolution fusion | flops 14557642752 | bytes 34603008 | tf_op jit(solution)/shard_map/dot_general | solution.py:69
  1079.4 15.3 %convolution_convert_fusion.1 = bf16[2048,3072]{1,0:T(8,128)(2,1)} fusion(bf16[192,3072]{1,0:T(8,128)(2,1)} %get-tuple-element.159, bf16[192,3072]{1,0:T(8,128)(2,1)} %get-tuple-element.160, bf16[192,3072]{1,0:T(8,128)(2,1)} %get-tuple-element.158, bf16[192,2048]{1,0:T(8,128)(2,1)} %copy-done.146, bf16[192,2048]{1,0:T(8,128)(2,1)} %copy-done.144, ...), kind=kOutput, calls=%fused_computation.38 | convolution fusion | flops 7271743488 | bytes 18481152 | tf_op jit(solution)/shard_map/dot_general | solution.py:69
  1133.2 19.5 %convolution_convert_fusion.2 = bf16[2048,2048]{0,1:T(8,128)(2,1)} fusion(bf16[192,2048]{1,0:T(8,128)(2,1)S(1)} %copy-done.150, bf16[192,2048]{1,0:T(8,128)(2,1)S(1)} %copy-done.151, bf16[192,2048]{1,0:T(8,128)(2,1)S(1)} %copy-done.149, bf16[192,512]{1,0:T(8,128)(2,1)S(1)} %bitcast.1085, bf16[192,512]{1,0:T(8,128)(2,1)S(1)} %bitcast.1083, ...), kind=kOutput, calls=%fused_computation.39 | convolution fusion | flops 4864344064 | bytes 13107200 | tf_op jit(solution)/shard_map/dot_general | solution.py:69
  1152.8 12.3 copy.571
  1178.5 33.5 %pad_maximum_fusion = bf16[2048,12288]{1,0:T(8,128)(2,1)} fusion(bf16[2048,3072]{1,0:T(8,128)(2,1)} %convolution_convert_fusion.1, bf16[2048,1024]{1,0:T(8,128)(2,1)} %convolution_convert_fusion.3, bf16[2048,6144]{1,0:T(8,128)(2,1)} %convolution_convert_fusion, bf16[2048,2048]{1,0:T(8,128)(2,1)} %copy.571), kind=kLoop, calls=%fused_computation | loop fusion | flops 201326592 | bytes 100663296 | tf_op jit(solution)/shard_map/concatenate | solution.py:380
  1218.1 51.5 %all-reduce.1 = (f32[1,2048]{1,0:T(1,128)}, f32[1,128]{1,0:T(1,128)}, f32[1,128]{1,0:T(1,128)}, f32[1,2048]{1,0:T(1,128)}) all-reduce(f32[1,2048]{1,0:T(1,128)S(1)} %bitcast.1113, f32[1,128]{1,0:T(1,128)S(1)} %add_bitcast_fusion.4, ...), channel_id=1, replica_groups=mesh['section'=2,'dp'=8,'tensor'=2] {'dp','tensor'}, use_global_device_ids=true, to_apply=%region_48.49 | all-reduce | flops 4352 | bytes 34816 | tf_op jit(solution)/shard_map/psum | solution.py:403
  1272.6 223.9 %reduce-scatter.40.cloned.1.call-done = bf16[256,12288]{1,0:T(8,128)(2,1)} async-done(((bf16[2048,12288]{1,0:T(8,128)(2,1)}), bf16[256,12288]{1,0:T(8,128)(2,1)}) %reduce-scatter.40.cloned.1.call-update) | async-done | bytes 6291472
  (816 shorter events, 564.3 us)
Async XLA Ops:
  7.2 33.4 %all-gather.16.cloned.1.call-start = ((), (), s32[]{:S(2)}) async-start(), calls=%async_computation.25 | async-start | bytes 2359296 | tf_op jit(solution)/shard_map/all_gather | solution.py:305
  7.9 62.4 %all-gather.18.cloned.1.call-start = ((), (), s32[]{:S(2)}) async-start(), calls=%async_computation.26 | async-start | bytes 2359296 | tf_op jit(solution)/shard_map/all_gather | solution.py:304
  8.7 100.3 %all-gather.20.cloned.1.call-start = ((), (), s32[]{:S(2)}) async-start(), calls=%async_computation.27 | async-start | bytes 4718592 | tf_op jit(solution)/shard_map/all_gather | solution.py:303
  9.4 138.8 %all-gather.22.cloned.1.call-start = ((), (), s32[]{:S(2)}) async-start(), calls=%async_computation.28 | async-start | bytes 4718592 | tf_op jit(solution)/shard_map/all_gather | solution.py:306
  10.0 159.9 %reduce-scatter.16.cloned.1.call-start = ((), (), s32[]{:S(2)}) async-start(), calls=%async_computation.13 | async-start | bytes 1179648 | tf_op jit(solution)/shard_map/reduce_scatter | solution.py:79
  13.0 407.5 %copy-start.19 = (bf16[1,96,2048]{2,1,0:T(8,128)(2,1)}, bf16[1,96,2048]{2,1,0:T(8,128)(2,1)S(1)}, u32[]{:S(2)}) copy-start(bf16[1,96,2048]{2,1,0:T(8,128)(2,1)S(1)} %get-tuple-element.144) | copy-start | bytes 1179652
  26.6 82.4 %copy-start.10 = (bf16[192,2048]{1,0:T(8,128)(2,1)}, bf16[192,2048]{1,0:T(8,128)(2,1)S(1)}, u32[]{:S(2)}) copy-start(bf16[192,2048]{1,0:T(8,128)(2,1)S(1)} %all_gather.38) | copy-start | bytes 2359300
  152.3 91.7 %all-gather.24.cloned.1.call-start = ((), (), s32[]{:S(2)}) async-start(), calls=%async_computation.29 | async-start | bytes 14155776 | tf_op jit(solution)/shard_map/all_gather | solution.py:311
  152.9 165.3 %all-gather.26.cloned.1.call-start = ((), (), s32[]{:S(2)}) async-start(), calls=%async_computation.30 | async-start | bytes 14155776 | tf_op jit(solution)/shard_map/all_gather | solution.py:312
  153.6 241.1 %all-gather.28.cloned.1.call-start = ((), (), s32[]{:S(2)}) async-start(), calls=%async_computation.31 | async-start | bytes 14155776 | tf_op jit(solution)/shard_map/all_gather | solution.py:313
  154.4 266.1 %reduce-scatter.18.cloned.1.call-start = ((), (), s32[]{:S(2)}) async-start(), calls=%async_computation.14 | async-start | bytes 1179648 | tf_op jit(solution)/shard_map/reduce_scatter | solution.py:79
  185.4 132.7 %copy-start.76 = (bf16[192,2048]{1,0:T(8,128)(2,1)}, bf16[192,2048]{1,0:T(8,128)(2,1)S(1)}, u32[]{:S(2)}) copy-start(bf16[192,2048]{1,0:T(8,128)(2,1)S(1)} %all_gather.43) | copy-start | bytes 2359300
  327.7 75.2 %copy-start.127 = (bf16[192,3072]{1,0:T(8,128)(2,1)}, bf16[192,3072]{1,0:T(8,128)(2,1)S(1)}, u32[]{:S(2)}) copy-start(bf16[192,3072]{1,0:T(8,128)(2,1)S(1)} %get-tuple-element.274) | copy-start | bytes 3538948
  402.9 101.9 %reduce-scatter.20.cloned.1.call-start = ((), (), s32[]{:S(2)}) async-start(), calls=%async_computation.15 | async-start | bytes 1179648 | tf_op jit(solution)/shard_map/reduce_scatter | solution.py:79
  421.8 12.9 collective-permute-start
  434.9 144.9 %copy-start.21 = (bf16[96,2048]{1,0:T(8,128)(2,1)}, bf16[96,2048]{1,0:T(8,128)(2,1)S(1)}, u32[]{:S(2)}) copy-start(bf16[96,2048]{1,0:T(8,128)(2,1)S(1)} %get-tuple-element.142) | copy-start | bytes 1179652
  485.1 94.7 %reduce-scatter.22.cloned.1.call-start = ((), (), s32[]{:S(2)}) async-start(), calls=%async_computation.16 | async-start | bytes 1179648 | tf_op jit(solution)/shard_map/reduce_scatter | solution.py:79
  541.6 134.7 %reduce-scatter.24.cloned.1.call-start = ((), (), s32[]{:S(2)}) async-start(), calls=%async_computation.17 | async-start | bytes 1179648 | tf_op jit(solution)/shard_map/reduce_scatter | solution.py:79
  581.8 14.4 collective-permute-start.1
  596.1 207.9 %copy-start.16 = (bf16[96,2048]{1,0:T(8,128)(2,1)}, bf16[96,2048]{1,0:T(8,128)(2,1)S(1)}, u32[]{:S(2)}) copy-start(bf16[96,2048]{1,0:T(8,128)(2,1)S(1)} %collective-permute-done.1) | copy-start | bytes 1179652
  656.8 101.9 %reduce-scatter.28.cloned.1.call-start = ((), (), s32[]{:S(2)}) async-start(), calls=%async_computation.19 | async-start | bytes 1179648 | tf_op jit(solution)/shard_map/reduce_scatter | solution.py:79
  741.1 79.7 %reduce-scatter.30.cloned.1.call-start = ((), (), s32[]{:S(2)}) async-start(), calls=%async_computation.20 | async-start | bytes 1179648 | tf_op jit(solution)/shard_map/reduce_scatter | solution.py:79
  803.2 100.2 %reduce-scatter.32.cloned.1.call-start = ((), (), s32[]{:S(2)}) async-start(), calls=%async_computation.21 | async-start | bytes 1179648 | tf_op jit(solution)/shard_map/reduce_scatter | solution.py:79
  824.9 22.0 %collective-permute-start.2 = (bf16[96,2048]{1,0:T(8,128)(2,1)S(1)}, bf16[96,2048]{1,0:T(8,128)(2,1)S(1)}, u32[]{:S(2)}, u32[]{:S(2)}) collective-permute-start(bf16[96,2048]{1,0:T(8,128)(2,1)S(1)} %fusion.282), channel_id=1, source_target_pairs={{16,0},{17,1},{18,2},{19,3},{20,4},{21,5},{22,6},{23,7},{24,8},{25... | collective-permute-start | bytes 1179656 | tf_op jit(solution)/shard_map/ppermute | solution.py:14
  846.9 58.7 %copy-start.51 = (bf16[96,2048]{1,0:T(8,128)(2,1)}, bf16[96,2048]{1,0:T(8,128)(2,1)S(1)}, u32[]{:S(2)}) copy-start(bf16[96,2048]{1,0:T(8,128)(2,1)S(1)} %bitcast_select_fusion.6) | copy-start | bytes 1179652
  887.6 77.5 %reduce-scatter.34.cloned.1.call-start = ((), (), s32[]{:S(2)}) async-start(), calls=%async_computation.22 | async-start | bytes 1179648 | tf_op jit(solution)/shard_map/reduce_scatter | solution.py:79
  946.4 148.3 %reduce-scatter.36.cloned.1.call-start = ((), (), s32[]{:S(2)}) async-start(), calls=%async_computation.23 | async-start | bytes 1179648 | tf_op jit(solution)/shard_map/reduce_scatter | solution.py:79
  969.1 21.3 %collective-permute-start.3 = (bf16[96,2048]{1,0:T(8,128)(2,1)S(1)}, bf16[96,2048]{1,0:T(8,128)(2,1)S(1)}, u32[]{:S(2)}, u32[]{:S(2)}) collective-permute-start(bf16[96,2048]{1,0:T(8,128)(2,1)S(1)} %fusion.276), channel_id=1, source_target_pairs={{16,0},{17,1},{18,2},{19,3},{20,4},{21,5},{22,6},{23,7},{24,8},{25... | collective-permute-start | bytes 1179656 | tf_op jit(solution)/shard_map/ppermute | solution.py:14
  1031.1 181.2 %reduce-scatter.26.cloned.1.call-start = ((), (), s32[]{:S(2)}) async-start(), calls=%async_computation.18 | async-start | bytes 1179648 | tf_op jit(solution)/shard_map/reduce_scatter | solution.py:79
  1045.1 171.6 %reduce-scatter.38.cloned.1.call-start = ((), (), s32[]{:S(2)}) async-start(), calls=%async_computation.24 | async-start | bytes 1179648 | tf_op jit(solution)/shard_map/reduce_scatter | solution.py:79
  1171.2 325.2 %reduce-scatter.40.cloned.1.call-start = ((), (), s32[]{:S(2)}) async-start(), calls=%async_computation.32 | async-start | bytes 56623104
  1212.2 57.3 %copy-start.68 = (bf16[96,2048]{1,0:T(8,128)(2,1)S(1)}, bf16[96,2048]{1,0:T(8,128)(2,1)}, u32[]{:S(2)}) copy-start(bf16[96,2048]{1,0:T(8,128)(2,1)} %reduce-scatter.36.cloned.1.call-done) | copy-start | bytes 1179652
  (220 other events, 1592.6 us)
Sparse Core Ops, SparseCore 0:
  9.9 30.5 all-gather.15
  42.4 27.8 all-gather.17
  72.3 36.7 all-gather.19
  110.7 37.4 all-gather.21
  152.4 17.4 reduce-scatter.15
  171.8 72.1 all-gather.23
  246.0 72.1 all-gather.25
  320.2 74.5 all-gather.27
  403.0 17.4 reduce-scatter.17
  485.2 19.5 reduce-scatter.19
  541.7 20.0 reduce-scatter.21
  656.9 19.3 reduce-scatter.23
  741.2 17.4 reduce-scatter.27
  803.3 17.4 reduce-scatter.29
  887.7 15.6 reduce-scatter.31
  946.5 17.4 reduce-scatter.33
  1031.2 15.4 reduce-scatter.35
  1049.4 17.4 reduce-scatter.25
  1171.3 15.7 reduce-scatter.37
  1212.2 284.1 reduce-scatter.39
where the time goes:
time: 1530 us; the launch traced here: 1520 us
  waiting for transfers between devices  660 us (43%)
  matrix products  293 us (19%)
  blocking collectives  200 us (13%)
  other arithmetic  168 us (11%)
  local copies, waits for them, and re-layouts  166 us (11%)
  between operations  17.5 us (1%)
    unnamed x21, waiting for transfers between devices  229 us
    all_gather x12, blocking collectives, seq_gather(): return lax.all_gather(values, 'tensor', axis=0, tiled=True)  149 us
    dot_general x21, matrix products, contract_last(): lax.dot_general(left_side, right_side, (((1,), (1,)), ((), ())), preferre...  108 us
    dot_general x21, matrix products, matmul(): return jnp.dot(left_side, right_side, preferred_element_type=jnp.float32)  97.1 us
    reduce_scatter x12, waiting for transfers between devices, seq_scatter(): lax.psum_scatter(values.astype(jnp.bfloat16), 'tensor', scatter_dimension...  90.6 us
    dot_general x4, matrix products, contract_first(): lax.dot_general(left_side, right_side, (((0,), (0,)), ((), ())), preferre...  69.2 us
    all_gather x1, waiting for transfers between devices, fetch_ffn(): lax.all_gather(down_weight[0], 'dp', axis=1, tiled=True)  67.1 us
    all_gather x1, waiting for transfers between devices, fetch_ffn(): lax.all_gather(up_weight[0], 'dp', axis=0, tiled=True)  65.6 us
  transfers between devices with their start and end apart: 24, of which 18 were waited for; matrix products, arithmetic and copies ran while one was open for 20% of the time, Pallas kernels for 0%

commit v1 on v0

v1 whole, which is shorter than its diff:
```python
import functools

import jax
import jax.numpy as jnp
from jax import lax
from jax.experimental import pallas as pl
from jax.experimental.pallas import tpu as pltpu
from jax.sharding import PartitionSpec as P

norm_eps = 1e-06
rope_base = 1000000.0
masked_score = -1e30
f32 = jnp.float32
bf16 = jnp.bfloat16
MIB = 1024 * 1024


def dot_nn(left, right):
    return lax.dot_general(left, right, (((1,), (0,)), ((), ())), preferred_element_type=f32)


def dot_nt(left, right):
    return lax.dot_general(left, right, (((1,), (1,)), ((), ())), preferred_element_type=f32)


def dot_tn(left, right):
    return lax.dot_general(left, right, (((0,), (0,)), ((), ())), preferred_element_type=f32)


def inverse_rms(values):
    return lax.rsqrt(jnp.mean(values * values, axis=-1, keepdims=True) + norm_eps)


def norm_back(grad_out, values, inverse, gain_vec):
    scaled = grad_out * gain_vec
    return inverse * (
        scaled - values * inverse * inverse * jnp.mean(scaled * values, axis=-1, keepdims=True)
    )


def rotated(raw, gain, cosine, signed_sine):
    inverse = inverse_rms(raw)
    scaled = raw * inverse * gain
    turned = scaled * cosine + pltpu.roll(scaled, 64, 1) * signed_sine
    return inverse, turned.astype(bf16)


def softmax_rows(query_rot, key_rot, allowed, scale):
    scores = jnp.where(allowed, dot_nt(query_rot, key_rot) * scale, masked_score)
    exponent = jnp.exp(scores - jnp.max(scores, axis=-1, keepdims=True))
    return exponent / jnp.sum(exponent, axis=-1, keepdims=True)


def attn_forward_kernel(
    group, width, normed, w_q, w_k, w_v, w_o, gains, cosine, signed_sine, mask,
    queries, keys, values, attended, partial, total,
):
    rows = normed[...]
    raw_q = dot_nn(rows, w_q[...])
    raw_k = dot_nn(rows, w_k[...])
    value = dot_nn(rows, w_v[...]).astype(bf16)
    queries[...] = raw_q
    keys[...] = raw_k
    values[...] = value
    cos, sin = cosine[...], signed_sine[...]
    allowed = mask[...] > 0.5
    _, key_rot = rotated(raw_k, gains[1:2, :], cos, sin)
    scale = width ** (-0.5)
    heads = []
    for head in range(group):
        _, query_rot = rotated(raw_q[:, head * width : (head + 1) * width], gains[0:1, :], cos, sin)
        weights = softmax_rows(query_rot, key_rot, allowed, scale)
        heads.append(dot_nn(weights.astype(bf16), value).astype(bf16))
    mixed = jnp.concatenate(heads, axis=1)
    attended[...] = mixed
    product = dot_nt(mixed, w_o[...])
    step = pl.program_id(0)

    @pl.when(step == 0)
    def _():
        total[...] = product

    @pl.when(step > 0)
    def _():
        total[...] += product

    @pl.when(step == pl.num_programs(0) - 1)
    def _():
        partial[...] = total[...].astype(bf16)


def attn_backward_kernel(
    group, width, grad_proj, queries, keys, values, w_q, w_k, w_v, w_o, gains, cosine, signed_sine,
    mask, grads, gain_grads, partial, total,
):
    step = pl.program_id(0)
    cos, sin = cosine[...], signed_sine[...]
    allowed = mask[...] > 0.5
    scale = width ** (-0.5)
    gain_q, gain_k = gains[0:1, :], gains[1:2, :]
    grad_attended = dot_nn(grad_proj[...], w_o[...]).astype(bf16)
    raw_k, value = keys[...], values[...]
    inverse_k, key_rot = rotated(raw_k, gain_k, cos, sin)
    grad_key = jnp.zeros_like(raw_k)
    grad_value = jnp.zeros_like(raw_k)
    gain_q_sum = jnp.zeros((1, width), f32)
    parts = []
    for head in range(group):
        raw_q = queries[:, head * width : (head + 1) * width]
        grad_head = grad_attended[:, head * width : (head + 1) * width]
        inverse_q, query_rot = rotated(raw_q, gain_q, cos, sin)
        weights = softmax_rows(query_rot, key_rot, allowed, scale)
        grad_weights = dot_nt(grad_head, value)
        delta = jnp.sum(weights * grad_weights, axis=-1, keepdims=True)
        grad_scores = (weights * (grad_weights - delta)).astype(bf16)
        grad_value += dot_tn(weights.astype(bf16), grad_head)
        grad_key += dot_tn(grad_scores, query_rot)
        grad_query = dot_nn(grad_scores, key_rot) * scale
        grad_query = grad_query * cos - pltpu.roll(grad_query, 64, 1) * sin
        gain_q_sum += jnp.sum(grad_query * raw_q * inverse_q, axis=0, keepdims=True)
        parts.append(norm_back(grad_query, raw_q, inverse_q, gain_q).astype(bf16))
    grad_key = grad_key * scale
    grad_key = grad_key * cos - pltpu.roll(grad_key, 64, 1) * sin
    gain_k_sum = jnp.sum(grad_key * raw_k * inverse_k, axis=0, keepdims=True)
    grad_q = jnp.concatenate(parts, axis=1)
    grad_k = norm_back(grad_key, raw_k, inverse_k, gain_k).astype(bf16)
    grad_v = grad_value.astype(bf16)
    grads[0, :, :] = jnp.concatenate([grad_q, grad_k, grad_v], axis=1)
    sums = jnp.concatenate([gain_q_sum, gain_k_sum, jnp.zeros((6, width), f32)], axis=0)
    product = dot_nt(grad_q, w_q[...]) + dot_nt(grad_k, w_k[...]) + dot_nt(grad_v, w_v[...])

    @pl.when(step == 0)
    def _():
        total[...] = product
        gain_grads[...] = sums

    @pl.when(step > 0)
    def _():
        total[...] += product
        gain_grads[...] += sums

    @pl.when(step == pl.num_programs(0) - 1)
    def _():
        partial[...] = total[...].astype(bf16)


def ffn_forward_kernel(normed, w_gate, w_up, w_down, gate, upward, activated, partial, total):
    step = pl.program_id(0)
    rows = normed[...]
    gate_block = dot_nn(rows, w_gate[...])
    up_block = dot_nn(rows, w_up[...])
    gate[...] = gate_block
    upward[...] = up_block
    active = (gate_block * jax.nn.sigmoid(gate_block) * up_block).astype(bf16)
    activated[...] = active
    product = dot_nt(active, w_down[...])

    @pl.when(step == 0)
    def _():
        total[...] = product

    @pl.when(step > 0)
    def _():
        total[...] += product

    @pl.when(step == pl.num_programs(0) - 1)
    def _():
        partial[...] = total[...].astype(bf16)


def ffn_backward_kernel(grad_down, gate, upward, w_gate, w_up, w_down, grads, partial, total):
    step = pl.program_id(0)
    grad_act = dot_nn(grad_down[...], w_down[...])
    gate_block, up_block = gate[...], upward[...]
    sig = jax.nn.sigmoid(gate_block)
    grad_gate = (grad_act * up_block * sig * (1.0 + gate_block * (1.0 - sig))).astype(bf16)
    grad_up = (grad_act * gate_block * sig).astype(bf16)
    grads[0, :, :] = grad_gate
    grads[1, :, :] = grad_up
    product = dot_nt(grad_gate, w_gate[...]) + dot_nt(grad_up, w_up[...])

    @pl.when(step == 0)
    def _():
        total[...] = product

    @pl.when(step > 0)
    def _():
        total[...] += product

    @pl.when(step == pl.num_programs(0) - 1)
    def _():
        partial[...] = total[...].astype(bf16)


def weight_grad_kernel(left_t, right, out):
    out[...] = dot_nn(left_t[0], right[0]).astype(bf16)


def whole(shape):
    return pl.BlockSpec(shape, lambda step: (0,) * len(shape))


def columns(rows, width, first):
    return pl.BlockSpec((rows, width), lambda step: (0, first + step))


def params(mib):
    return pltpu.CompilerParams(
        dimension_semantics=("arbitrary",), vmem_limit_bytes=mib * MIB
    )


def cost(flops, size):
    return pl.CostEstimate(flops=int(flops), bytes_accessed=int(size), transcendentals=0)


def attn_forward(normed, pack, gains, tables, mask):
    length, depth = normed.shape
    width = gains.shape[1]
    q_width = pack.shape[1] // 3
    kv_heads = q_width // 2 // width
    group = q_width // width // kv_heads
    blk = group * width
    return pl.pallas_call(
        functools.partial(attn_forward_kernel, group, width),
        grid=(kv_heads,),
        in_specs=[
            whole((length, depth)),
            columns(depth, blk, 0),
            columns(depth, width, q_width // width),
            columns(depth, width, q_width // width + kv_heads),
            columns(depth, blk, 2 * q_width // blk),
            whole(gains.shape),
            whole((length, width)),
            whole((length, width)),
            whole((length, length)),
        ],
        out_specs=[
            columns(length, blk, 0),
            columns(length, width, 0),
            columns(length, width, 0),
            columns(length, blk, 0),
            whole((length, depth)),
        ],
        out_shape=[
            jax.ShapeDtypeStruct((length, q_width), f32),
            jax.ShapeDtypeStruct((length, q_width // 2), f32),
            jax.ShapeDtypeStruct((length, q_width // 2), bf16),
            jax.ShapeDtypeStruct((length, q_width), bf16),
            jax.ShapeDtypeStruct((length, depth), bf16),
        ],
        scratch_shapes=[pltpu.VMEM((length, depth), f32)],
        compiler_params=params(32),
        cost_estimate=cost(2 * length * depth * pack.shape[1], pack.size * 2),
        name="attn_forward",
    )(normed, pack, pack, pack, pack, gains, *tables, mask)


def attn_backward(grad_proj, queries, keys, values, pack, gains, tables, mask):
    length, depth = grad_proj.shape
    width = gains.shape[1]
    q_width = pack.shape[1] // 3
    kv_heads = q_width // 2 // width
    group = q_width // width // kv_heads
    blk = group * width
    return pl.pallas_call(
        functools.partial(attn_backward_kernel, group, width),
        grid=(kv_heads,),
        in_specs=[
            whole((length, depth)),
            columns(length, blk, 0),
            columns(length, width, 0),
            columns(length, width, 0),
            columns(depth, blk, 0),
            columns(depth, width, q_width // width),
            columns(depth, width, q_width // width + kv_heads),
            columns(depth, blk, 2 * q_width // blk),
            whole(gains.shape),
            whole((length, width)),
            whole((length, width)),
            whole((length, length)),
        ],
        out_specs=[
            pl.BlockSpec((1, length, blk + 2 * width), lambda step: (step, 0, 0)),
            whole((8, width)),
            whole((length, depth)),
        ],
        out_shape=[
            jax.ShapeDtypeStruct((kv_heads, length, blk + 2 * width), bf16),
            jax.ShapeDtypeStruct((8, width), f32),
            jax.ShapeDtypeStruct((length, depth), bf16),
        ],
        scratch_shapes=[pltpu.VMEM((length, depth), f32)],
        compiler_params=params(32),
        cost_estimate=cost(2 * length * depth * pack.shape[1], pack.size * 2),
        name="attn_backward",
    )(grad_proj, queries, keys, values, pack, pack, pack, pack, gains, *tables, mask)


def unit_block(units):
    return 512 if units % 512 == 0 else 256


def ffn_forward(normed, pack):
    length, depth = normed.shape
    units = pack.shape[1] // 3
    blk = unit_block(units)
    steps = units // blk
    return pl.pallas_call(
        ffn_forward_kernel,
        grid=(steps,),
        in_specs=[
            whole((length, depth)),
            columns(depth, blk, 0),
            columns(depth, blk, steps),
            columns(depth, blk, 2 * steps),
        ],
        out_specs=[
            columns(length, blk, 0),
            columns(length, blk, 0),
            columns(length, blk, 0),
            whole((length, depth)),
        ],
        out_shape=[
            jax.ShapeDtypeStruct((length, units), f32),
            jax.ShapeDtypeStruct((length, units), f32),
            jax.ShapeDtypeStruct((length, units), bf16),
            jax.ShapeDtypeStruct((length, depth), bf16),
        ],
        scratch_shapes=[pltpu.VMEM((length, depth), f32)],
        compiler_params=params(40),
        cost_estimate=cost(2 * length * depth * pack.shape[1], pack.size * 2),
        name="ffn_forward",
    )(normed, pack, pack, pack)


def ffn_backward(grad_down, gate, upward, pack):
    length, depth = grad_down.shape
    units = pack.shape[1] // 3
    blk = unit_block(units)
    steps = units // blk
    return pl.pallas_call(
        ffn_backward_kernel,
        grid=(steps,),
        in_specs=[
            whole((length, depth)),
            columns(length, blk, 0),
            columns(length, blk, 0),
            columns(depth, blk, 0),
            columns(depth, blk, steps),
            columns(depth, blk, 2 * steps),
        ],
        out_specs=[
            pl.BlockSpec((2, length, blk), lambda step: (0, 0, step)),
            whole((length, depth)),
        ],
        out_shape=[
            jax.ShapeDtypeStruct((2, length, units), bf16),
            jax.ShapeDtypeStruct((length, depth), bf16),
        ],
        scratch_shapes=[pltpu.VMEM((length, depth), f32)],
        compiler_params=params(40),
        cost_estimate=cost(2 * length * depth * pack.shape[1], pack.size * 2),
        name="ffn_backward",
    )(grad_down, gate, upward, pack, pack, pack)


def weight_grad(left_t, right, which):
    _, depth, tokens = left_t.shape
    count, _, width = right.shape
    blk = unit_block(width)
    per = width // blk
    return pl.pallas_call(
        weight_grad_kernel,
        grid=(count * per,),
        in_specs=[
            pl.BlockSpec((1, depth, tokens), lambda step: (which(step // per), 0, 0)),
            pl.BlockSpec((1, tokens, blk), lambda step: (step // per, 0, step % per)),
        ],
        out_specs=pl.BlockSpec((depth, blk), lambda step: (0, step)),
        out_shape=jax.ShapeDtypeStruct((depth, count * width), bf16),
        compiler_params=params(40),
        cost_estimate=cost(
            2 * depth * tokens * count * width, depth * count * width * 2 + right.size * 2
        ),
        name="weight_grad",
    )(left_t, right)


def rope_tables(position, head_width):
    exponent = jnp.arange(0, head_width, 2).astype(f32) / head_width
    inverse = rope_base ** (-exponent)
    angles = position.astype(f32)[:, None] * inverse[None, :]
    cosine, sine = jnp.cos(angles), jnp.sin(angles)
    return (
        jnp.concatenate([cosine, cosine], axis=-1),
        jnp.concatenate([-sine, sine], axis=-1),
    )


def per_device(
    block_input,
    segment_ids,
    out_cotangent,
    attn_norm,
    q_weight,
    k_weight,
    v_weight,
    o_weight,
    q_norm,
    k_norm,
    ffn_norm,
    gate_weight,
    up_weight,
    down_weight,
):
    section = lax.axis_index("section")
    place = lax.axis_index("dp")
    core = place % 2
    half = lax.axis_index("tensor")
    n_dp = lax.axis_size("dp")
    n_chip = n_dp // 2
    micro_count, own_rows, depth = block_input.shape
    quarter = own_rows // 2
    length = 2 * own_rows
    head_width = q_norm.shape[1]
    first_core = core == 0
    swap_core = [(i, i ^ 1) for i in range(n_dp)]
    swap_half = [(0, 1), (1, 0)]
    chip_groups = [[2 * chip + one for chip in range(n_chip)] for one in (0, 1)]

    def to_core(values):
        return lax.ppermute(values, "dp", swap_core)

    def to_half(values):
        return lax.ppermute(values, "tensor", swap_half)

    def split_columns(weight):
        side = weight.shape[1] // 2
        left, right = weight[:, :side], weight[:, side:]
        return jnp.where(first_core, left, right), jnp.where(first_core, right, left)

    def split_rows(weight):
        side = weight.shape[0] // 2
        left, right = weight[:side].T, weight[side:].T
        return jnp.where(first_core, left, right), jnp.where(first_core, right, left)

    def gathered(pairs):
        mine = jnp.concatenate([pair[0] for pair in pairs], axis=1)
        theirs = to_core(jnp.concatenate([pair[1] for pair in pairs], axis=1))
        chip_block = jnp.concatenate(
            [jnp.where(first_core, mine, theirs), jnp.where(first_core, theirs, mine)], axis=0
        )
        return lax.all_gather(
            chip_block, "dp", axis=0, tiled=True, axis_index_groups=chip_groups
        )

    attn_pack = gathered(
        [
            split_columns(q_weight[0]),
            split_columns(k_weight[0]),
            split_columns(v_weight[0]),
            split_rows(o_weight[0]),
        ]
    )
    ffn_pack = gathered(
        [split_columns(gate_weight[0]), split_columns(up_weight[0]), split_rows(down_weight[0])]
    )

    attn_gain, ffn_gain = attn_norm[0], ffn_norm[0]
    head_gains = jnp.concatenate([q_norm, k_norm, jnp.zeros((6, head_width), f32)], axis=0)

    both = jnp.stack([block_input, out_cotangent])
    kept = jnp.where(first_core, both[:, :, :quarter], both[:, :, quarter:])
    received = to_core(jnp.where(first_core, both[:, :, quarter:], both[:, :, :quarter]))
    first_rows = jnp.where(first_core, kept, received)
    second_rows = jnp.where(first_core, received, kept)
    inputs = [[rows[0, micro] for rows in (first_rows, second_rows)] for micro in range(micro_count)]
    cotangents = [
        [rows[1, micro] for rows in (first_rows, second_rows)] for micro in range(micro_count)
    ]

    def arranged(values):
        parts = values.reshape(2, 2, quarter)
        parts = jnp.where(half == 0, parts, parts[::-1])
        parts = jnp.where(first_core, parts, parts[:, ::-1])
        return parts.transpose(1, 0, 2).reshape(length)

    position = arranged(jnp.arange(length, dtype=jnp.int32))
    tables = rope_tables(position, head_width)
    other_ids = to_core(segment_ids)
    masks = []
    for micro in range(micro_count):
        own, other = segment_ids[micro], other_ids[micro]
        pair = []
        for ids in (jnp.where(first_core, own, other), jnp.where(first_core, other, own)):
            ids = arranged(ids)
            allowed = (position[:, None] >= position[None, :]) & (ids[:, None] == ids[None, :])
            pair.append(allowed.astype(f32))
        masks.append(pair)

    def row_gather(rows):
        pair = jnp.concatenate([rows, to_half(rows)], axis=0)
        return jnp.concatenate([pair, to_core(pair)], axis=0)

    def row_scatter(partial):
        side = 2 * quarter
        pair = partial[:side].astype(f32) + to_core(partial[side:]).astype(f32)
        return pair[:quarter] + to_half(pair[quarter:].astype(bf16)).astype(f32)

    def layer_forward(hidden_in, mask):
        hidden = hidden_in.astype(f32)
        inverse_in = inverse_rms(hidden)
        normed = row_gather((hidden * inverse_in * attn_gain).astype(bf16))
        queries, keys, values, attended, partial = attn_forward(
            normed, attn_pack, head_gains, tables, mask
        )
        mixed = hidden + row_scatter(partial)
        inverse_mid = inverse_rms(mixed)
        normed_ffn = row_gather((mixed * inverse_mid * ffn_gain).astype(bf16))
        gate, upward, activated, partial = ffn_forward(normed_ffn, ffn_pack)
        result = (mixed + row_scatter(partial)).astype(bf16)
        back = (hidden_in, queries, keys, values, mixed, gate, upward)
        saved = (normed, attended, normed_ffn, activated)
        return result, back, saved

    def layer_backward(grad_in, back, mask):
        hidden_in, queries, keys, values, mixed, gate, upward = back
        grad_down = row_gather(grad_in)
        ffn_grads, partial = ffn_backward(grad_down, gate, upward, ffn_pack)
        grad_normed_ffn = row_scatter(partial)
        inverse_mid = inverse_rms(mixed)
        ffn_gain_grad = jnp.sum(grad_normed_ffn * mixed * inverse_mid, axis=0)
        grad_mixed = grad_in.astype(f32) + norm_back(
            grad_normed_ffn, mixed, inverse_mid, ffn_gain
        )
        grad_proj = row_gather(grad_mixed.astype(bf16))
        attn_grads, head_gain_grads, partial = attn_backward(
            grad_proj, queries, keys, values, attn_pack, head_gains, tables, mask
        )
        grad_normed = row_scatter(partial)
        hidden = hidden_in.astype(f32)
        inverse_in = inverse_rms(hidden)
        attn_gain_grad = jnp.sum(grad_normed * hidden * inverse_in, axis=0)
        grad_hidden = (grad_mixed + norm_back(grad_normed, hidden, inverse_in, attn_gain)).astype(
            bf16
        )
        saved = (grad_down, ffn_grads, grad_proj, attn_grads)
        gains = (attn_gain_grad, ffn_gain_grad, head_gain_grads)
        return grad_hidden, saved, gains

    at_first = section == 0

    def pick(first, second):
        return jax.tree.map(lambda a, b: jnp.where(at_first, a, b), first, second)

    chunks = range(2)
    forward_route = [(0, 1)]
    backward_route = [(1, 0)]
    zero_rows = jnp.zeros_like(inputs[0][0])
    forward_masks = [masks[0], pick(masks[1], masks[0]), masks[1]]
    results, backs, saves = [], [], []
    for step in range(3):
        step_out = []
        for chunk in chunks:
            own = inputs[step][chunk] if step < 2 else zero_rows
            if step > 0:
                arrived = lax.ppermute(results[step - 1][chunk], "section", forward_route)
                own = jnp.where(at_first, own, arrived)
            step_out.append(layer_forward(own, forward_masks[step][chunk]))
        results.append([out[0] for out in step_out])
        backs.append([out[1] for out in step_out])
        saves.append([out[2] for out in step_out])
    backward_masks = [masks[0], pick(masks[0], masks[1]), masks[1]]
    grads, back_saves, gain_total = [], [], None
    for step in range(3):
        step_out = []
        for chunk in chunks:
            own = cotangents[step][chunk] if step < 2 else zero_rows
            if step > 0:
                arrived = lax.ppermute(grads[step - 1][chunk], "section", backward_route)
            else:
                arrived = zero_rows
            own = jnp.where(at_first, arrived, own)
            back = pick(backs[0][chunk], backs[2][chunk]) if step == 1 else backs[1][chunk]
            step_out.append(layer_backward(own, back, backward_masks[step][chunk]))
            gains = step_out[-1][2]
            gain_total = gains if gain_total is None else jax.tree.map(jnp.add, gain_total, gains)
        grads.append([out[0] for out in step_out])
        back_saves.append([out[1] for out in step_out])

    def micro_rows(table, first_step, second_step):
        return [pick(table[first_step][chunk], table[second_step][chunk]) for chunk in chunks]

    out_rows = jnp.stack(
        [jnp.stack(micro_rows(results, micro, micro + 1)) for micro in range(2)]
        + [jnp.stack(micro_rows(grads, micro + 1, micro)) for micro in range(2)]
    )
    mine = jnp.where(first_core, out_rows[:, 0], out_rows[:, 1])
    theirs = to_core(jnp.where(first_core, out_rows[:, 1], out_rows[:, 0]))
    whole_rows = jnp.concatenate(
        [jnp.where(first_core, mine, theirs), jnp.where(first_core, theirs, mine)], axis=1
    )
    section_outputs, section_input_grads = whole_rows[None, :2], whole_rows[None, 2:]

    saved = [
        pick(saves[micro][chunk], saves[micro + 1][chunk]) for micro in range(2) for chunk in chunks
    ]
    back_saved = [
        pick(back_saves[micro + 1][chunk], back_saves[micro][chunk])
        for micro in range(2)
        for chunk in chunks
    ]

    def stacked(items, axis=0):
        return jnp.concatenate(items, axis=axis)

    normed_t = stacked([item[0] for item in saved]).T
    attended = stacked([item[1] for item in saved])
    normed_ffn_t = stacked([item[2] for item in saved]).T
    activated = stacked([item[3] for item in saved])
    grad_down_t = stacked([item[0] for item in back_saved]).T
    ffn_grads = stacked([item[1] for item in back_saved], axis=1)
    grad_proj_t = stacked([item[2] for item in back_saved]).T
    attn_grads = stacked([item[3] for item in back_saved], axis=1)

    def reduced(partial):
        rows = lax.psum_scatter(
            partial, "dp", scatter_dimension=0, tiled=True, axis_index_groups=chip_groups
        )
        side = rows.shape[0] // 2
        own = jnp.where(first_core, rows[:side], rows[side:])
        other = to_core(jnp.where(first_core, rows[side:], rows[:side]))
        return (
            jnp.where(first_core, own, other).astype(f32),
            jnp.where(first_core, other, own).astype(f32),
        )

    ffn_sides = reduced(
        weight_grad(
            jnp.stack([normed_ffn_t, grad_down_t]),
            jnp.concatenate([ffn_grads, activated[None]], axis=0),
            lambda block: block // 2,
        )
    )
    attn_right = jnp.concatenate([attn_grads, attended[None]], axis=0)
    kv_heads = attn_grads.shape[0]
    attn_sides = reduced(
        weight_grad(
            jnp.stack([normed_t, grad_proj_t]), attn_right, lambda block: block // kv_heads
        )
    )
    units = gate_weight.shape[2] // 2
    q_width = q_weight.shape[2] // 2
    blk = attn_grads.shape[2]
    q_blk = blk - 2 * head_width

    def across(first, last):
        return jnp.concatenate([side[:, first:last] for side in ffn_sides], axis=1)[None]

    def heads_of(first, last):
        return jnp.concatenate(
            [
                side[:, blk * head + first : blk * head + last]
                for side in attn_sides
                for head in range(kv_heads)
            ],
            axis=1,
        )[None]

    down_grad = jnp.concatenate([side[:, 2 * units :].T for side in ffn_sides], axis=0)[None]
    o_grad = jnp.concatenate([side[:, kv_heads * blk :].T for side in attn_sides], axis=0)[None]

    packed = jnp.concatenate(
        [gain_total[0], gain_total[1], gain_total[2][0], gain_total[2][1]]
    ).reshape(-1, head_width)
    packed = packed + to_core(packed)
    packed = packed + to_half(packed)
    reach = 2
    while reach < n_dp:
        packed = packed + lax.ppermute(packed, "dp", [(i, i ^ reach) for i in range(n_dp)])
        reach *= 2
    packed = packed.reshape(-1)
    return (
        section_outputs,
        section_input_grads,
        packed[None, :depth],
        heads_of(0, q_blk),
        heads_of(q_blk, q_blk + head_width),
        heads_of(q_blk + head_width, blk),
        o_grad,
        packed[None, 2 * depth : 2 * depth + head_width],
        packed[None, 2 * depth + head_width :],
        packed[None, depth : 2 * depth],
        across(0, units),
        across(units, 2 * units),
        down_grad,
    )


def solution(mesh):
    rows = P(None, ("dp", "tensor"), None)
    out_rows = P("section", None, ("dp", "tensor"), None)
    gain = P("section", None)
    wide = P("section", "dp", "tensor")
    tall = P("section", "tensor", "dp")
    return jax.shard_map(
        per_device,
        mesh=mesh,
        in_specs=(
            rows, P(None, "dp"), rows, gain, wide, wide, wide, tall, gain, gain, gain, wide, wide, tall,
        ),
        out_specs=(
            out_rows, out_rows, gain, wide, wide, wide, tall, gain, gain, gain, wide, wide, tall,
        ),
        check_vma=False,
    )
```

time: 1530 us -> 1860 us (1.22)
  waiting for transfers between devices: 660 us -> 1000 us
  matrix products: 293 us -> 0 us
  Pallas kernels: 0 us -> 216 us
  blocking collectives: 200 us -> 0 us
  starting transfers between devices: 13.4 us -> 127 us
  local copies, waits for them, and re-layouts: 166 us -> 264 us
  other arithmetic: 168 us -> 225 us
    ppermute x4 -> x115, waiting for transfers between devices: 46.8 us -> 728 us  [the longest x49 524 us: to_half(): return lax.ppermute(values, 'tensor', swap_half)]
    dot_general x67 -> x0, matrix products: 293 us -> none  [the longest x21 108 us: contract_last(): lax.dot_general(left_side, right_side, (((1,), (1,)), ((), ())), preferre...]
    unnamed x21 -> x4, waiting for transfers between devices: 229 us -> 0.07 us
    pallas_call x0 -> x26, Pallas kernels: none -> 216 us  [the longest x6 62.6 us: ffn_backward(): pl.pallas_call(ffn_backward_kernel, grid=(steps,), in_specs=[whole((lengt...]
    all_gather x12 -> x0, blocking collectives: 149 us -> none  [seq_gather(): return lax.all_gather(values, 'tensor', axis=0, tiled=True)]
    all_gather x7 -> x2, waiting for transfers between devices: 294 us -> 152 us  [gathered(): lax.all_gather(chip_block, 'dp', axis=0, tiled=True, axis_index_groups=ch...]
    ppermute x4 -> x115, starting transfers between devices: 11.5 us -> 126 us  [the longest x49 91 us: to_half(): return lax.ppermute(values, 'tensor', swap_half)]
    unnamed x469 -> x738, local copies, waits for them, and re-layouts: 40.5 us -> 138 us
  transfers between devices with their start and end apart: 24 -> 119, of which waited for: 18 -> 94; matrix products, arithmetic and copies ran while one was open for 20% -> 9% of each run, Pallas kernels for 0% -> 2%
where the time goes in v1:
time: 1860 us
  waiting for transfers between devices  1000 us (54%)
  local copies, waits for them, and re-layouts  264 us (14%)
  other arithmetic  225 us (12%)
  Pallas kernels  216 us (12%)
  starting transfers between devices  127 us (7%)
    ppermute x49, waiting for transfers between devices, to_half(): return lax.ppermute(values, 'tensor', swap_half)  524 us
    all_gather x2, waiting for transfers between devices, gathered(): lax.all_gather(chip_block, 'dp', axis=0, tiled=True, axis_index_groups=ch...  152 us
    unnamed x738, local copies, waits for them, and re-layouts  138 us
    reduce_scatter x2, waiting for transfers between devices, reduced(): lax.psum_scatter(partial, 'dp', scatter_dimension=0, tiled=True, axis_ind...  125 us
    ppermute x4, waiting for transfers between devices, per_device(): arrived = lax.ppermute(grads[step - 1][chunk], 'section', backward_route)  101 us
    ppermute x49, starting transfers between devices, to_half(): return lax.ppermute(values, 'tensor', swap_half)  91 us
    pallas_call x6, Pallas kernels, ffn_backward(): pl.pallas_call(ffn_backward_kernel, grid=(steps,), in_specs=[whole((lengt...  62.6 us
    select_n x35, other arithmetic, pick(): return jax.tree.map(lambda a, b: jnp.where(at_first, a, b), first, second)  60.8 us
  transfers between devices with their start and end apart: 119, of which 94 were waited for; matrix products, arithmetic and copies ran while one was open for 9% of the time, Pallas kernels for 2%

profile of v1, /device:TPU:0, one launch (start us, length us, event | category | flops | bytes accessed | tf_op | source)
XLA Modules:
  0.0 1855.4 jit_solution(8188422782148170822)
XLA Ops:
  61.3 24.6 %all-gather.3.cloned.1.call-done.w_q.w_k.w_v.w_o = bf16[2048,1536]{1,0:T(8,128)(2,1)} async-done(((bf16[512,1536]{1,0:T(8,128)(2,1)}), bf16[2048,1536]{1,0:T(8,128)(2,1)}) %all-gather.3.cloned.1.call-update) | async-done | bytes 6291472 | tf_op jit(solution)/shard_map/all_gather | solution.py:454
  103.8 12.5 collective-permute-done.6
  136.6 127.1 %all-gather.5.cloned.1.call-done.w_gate.w_up.w_down = bf16[2048,4608]{1,0:T(8,128)(2,1)} async-done(((bf16[512,4608]{1,0:T(8,128)(2,1)}), bf16[2048,4608]{1,0:T(8,128)(2,1)}) %all-gather.5.cloned.1.call-update) | async-done | bytes 18874384 | tf_op jit(solution)/shard_map/all_gather | solution.py:454
  283.6 12.5 collective-permute-done.11
  313.0 12.7 collective-permute-start.13
  441.7 12.4 collective-permute-done.59
  586.7 25.1 %collective-permute-done.64 = bf16[48,2048]{0,1:T(8,128)(2,1)S(1)} collective-permute-done((bf16[48,2048]{0,1:T(8,128)(2,1)S(1)}, bf16[48,2048]{0,1:T(8,128)(2,1)S(1)}, u32[]{:S(2)}, u32[]{:S(2)}) %collective-permute-start.64) | collective-permute-done | bytes 196640 | tf_op jit(solution)/shard_map/ppermute | solution.py:581
  682.7 13.9 collective-permute-done.68
  700.4 12.4 collective-permute-done.69
  743.3 13.7 collective-permute-done.72
  761.0 25.6 %collective-permute-done.90 = bf16[48,2048]{0,1:T(8,128)(2,1)S(1)} collective-permute-done((bf16[48,2048]{0,1:T(8,128)(2,1)S(1)}, bf16[48,2048]{0,1:T(8,128)(2,1)S(1)}, u32[]{:S(2)}, u32[]{:S(2)}) %collective-permute-start.90) | collective-permute-done | bytes 196640 | tf_op jit(solution)/shard_map/ppermute | solution.py:581
  787.5 13.8 collective-permute-done.91
  824.2 13.7 collective-permute-done.94
  840.9 12.9 collective-permute-done.95
  873.5 13.7 collective-permute-done.98
  890.2 12.9 collective-permute-done.21
  924.1 13.7 collective-permute-done.24
  940.8 12.9 collective-permute-done.25
  976.4 13.7 collective-permute-done.28
  1130.1 12.5 collective-permute-done.76
  1275.0 25.1 %collective-permute-done.81 = bf16[48,2048]{0,1:T(8,128)(2,1)S(1)} collective-permute-done((bf16[48,2048]{0,1:T(8,128)(2,1)S(1)}, bf16[48,2048]{0,1:T(8,128)(2,1)S(1)}, u32[]{:S(2)}, u32[]{:S(2)}) %collective-permute-start.81) | collective-permute-done | bytes 196640 | tf_op jit(solution)/shard_map/ppermute | solution.py:581
  1370.9 13.9 collective-permute-done.85
  1388.6 12.4 collective-permute-done.86
  1432.1 13.7 collective-permute-done.89
  1449.8 25.6 %collective-permute-done.99 = bf16[48,2048]{0,1:T(8,128)(2,1)S(1)} collective-permute-done((bf16[48,2048]{0,1:T(8,128)(2,1)S(1)}, bf16[48,2048]{0,1:T(8,128)(2,1)S(1)}, u32[]{:S(2)}, u32[]{:S(2)}) %collective-permute-start.99) | collective-permute-done | bytes 196640 | tf_op jit(solution)/shard_map/ppermute | solution.py:581
  1476.4 13.8 collective-permute-done.100
  1514.0 12.9 collective-permute-done.103
  1530.0 12.8 collective-permute-done.104
  1593.6 18.6 %weight_grad.3 = bf16[2048,4608]{1,0:T(8,128)(2,1)} custom-call(bf16[2,2048,768]{2,1,0:T(8,128)(2,1)S(1)} %pad_maximum_fusion.2.left_t, bf16[3,768,1536]{2,1,0:T(8,128)(2,1)S(1)} %pad_maximum_fusion.right), custom_call_target="tpu_custom_call" | custom-call | flops 14495514624 | bytes 25952256 | tf_op jit(solution)/shard_map/weight_grad/pallas_call | solution.py:373
  1641.1 12.3 collective-permute-done.55
  1661.2 13.4 collective-permute-done.107
  1694.5 124.5 %reduce-scatter.5.cloned.1.call-done = bf16[512,4608]{1,0:T(8,128)(2,1)} async-done(((bf16[2048,4608]{1,0:T(8,128)(2,1)}), bf16[512,4608]{1,0:T(8,128)(2,1)}) %reduce-scatter.5.cloned.1.call-update) | async-done | bytes 4718608 | tf_op jit(solution)/shard_map/reduce_scatter | solution.py:628
  (1356 shorter events, 1126.0 us)
Async XLA Ops:
  7.2 78.7 %all-gather.3.cloned.1.call-start = ((), (), s32[]{:S(2)}) async-start(), calls=%async_computation.2 | async-start | bytes 7864320 | tf_op jit(solution)/shard_map/all_gather | solution.py:454
  12.9 250.8 %all-gather.5.cloned.1.call-start = ((), (), s32[]{:S(2)}) async-start(), calls=%async_computation.3 | async-start | bytes 23592960 | tf_op jit(solution)/shard_map/all_gather | solution.py:454
  24.6 1668.1 %reduce-scatter.3.cloned.1.call-start = ((), (), s32[]{:S(2)}) async-start(), calls=%async_computation.4 | async-start | bytes 7864320 | tf_op jit(solution)/shard_map/reduce_scatter | solution.py:628
  41.3 15.3 collective-permute-start.1
  296.2 15.0 collective-permute-start.12
  313.0 24.8 %collective-permute-start.13 = (bf16[48,2048]{0,1:T(8,128)(2,1)S(1)}, bf16[48,2048]{0,1:T(8,128)(2,1)S(1)}, u32[]{:S(2)}, u32[]{:S(2)}) collective-permute-start(bf16[48,2048]{0,1:T(8,128)(2,1)S(1)} %fusion.25), channel_id=1, source_target_pairs={{0,1},{1,0},{2,3},{3,2},{4,5},{5,4},{6,7},{7,6},{8,9},{9,8},{10,11... | collective-permute-start | bytes 589832 | tf_op jit(solution)/shard_map/ppermute | solution.py:436
  364.4 23.2 %collective-permute-start.56 = (bf16[48,2048]{0,1:T(8,128)(2,1)S(1)}, bf16[48,2048]{0,1:T(8,128)(2,1)S(1)}, u32[]{:S(2)}, u32[]{:S(2)}) collective-permute-start(bf16[48,2048]{0,1:T(8,128)(2,1)S(1)} %fusion.98), channel_id=1, source_target_pairs={{0,1},{1,0},{2,3},{3,2},{4,5},{5,4},{6,7},{7,6},{8,9},{9,8},{10,11... | collective-permute-start | bytes 589832 | tf_op jit(solution)/shard_map/ppermute | solution.py:436
  377.0 21.0 %collective-permute-start.17 = (bf16[48,2048]{0,1:T(8,128)(2,1)S(1)}, bf16[48,2048]{0,1:T(8,128)(2,1)S(1)}, u32[]{:S(2)}, u32[]{:S(2)}) collective-permute-start(bf16[48,2048]{0,1:T(8,128)(2,1)S(1)} %multiply_convert_fusion.4), channel_id=1, source_target_pairs={{0,1},{1,0},{2,3},{3,2},{4,5},{5,4},{6,7},{7,6},{8,9},{9,8},{10,11... | collective-permute-start | bytes 589832 | tf_op jit(solution)/shard_map/ppermute | solution.py:436
  475.5 25.8 %collective-permute-start.20 = (bf16[48,2048]{0,1:T(8,128)(2,1)}, bf16[48,2048]{0,1:T(8,128)(2,1)}, u32[]{:S(2)}, u32[]{:S(2)}) collective-permute-start(bf16[48,2048]{0,1:T(8,128)(2,1)} %slice.1164), channel_id=1, source_target_pairs={{0,1},{1,0},{2,3},{3,2},{4,5},{5,4},{6,7},{7,6},{8,9},{9,8},{10,11... | collective-permute-start | bytes 589832 | tf_op jit(solution)/shard_map/ppermute | solution.py:436
  501.0 20.4 %collective-permute-start.62 = (bf16[96,2048]{0,1:T(8,128)(2,1)S(1)}, bf16[96,2048]{0,1:T(8,128)(2,1)S(1)}, u32[]{:S(2)}, u32[]{:S(2)}) collective-permute-start(bf16[96,2048]{0,1:T(8,128)(2,1)S(1)} %slice.744), channel_id=1, source_target_pairs={{0,2},{2,0},{4,6},{6,4},{8,10},{10,8},{12,14},{14,12},{1,3},{3,1},... | collective-permute-start | bytes 1179656 | tf_op jit(solution)/shard_map/ppermute | solution.py:433
  504.0 17.1 collective-permute-start.38
  521.8 23.1 %collective-permute-start.63 = (bf16[48,2048]{0,1:T(8,128)(2,1)S(1)}, bf16[48,2048]{0,1:T(8,128)(2,1)S(1)}, u32[]{:S(2)}, u32[]{:S(2)}) collective-permute-start(bf16[48,2048]{0,1:T(8,128)(2,1)S(1)} %slice.1154), channel_id=1, source_target_pairs={{0,1},{1,0},{2,3},{3,2},{4,5},{5,4},{6,7},{7,6},{8,9},{9,8},{10,11... | collective-permute-start | bytes 589832 | tf_op jit(solution)/shard_map/ppermute | solution.py:436
  583.3 28.5 %collective-permute-start.64 = (bf16[48,2048]{0,1:T(8,128)(2,1)S(1)}, bf16[48,2048]{0,1:T(8,128)(2,1)S(1)}, u32[]{:S(2)}, u32[]{:S(2)}) collective-permute-start(bf16[48,2048]{0,1:T(8,128)(2,1)S(1)} %fusion.11), channel_id=1, source_target_pairs={{16,0},{17,1},{18,2},{19,3},{20,4},{21,5},{22,6},{23,7},{24,8},{25... | collective-permute-start | bytes 589832 | tf_op jit(solution)/shard_map/ppermute | solution.py:581
  585.2 26.8 %collective-permute-start.42 = (bf16[48,2048]{0,1:T(8,128)(2,1)S(1)}, bf16[48,2048]{0,1:T(8,128)(2,1)S(1)}, u32[]{:S(2)}, u32[]{:S(2)}) collective-permute-start(bf16[48,2048]{0,1:T(8,128)(2,1)S(1)} %slice.1159), channel_id=1, source_target_pairs={{0,1},{1,0},{2,3},{3,2},{4,5},{5,4},{6,7},{7,6},{8,9},{9,8},{10,11... | collective-permute-start | bytes 589832 | tf_op jit(solution)/shard_map/ppermute | solution.py:436
  612.0 14.9 collective-permute-start.65
  615.8 21.0 %collective-permute-start.43 = (bf16[48,2048]{0,1:T(8,128)(2,1)S(1)}, bf16[48,2048]{0,1:T(8,128)(2,1)S(1)}, u32[]{:S(2)}, u32[]{:S(2)}) collective-permute-start(bf16[48,2048]{0,1:T(8,128)(2,1)S(1)} %get-tuple-element.368), channel_id=1, source_target_pairs={{0,1},{1,0},{2,3},{3,2},{4,5},{5,4},{6,7},{7,6},{8,9},{9,8},{10,11... | collective-permute-start | bytes 589832 | tf_op jit(solution)/shard_map/ppermute | solution.py:436
  759.6 27.0 %collective-permute-start.90 = (bf16[48,2048]{0,1:T(8,128)(2,1)S(1)}, bf16[48,2048]{0,1:T(8,128)(2,1)S(1)}, u32[]{:S(2)}, u32[]{:S(2)}) collective-permute-start(bf16[48,2048]{0,1:T(8,128)(2,1)S(1)} %get-tuple-element.285), channel_id=1, source_target_pairs={{16,0},{17,1},{18,2},{19,3},{20,4},{21,5},{22,6},{23,7},{24,8},{25... | collective-permute-start | bytes 589832 | tf_op jit(solution)/shard_map/ppermute | solution.py:581
  1004.4 22.4 %collective-permute-start.30 = (bf16[48,2048]{0,1:T(8,128)(2,1)S(1)}, bf16[48,2048]{0,1:T(8,128)(2,1)S(1)}, u32[]{:S(2)}, u32[]{:S(2)}) collective-permute-start(bf16[48,2048]{0,1:T(8,128)(2,1)S(1)} %fusion.24), channel_id=1, source_target_pairs={{0,1},{1,0},{2,3},{3,2},{4,5},{5,4},{6,7},{7,6},{8,9},{9,8},{10,11... | collective-permute-start | bytes 589832 | tf_op jit(solution)/shard_map/ppermute | solution.py:436
  1052.8 23.2 %collective-permute-start.73 = (bf16[48,2048]{0,1:T(8,128)(2,1)S(1)}, bf16[48,2048]{0,1:T(8,128)(2,1)S(1)}, u32[]{:S(2)}, u32[]{:S(2)}) collective-permute-start(bf16[48,2048]{0,1:T(8,128)(2,1)S(1)} %fusion.96), channel_id=1, source_target_pairs={{0,1},{1,0},{2,3},{3,2},{4,5},{5,4},{6,7},{7,6},{8,9},{9,8},{10,11... | collective-permute-start | bytes 589832 | tf_op jit(solution)/shard_map/ppermute | solution.py:436
  1065.4 21.0 %collective-permute-start.34 = (bf16[48,2048]{0,1:T(8,128)(2,1)S(1)}, bf16[48,2048]{0,1:T(8,128)(2,1)S(1)}, u32[]{:S(2)}, u32[]{:S(2)}) collective-permute-start(bf16[48,2048]{0,1:T(8,128)(2,1)S(1)} %multiply_convert_fusion.2), channel_id=1, source_target_pairs={{0,1},{1,0},{2,3},{3,2},{4,5},{5,4},{6,7},{7,6},{8,9},{9,8},{10,11... | collective-permute-start | bytes 589832 | tf_op jit(solution)/shard_map/ppermute | solution.py:436
  1164.1 26.4 %collective-permute-start.37 = (bf16[48,2048]{0,1:T(8,128)(2,1)}, bf16[48,2048]{0,1:T(8,128)(2,1)}, u32[]{:S(2)}, u32[]{:S(2)}) collective-permute-start(bf16[48,2048]{0,1:T(8,128)(2,1)} %slice.1160), channel_id=1, source_target_pairs={{0,1},{1,0},{2,3},{3,2},{4,5},{5,4},{6,7},{7,6},{8,9},{9,8},{10,11... | collective-permute-start | bytes 589832 | tf_op jit(solution)/shard_map/ppermute | solution.py:436
  1190.2 20.4 %collective-permute-start.79 = (bf16[96,2048]{0,1:T(8,128)(2,1)S(1)}, bf16[96,2048]{0,1:T(8,128)(2,1)S(1)}, u32[]{:S(2)}, u32[]{:S(2)}) collective-permute-start(bf16[96,2048]{0,1:T(8,128)(2,1)S(1)} %slice.762), channel_id=1, source_target_pairs={{0,2},{2,0},{4,6},{6,4},{8,10},{10,8},{12,14},{14,12},{1,3},{3,1},... | collective-permute-start | bytes 1179656 | tf_op jit(solution)/shard_map/ppermute | solution.py:433
  1193.2 17.1 collective-permute-start.47
  1210.9 23.1 %collective-permute-start.80 = (bf16[48,2048]{0,1:T(8,128)(2,1)S(1)}, bf16[48,2048]{0,1:T(8,128)(2,1)S(1)}, u32[]{:S(2)}, u32[]{:S(2)}) collective-permute-start(bf16[48,2048]{0,1:T(8,128)(2,1)S(1)} %slice.1150), channel_id=1, source_target_pairs={{0,1},{1,0},{2,3},{3,2},{4,5},{5,4},{6,7},{7,6},{8,9},{9,8},{10,11... | collective-permute-start | bytes 589832 | tf_op jit(solution)/shard_map/ppermute | solution.py:436
  1271.6 28.5 %collective-permute-start.81 = (bf16[48,2048]{0,1:T(8,128)(2,1)S(1)}, bf16[48,2048]{0,1:T(8,128)(2,1)S(1)}, u32[]{:S(2)}, u32[]{:S(2)}) collective-permute-start(bf16[48,2048]{0,1:T(8,128)(2,1)S(1)} %fusion.19), channel_id=1, source_target_pairs={{16,0},{17,1},{18,2},{19,3},{20,4},{21,5},{22,6},{23,7},{24,8},{25... | collective-permute-start | bytes 589832 | tf_op jit(solution)/shard_map/ppermute | solution.py:581
  1273.5 26.8 %collective-permute-start.51 = (bf16[48,2048]{0,1:T(8,128)(2,1)S(1)}, bf16[48,2048]{0,1:T(8,128)(2,1)S(1)}, u32[]{:S(2)}, u32[]{:S(2)}) collective-permute-start(bf16[48,2048]{0,1:T(8,128)(2,1)S(1)} %slice.1157), channel_id=1, source_target_pairs={{0,1},{1,0},{2,3},{3,2},{4,5},{5,4},{6,7},{7,6},{8,9},{9,8},{10,11... | collective-permute-start | bytes 589832 | tf_op jit(solution)/shard_map/ppermute | solution.py:436
  1300.3 14.9 collective-permute-start.82
  1304.1 20.9 %collective-permute-start.52 = (bf16[48,2048]{0,1:T(8,128)(2,1)S(1)}, bf16[48,2048]{0,1:T(8,128)(2,1)S(1)}, u32[]{:S(2)}, u32[]{:S(2)}) collective-permute-start(bf16[48,2048]{0,1:T(8,128)(2,1)S(1)} %get-tuple-element.369), channel_id=1, source_target_pairs={{0,1},{1,0},{2,3},{3,2},{4,5},{5,4},{6,7},{7,6},{8,9},{9,8},{10,11... | collective-permute-start | bytes 589832 | tf_op jit(solution)/shard_map/ppermute | solution.py:436
  1448.4 27.0 %collective-permute-start.99 = (bf16[48,2048]{0,1:T(8,128)(2,1)S(1)}, bf16[48,2048]{0,1:T(8,128)(2,1)S(1)}, u32[]{:S(2)}, u32[]{:S(2)}) collective-permute-start(bf16[48,2048]{0,1:T(8,128)(2,1)S(1)} %get-tuple-element.287), channel_id=1, source_target_pairs={{16,0},{17,1},{18,2},{19,3},{20,4},{21,5},{22,6},{23,7},{24,8},{25... | collective-permute-start | bytes 589832 | tf_op jit(solution)/shard_map/ppermute | solution.py:581
  1577.0 242.0 %reduce-scatter.5.cloned.1.call-start = ((), (), s32[]{:S(2)}) async-start(), calls=%async_computation.5 | async-start | bytes 23592960 | tf_op jit(solution)/shard_map/reduce_scatter | solution.py:628
  1622.2 16.1 collective-permute-start.54
  1694.4 128.7 %collective-permute-start.113 = (bf16[256,1536]{1,0:T(8,128)(2,1)S(1)}, bf16[256,1536]{1,0:T(8,128)(2,1)}, u32[]{:S(2)}, u32[]{:S(2)}) collective-permute-start(bf16[256,1536]{1,0:T(8,128)(2,1)S(1)} %broadcast_select_fusion.28), channel_id=1, source_target_pairs={{0,2},{2,0},{4,6},{6,4},{8,10},{10,8},{12,14},{14,12},{1,3},{3,1},... | collective-permute-start | bytes 2359304 | tf_op jit(solution)/shard_map/ppermute | solution.py:433
  (452 other events, 4136.8 us)
Sparse Core Ops, SparseCore 0:
  13.1 72.7 all-gather.2
  87.7 175.9 all-gather.4
  1577.1 67.5 reduce-scatter.2
  1647.7 171.3 reduce-scatter.4

commit v2 on v1

v2 whole, which is shorter than its diff:
```python
import functools

import jax
import jax.numpy as jnp
from jax import lax
from jax.experimental import pallas as pl
from jax.experimental.pallas import tpu as pltpu
from jax.sharding import PartitionSpec as P

norm_eps = 1e-06
rope_base = 1000000.0
masked_score = -1e30
row_chunks = 4
f32 = jnp.float32
bf16 = jnp.bfloat16
MIB = 1024 * 1024
MESH = pl.DeviceIdType.MESH


def dot_nn(left, right):
    return lax.dot_general(left, right, (((1,), (0,)), ((), ())), preferred_element_type=f32)


def dot_nt(left, right):
    return lax.dot_general(left, right, (((1,), (1,)), ((), ())), preferred_element_type=f32)


def dot_tn(left, right):
    return lax.dot_general(left, right, (((0,), (0,)), ((), ())), preferred_element_type=f32)


def inverse_rms(values):
    return lax.rsqrt(jnp.mean(values * values, axis=-1, keepdims=True) + norm_eps)


def norm_back(grad_out, values, inverse, gain_vec):
    scaled = grad_out * gain_vec
    return inverse * (
        scaled - values * inverse * inverse * jnp.mean(scaled * values, axis=-1, keepdims=True)
    )


class Exchange:
    def __init__(self, send_sems, recv_sems):
        place = lax.axis_index("dp")
        self.core = {"dp": place + 1 - 2 * (place % 2)}
        self.half = {"tensor": 1 - lax.axis_index("tensor")}
        self.section = {"section": 1 - lax.axis_index("section")}
        self.send_sems, self.recv_sems = send_sems, recv_sems

    def greet(self, with_section):
        barrier = pltpu.get_barrier_semaphore()
        others = [self.core, self.half] + ([self.section] if with_section else [])
        for other in others:
            pl.semaphore_signal(barrier, inc=1, device_id=other, device_id_type=MESH)
        pl.semaphore_wait(barrier, len(others))

    def copy(self, source, target, other, stage, chunk):
        return pltpu.make_async_remote_copy(
            src_ref=source,
            dst_ref=target,
            send_sem=self.send_sems.at[stage, chunk],
            recv_sem=self.recv_sems.at[stage, chunk],
            device_id=other,
            device_id_type=MESH,
        )


def gather_then(exchange, rows, use):
    chunks, total, _ = rows.shape
    own = total // 4
    first = [
        exchange.copy(rows.at[c, pl.ds(0, own)], rows.at[c, pl.ds(own, own)], exchange.half, 0, c)
        for c in range(chunks)
    ]
    second = [
        exchange.copy(
            rows.at[c, pl.ds(0, 2 * own)], rows.at[c, pl.ds(2 * own, 2 * own)], exchange.core, 1, c
        )
        for c in range(chunks)
    ]
    for c in range(chunks):
        first[c].start()
    for c in range(chunks):
        first[c].wait_recv()
        second[c].start()
        if c > 0:
            second[c - 1].wait_recv()
            use(c - 1)
    second[chunks - 1].wait_recv()
    use(chunks - 1)
    return first + second


def scatter_from(exchange, make, finish, keep, send_core, recv_core, send_half, recv_half):
    chunks, pair, _ = keep.shape
    own = pair // 2
    first = [
        exchange.copy(send_core.at[c], recv_core.at[c], exchange.core, 2, c) for c in range(chunks)
    ]
    second = [
        exchange.copy(send_half.at[c], recv_half.at[c], exchange.half, 3, c) for c in range(chunks)
    ]

    def middle(c):
        first[c].wait_recv()
        summed = keep[c] + recv_core[c].astype(f32)
        send_half[c] = summed[own:].astype(bf16)
        second[c].start()
        keep[c, :own] = summed[:own]

    for c in range(chunks):
        product = make(c)
        send_core[c] = product[pair:].astype(bf16)
        first[c].start()
        keep[c] = product[:pair]
        if c > 0:
            middle(c - 1)
    middle(chunks - 1)
    for c in range(chunks):
        second[c].wait_recv()
        finish(c, keep[c, :own] + recv_half[c].astype(f32))
    return first + second


def load_pack(pack, held, sems):
    depth = held.shape[0] // 4
    return [
        pltpu.make_async_copy(
            pack.at[pl.ds(c * depth, depth)], held.at[pl.ds(c * depth, depth)], sems.at[c]
        )
        for c in range(4)
    ]


def row_mean(values):
    size = values.shape[0] * values.shape[2]
    return jnp.sum(jnp.sum(values, axis=0), axis=-1, keepdims=True)[None] * (1.0 / size)


def accumulate(total, left, weights, first_row, first_col, width, start):
    depth = left.shape[1]
    blk = 512 if width % 512 == 0 else 256

    def body(index, _):
        at = pl.multiple_of(index * blk, blk)
        product = dot_nn(left, weights[pl.ds(first_row, depth), pl.ds(first_col + at, blk)])
        if start:
            total[:, pl.ds(at, blk)] = product
        else:
            total[:, pl.ds(at, blk)] += product
        return 0

    lax.fori_loop(0, width // blk, body, 0)


def rotated(raw, gain, cosine, signed_sine):
    inverse = inverse_rms(raw)
    scaled = raw * inverse * gain
    turned = scaled * cosine + pltpu.roll(scaled, 64, 1) * signed_sine
    return inverse, turned.astype(bf16)


def softmax_rows(query_rot, key_rot, allowed, scale):
    scores = jnp.where(allowed, dot_nt(query_rot, key_rot) * scale, masked_score)
    exponent = jnp.exp(scores - jnp.max(scores, axis=-1, keepdims=True))
    return exponent / jnp.sum(exponent, axis=-1, keepdims=True)


def attn_forward_kernel(
    width, hidden, pack, model_gains, gains, cosine, signed_sine, masks,
    normed, projected, values, attended, mixed, normed_ffn_rows,
    held, keep, send_core, recv_core, send_half, recv_half, load_sems, send_sems, recv_sems,
):
    exchange = Exchange(send_sems, recv_sems)
    exchange.greet(False)
    loads = load_pack(pack, held, load_sems)
    for load in loads:
        load.start()
    chunks, own, cols = hidden.shape
    length = 2 * own
    q_width = attended.shape[1]
    kv_width = q_width // 2
    kv_heads = kv_width // width
    group = q_width // kv_width
    rows = hidden[...].astype(f32)
    inverse = lax.rsqrt(row_mean(rows * rows) + norm_eps)
    for c in range(chunks):
        normed[c, :own] = (rows[c] * inverse[0] * model_gains[0, c][None, :]).astype(bf16)

    def project(c):
        loads[c].wait()
        accumulate(projected, normed[c], held, c * cols, 0, 2 * q_width, c == 0)

    copies = gather_then(exchange, normed, project)
    cos, sin = cosine[...], signed_sine[...]
    gain_q, gain_k = gains[0:1, :], gains[1:2, :]
    scale = width ** (-0.5)
    values[...] = projected[:, q_width + kv_width :].astype(bf16)
    for seq in range(2):
        at = slice(seq * length, (seq + 1) * length)
        allowed = masks[seq] > 0.5
        for kv in range(kv_heads):
            raw_k = projected[at, q_width + kv * width : q_width + (kv + 1) * width]
            value = values[at, kv * width : (kv + 1) * width]
            _, key_rot = rotated(raw_k, gain_k, cos, sin)
            for one in range(group):
                head = slice((kv * group + one) * width, (kv * group + one + 1) * width)
                _, query_rot = rotated(projected[at, head], gain_q, cos, sin)
                weights = softmax_rows(query_rot, key_rot, allowed, scale)
                attended[at, head] = dot_nn(weights.astype(bf16), value).astype(bf16)

    def make(c):
        return dot_nt(attended[...], held[c * cols : (c + 1) * cols, 2 * q_width :])

    def finish(c, summed):
        mixed[c] = hidden[c].astype(f32) + summed

    copies += scatter_from(exchange, make, finish, keep, send_core, recv_core, send_half, recv_half)
    rows = mixed[...]
    inverse = lax.rsqrt(row_mean(rows * rows) + norm_eps)
    for c in range(chunks):
        normed_ffn_rows[c] = (rows[c] * inverse[0] * model_gains[1, c][None, :]).astype(bf16)
    for copy in copies:
        copy.wait_send()


def ffn_forward_kernel(
    hop, rows, mixed, pack, normed, gate_up, activated, result, *rest
):
    if hop:
        arrived, rest = rest[0], rest[1:]
    (
        held, total, keep, send_core, recv_core, send_half, recv_half,
        load_sems, save_sem, send_sems, recv_sems,
    ) = rest
    exchange = Exchange(send_sems, recv_sems)
    exchange.greet(hop)
    loads = load_pack(pack, held, load_sems)
    for load in loads:
        load.start()
    chunks, own, cols = rows.shape
    units = activated.shape[1]
    for c in range(chunks):
        normed[c, :own] = rows[c]

    def project(c):
        loads[c].wait()
        accumulate(total, normed[c], held, c * cols, 0, 2 * units, c == 0)

    copies = gather_then(exchange, normed, project)
    save = pltpu.make_async_copy(total, gate_up, save_sem.at[0])
    save.start()
    blk = 256

    def activate(index, _):
        at = pl.multiple_of(index * blk, blk)
        gate = total[:, pl.ds(at, blk)]
        upward = total[:, pl.ds(units + at, blk)]
        activated[:, pl.ds(at, blk)] = (gate * jax.nn.sigmoid(gate) * upward).astype(bf16)
        return 0

    lax.fori_loop(0, units // blk, activate, 0)
    hops = []

    def make(c):
        return dot_nt(activated[...], held[c * cols : (c + 1) * cols, 2 * units :])

    def finish(c, summed):
        result[c] = (mixed[c] + summed).astype(bf16)
        if hop:
            hops.append(exchange.copy(result.at[c], arrived.at[c], exchange.section, 4, c))
            hops[-1].start()

    copies += scatter_from(exchange, make, finish, keep, send_core, recv_core, send_half, recv_half)
    save.wait()
    for copy in hops:
        copy.wait()
    for copy in copies:
        copy.wait_send()


def ffn_backward_kernel(
    rows, mixed, gate_up, pack, model_gains, grad_down, grads, grad_mixed, grad_proj_rows, gain_grad,
    held, pre, total, keep, send_core, recv_core, send_half, recv_half,
    load_sems, save_sem, send_sems, recv_sems,
):
    exchange = Exchange(send_sems, recv_sems)
    exchange.greet(False)
    loads = load_pack(pack, held, load_sems)
    for load in loads:
        load.start()
    fetch = pltpu.make_async_copy(gate_up, pre, save_sem.at[0])
    fetch.start()
    chunks, own, cols = rows.shape
    units = grads.shape[1] // 2
    for c in range(chunks):
        grad_down[c, :own] = rows[c]

    def project(c):
        loads[c].wait()
        accumulate(total, grad_down[c], held, c * cols, 2 * units, units, c == 0)

    copies = gather_then(exchange, grad_down, project)
    fetch.wait()
    blk = 256

    def activate(index, _):
        at = pl.multiple_of(index * blk, blk)
        gate = pre[:, pl.ds(at, blk)]
        upward = pre[:, pl.ds(units + at, blk)]
        grad_act = total[:, pl.ds(at, blk)]
        sig = jax.nn.sigmoid(gate)
        grads[:, pl.ds(at, blk)] = (grad_act * upward * sig * (1.0 + gate * (1.0 - sig))).astype(bf16)
        grads[:, pl.ds(units + at, blk)] = (grad_act * gate * sig).astype(bf16)
        return 0

    lax.fori_loop(0, units // blk, activate, 0)

    def make(c):
        return dot_nt(grads[...], held[c * cols : (c + 1) * cols, : 2 * units])

    def finish(c, summed):
        grad_mixed[c] = summed

    copies += scatter_from(exchange, make, finish, keep, send_core, recv_core, send_half, recv_half)
    norm_step(mixed[...], grad_mixed[...], model_gains, 1, rows, grad_mixed, gain_grad)
    for c in range(chunks):
        grad_proj_rows[c] = grad_mixed[c].astype(bf16)
    for copy in copies:
        copy.wait_send()


def norm_step(values, grad_out, model_gains, which, base, out, gain_grad):
    inverse = lax.rsqrt(row_mean(values * values) + norm_eps)
    gain = jnp.concatenate([model_gains[which, c][None, None, :] for c in range(out.shape[0])], axis=0)
    scaled = grad_out * gain
    centre = row_mean(scaled * values) * inverse * inverse
    out[...] = (base[...].astype(f32) + inverse * (scaled - values * centre)).astype(out.dtype)
    for c in range(out.shape[0]):
        gain_grad[c, :] = jnp.sum(grad_out[c] * values[c] * inverse[0], axis=0)


def attn_backward_kernel(
    width, hop, rows, grad_mixed, hidden, projected, values, pack, model_gains, gains, cosine,
    signed_sine, masks, grad_proj, grads, grad_hidden, gain_grad, head_gain_grads, *rest
):
    if hop:
        arrived, rest = rest[0], rest[1:]
    (
        held, total, summed_rows, keep, send_core, recv_core, send_half, recv_half,
        load_sems, send_sems, recv_sems,
    ) = rest
    exchange = Exchange(send_sems, recv_sems)
    exchange.greet(hop)
    loads = load_pack(pack, held, load_sems)
    for load in loads:
        load.start()
    chunks, own, cols = rows.shape
    length = 2 * own
    q_width = grads.shape[1] // 2
    kv_width = q_width // 2
    kv_heads = kv_width // width
    group = q_width // kv_width
    for c in range(chunks):
        grad_proj[c, :own] = rows[c]

    def project(c):
        loads[c].wait()
        accumulate(total, grad_proj[c], held, c * cols, 2 * q_width, q_width, c == 0)

    copies = gather_then(exchange, grad_proj, project)
    cos, sin = cosine[...], signed_sine[...]
    gain_q, gain_k = gains[0:1, :], gains[1:2, :]
    scale = width ** (-0.5)
    gain_q_sum = jnp.zeros((1, width), f32)
    gain_k_sum = jnp.zeros((1, width), f32)
    for seq in range(2):
        at = slice(seq * length, (seq + 1) * length)
        allowed = masks[seq] > 0.5
        for kv in range(kv_heads):
            raw_k = projected[at, q_width + kv * width : q_width + (kv + 1) * width]
            value = values[at, kv * width : (kv + 1) * width]
            inverse_k, key_rot = rotated(raw_k, gain_k, cos, sin)
            grad_key = jnp.zeros((length, width), f32)
            grad_value = jnp.zeros((length, width), f32)
            for one in range(group):
                head = slice((kv * group + one) * width, (kv * group + one + 1) * width)
                raw_q = projected[at, head]
                grad_head = total[at, head].astype(bf16)
                inverse_q, query_rot = rotated(raw_q, gain_q, cos, sin)
                weights = softmax_rows(query_rot, key_rot, allowed, scale)
                grad_weights = dot_nt(grad_head, value)
                delta = jnp.sum(weights * grad_weights, axis=-1, keepdims=True)
                grad_scores = (weights * (grad_weights - delta)).astype(bf16)
                grad_value += dot_tn(weights.astype(bf16), grad_head)
                grad_key += dot_tn(grad_scores, query_rot)
                grad_query = dot_nn(grad_scores, key_rot) * scale
                grad_query = grad_query * cos - pltpu.roll(grad_query, 64, 1) * sin
                gain_q_sum += jnp.sum(grad_query * raw_q * inverse_q, axis=0, keepdims=True)
                grads[at, head] = norm_back(grad_query, raw_q, inverse_q, gain_q).astype(bf16)
            grad_key = grad_key * scale
            grad_key = grad_key * cos - pltpu.roll(grad_key, 64, 1) * sin
            gain_k_sum += jnp.sum(grad_key * raw_k * inverse_k, axis=0, keepdims=True)
            first = q_width + kv * width
            grads[at, first : first + width] = norm_back(grad_key, raw_k, inverse_k, gain_k).astype(bf16)
            first += kv_width
            grads[at, first : first + width] = grad_value.astype(bf16)
    head_gain_grads[...] = jnp.concatenate(
        [gain_q_sum, gain_k_sum, jnp.zeros((6, width), f32)], axis=0
    )

    def make(c):
        return dot_nt(grads[...], held[c * cols : (c + 1) * cols, : 2 * q_width])

    def finish(c, summed):
        summed_rows[c] = summed

    copies += scatter_from(exchange, make, finish, keep, send_core, recv_core, send_half, recv_half)
    norm_step(
        hidden[...].astype(f32), summed_rows[...], model_gains, 0, grad_mixed, grad_hidden, gain_grad
    )
    if hop:
        hops = [
            exchange.copy(grad_hidden.at[c], arrived.at[c], exchange.section, 4, c)
            for c in range(chunks)
        ]
        for copy in hops:
            copy.start()
        for copy in hops:
            copy.wait()
    for copy in copies:
        copy.wait_send()


def weight_grad_kernel(split, first_a, first_b, second_a, second_b, main_a, main_b, last_a, last_b, out):
    step = pl.program_id(0)

    @pl.when(step < split)
    def _():
        out[...] = (dot_nn(first_a[...], main_a[...]) + dot_nn(first_b[...], main_b[...])).astype(bf16)

    @pl.when(step >= split)
    def _():
        out[...] = (dot_nn(second_a[...], last_a[...]) + dot_nn(second_b[...], last_b[...])).astype(bf16)


VMEM_SPEC = pl.BlockSpec(memory_space=pltpu.VMEM)
ANY_SPEC = pl.BlockSpec(memory_space=pl.ANY)


def shape(dims, kind):
    return jax.ShapeDtypeStruct(dims, kind)


def exchange_scratch(chunks, own, cols):
    return [
        pltpu.VMEM((chunks, 2 * own, cols), f32),
        pltpu.VMEM((chunks, 2 * own, cols), bf16),
        pltpu.VMEM((chunks, 2 * own, cols), bf16),
        pltpu.VMEM((chunks, own, cols), bf16),
        pltpu.VMEM((chunks, own, cols), bf16),
        pltpu.SemaphoreType.DMA((4,)),
    ]


def exchange_sems(chunks):
    return [pltpu.SemaphoreType.DMA((5, chunks)), pltpu.SemaphoreType.DMA((5, chunks))]


def params(mib, number=None):
    if number is None:
        return pltpu.CompilerParams(vmem_limit_bytes=mib * MIB)
    return pltpu.CompilerParams(
        vmem_limit_bytes=mib * MIB, collective_id=number, has_side_effects=True
    )


def cost(flops, size):
    return pl.CostEstimate(flops=int(flops), bytes_accessed=int(size), transcendentals=0)


def attn_forward(hidden, pack, model_gains, gains, tables, masks):
    chunks, own, cols = hidden.shape
    tokens, q_width, width = 4 * own, pack.shape[1] // 3, gains.shape[1]
    return pl.pallas_call(
        functools.partial(attn_forward_kernel, width),
        in_specs=[VMEM_SPEC, ANY_SPEC] + [VMEM_SPEC] * 5,
        out_specs=[VMEM_SPEC] * 6,
        out_shape=[
            shape((chunks, tokens, cols), bf16),
            shape((tokens, 2 * q_width), f32),
            shape((tokens, q_width // 2), bf16),
            shape((tokens, q_width), bf16),
            shape((chunks, own, cols), f32),
            shape((chunks, own, cols), bf16),
        ],
        scratch_shapes=[pltpu.VMEM(pack.shape, bf16)]
        + exchange_scratch(chunks, own, cols)
        + exchange_sems(chunks),
        compiler_params=params(40, 0),
        cost_estimate=cost(2 * tokens * pack.size, pack.size * 2),
        name="attn_forward",
    )(hidden, pack, model_gains, gains, *tables, masks)


def ffn_forward(rows, mixed, pack, hop):
    chunks, own, cols = rows.shape
    tokens, units = 4 * own, pack.shape[1] // 3
    scratch = exchange_scratch(chunks, own, cols)
    return pl.pallas_call(
        functools.partial(ffn_forward_kernel, hop),
        in_specs=[VMEM_SPEC, VMEM_SPEC, ANY_SPEC],
        out_specs=[VMEM_SPEC, ANY_SPEC] + [VMEM_SPEC] * (3 if hop else 2),
        out_shape=[
            shape((chunks, tokens, cols), bf16),
            shape((tokens, 2 * units), f32),
            shape((tokens, units), bf16),
        ]
        + [shape((chunks, own, cols), bf16)] * (2 if hop else 1),
        scratch_shapes=[pltpu.VMEM(pack.shape, bf16), pltpu.VMEM((tokens, 2 * units), f32)]
        + scratch
        + [pltpu.SemaphoreType.DMA((1,))]
        + exchange_sems(chunks),
        compiler_params=params(52, 1 if hop else 2),
        cost_estimate=cost(2 * tokens * pack.size, pack.size * 2),
        name="ffn_forward",
    )(rows, mixed, pack)


def ffn_backward(rows, mixed, gate_up, pack, model_gains):
    chunks, own, cols = rows.shape
    tokens, units = 4 * own, pack.shape[1] // 3
    return pl.pallas_call(
        ffn_backward_kernel,
        in_specs=[VMEM_SPEC, VMEM_SPEC, ANY_SPEC, ANY_SPEC, VMEM_SPEC],
        out_specs=[VMEM_SPEC] * 5,
        out_shape=[
            shape((chunks, tokens, cols), bf16),
            shape((tokens, 2 * units), bf16),
            shape((chunks, own, cols), f32),
            shape((chunks, own, cols), bf16),
            shape((chunks, cols), f32),
        ],
        scratch_shapes=[
            pltpu.VMEM(pack.shape, bf16),
            pltpu.VMEM((tokens, 2 * units), f32),
            pltpu.VMEM((tokens, units), f32),
        ]
        + exchange_scratch(chunks, own, cols)
        + [pltpu.SemaphoreType.DMA((1,))]
        + exchange_sems(chunks),
        compiler_params=params(56, 3),
        cost_estimate=cost(2 * tokens * pack.size, pack.size * 2),
        name="ffn_backward",
    )(rows, mixed, gate_up, pack, model_gains)


def attn_backward(
    rows, grad_mixed, hidden, projected, values, pack, model_gains, gains, tables, masks, hop
):
    chunks, own, cols = rows.shape
    tokens, q_width, width = 4 * own, pack.shape[1] // 3, gains.shape[1]
    return pl.pallas_call(
        functools.partial(attn_backward_kernel, width, hop),
        in_specs=[VMEM_SPEC] * 5 + [ANY_SPEC] + [VMEM_SPEC] * 5,
        out_specs=[VMEM_SPEC] * (6 if hop else 5),
        out_shape=[
            shape((chunks, tokens, cols), bf16),
            shape((tokens, 2 * q_width), bf16),
            shape((chunks, own, cols), bf16),
            shape((chunks, cols), f32),
            shape((8, width), f32),
        ]
        + [shape((chunks, own, cols), bf16)] * (1 if hop else 0),
        scratch_shapes=[
            pltpu.VMEM(pack.shape, bf16),
            pltpu.VMEM((tokens, q_width), f32),
            pltpu.VMEM((chunks, own, cols), f32),
        ]
        + exchange_scratch(chunks, own, cols)
        + exchange_sems(chunks),
        compiler_params=params(40, 4 if hop else 5),
        cost_estimate=cost(2 * tokens * pack.size, pack.size * 2),
        name="attn_backward",
    )(rows, grad_mixed, hidden, projected, values, pack, model_gains, gains, *tables, masks)


def weight_grad(first, second, main, last):
    depth, tokens = first[0].shape
    blk = 512
    split, rest = main[0].shape[1] // blk, last[0].shape[1] // blk
    turned = pl.BlockSpec((depth, tokens), lambda step: (0, 0))
    main_spec = pl.BlockSpec((tokens, blk), lambda step: (0, jnp.minimum(step, split - 1)))
    last_spec = pl.BlockSpec((tokens, blk), lambda step: (0, jnp.maximum(step - split, 0)))
    width = (split + rest) * blk
    return pl.pallas_call(
        functools.partial(weight_grad_kernel, split),
        grid=(split + rest,),
        in_specs=[turned] * 4 + [main_spec] * 2 + [last_spec] * 2,
        out_specs=pl.BlockSpec((depth, blk), lambda step: (0, step)),
        out_shape=shape((depth, width), bf16),
        compiler_params=params(40),
        cost_estimate=cost(4 * depth * tokens * width, 2 * depth * width),
        name="weight_grad",
    )(*first, *second, *main, *last)


def rope_tables(position, head_width):
    exponent = jnp.arange(0, head_width, 2).astype(f32) / head_width
    inverse = rope_base ** (-exponent)
    angles = position.astype(f32)[:, None] * inverse[None, :]
    cosine, sine = jnp.cos(angles), jnp.sin(angles)
    return (
        jnp.concatenate([cosine, cosine], axis=-1),
        jnp.concatenate([-sine, sine], axis=-1),
    )


def per_device(
    block_input,
    segment_ids,
    out_cotangent,
    attn_norm,
    q_weight,
    k_weight,
    v_weight,
    o_weight,
    q_norm,
    k_norm,
    ffn_norm,
    gate_weight,
    up_weight,
    down_weight,
):
    section = lax.axis_index("section")
    place = lax.axis_index("dp")
    core = place % 2
    half = lax.axis_index("tensor")
    n_dp = lax.axis_size("dp")
    n_chip = n_dp // 2
    micro_count, own_rows, depth = block_input.shape
    length = 2 * own_rows
    head_width = q_norm.shape[1]
    first_core = core == 0
    swap_core = [(i, i ^ 1) for i in range(n_dp)]
    swap_half = [(0, 1), (1, 0)]
    chip_groups = [[2 * chip + one for chip in range(n_chip)] for one in (0, 1)]

    def to_core(values):
        return lax.ppermute(values, "dp", swap_core)

    def to_half(values):
        return lax.ppermute(values, "tensor", swap_half)

    def split_columns(weight):
        side = weight.shape[1] // 2
        left, right = weight[:, :side], weight[:, side:]
        return jnp.where(first_core, left, right), jnp.where(first_core, right, left)

    def split_rows(weight):
        side = weight.shape[0] // 2
        left, right = weight[:side].T, weight[side:].T
        return jnp.where(first_core, left, right), jnp.where(first_core, right, left)

    def gathered(pairs):
        mine = jnp.concatenate([pair[0] for pair in pairs], axis=1)
        theirs = to_core(jnp.concatenate([pair[1] for pair in pairs], axis=1))
        chip_block = jnp.concatenate(
            [jnp.where(first_core, mine, theirs), jnp.where(first_core, theirs, mine)], axis=0
        )
        return lax.all_gather(
            chip_block, "dp", axis=0, tiled=True, axis_index_groups=chip_groups
        )

    attn_pack = gathered(
        [
            split_columns(q_weight[0]),
            split_columns(k_weight[0]),
            split_columns(v_weight[0]),
            split_rows(o_weight[0]),
        ]
    )
    ffn_pack = gathered(
        [split_columns(gate_weight[0]), split_columns(up_weight[0]), split_rows(down_weight[0])]
    )

    cols = depth // row_chunks
    model_gains = jnp.concatenate([attn_norm, ffn_norm], axis=0).reshape(2, row_chunks, cols)
    head_gains = jnp.concatenate([q_norm, k_norm, jnp.zeros((6, head_width), f32)], axis=0)

    def chunked(rows):
        return rows.reshape(rows.shape[0], row_chunks, cols).transpose(1, 0, 2)

    def joined(rows):
        return rows.transpose(1, 0, 2).reshape(rows.shape[1], depth)

    def turned(rows):
        return rows.transpose(0, 2, 1).reshape(depth, rows.shape[1])

    inputs = [chunked(block_input[micro]) for micro in range(2)]
    cotangents = [chunked(out_cotangent[micro]) for micro in range(2)]

    def arranged(values):
        sides = values[..., :own_rows], values[..., own_rows:]
        return jnp.concatenate(
            [jnp.where(half == 0, *sides), jnp.where(half == 0, *sides[::-1])], axis=-1
        )

    position = arranged(jnp.arange(length, dtype=jnp.int32))
    tables = rope_tables(position, head_width)
    ids = arranged(jnp.stack([segment_ids, to_core(segment_ids)], axis=1))
    causal = position[:, None] >= position[None, :]
    masks = (causal & (ids[..., :, None] == ids[..., None, :])).astype(f32)

    at_first = section == 0

    def pick(first, second):
        return jax.tree.map(lambda a, b: jnp.where(at_first, a, b), first, second)

    zero_rows = jnp.zeros_like(inputs[0])
    forward_masks = [masks[0], pick(masks[1], masks[0]), masks[1]]
    results, backs, saves, arrived = [], [], [], zero_rows
    for step in range(3):
        hidden = inputs[step] if step < 2 else zero_rows
        if step > 0:
            hidden = pick(hidden, arrived)
        normed, projected, values, attended, mixed, rows = attn_forward(
            hidden, attn_pack, model_gains, head_gains, tables, forward_masks[step]
        )
        normed_ffn, gate_up, activated, result, *rest = ffn_forward(rows, mixed, ffn_pack, step < 2)
        arrived = rest[0] if rest else None
        results.append(result)
        backs.append((hidden, projected, values, mixed, gate_up))
        saves.append((normed, attended, normed_ffn, activated))
    def forward_pair(item):
        return [pick(saves[micro][item], saves[micro + 1][item]) for micro in range(2)]

    def backward_pair(table, item):
        return [pick(table[micro + 1][item], table[micro][item]) for micro in range(2)]

    def turned_pair(pair):
        return [turned(rows) for rows in pair]

    backward_masks = [masks[0], pick(masks[0], masks[1]), masks[1]]
    grads, ffn_saves, attn_saves, gain_total, arrived = [], [], [], None, zero_rows
    for step in range(3):
        rows = pick(arrived, cotangents[step] if step < 2 else zero_rows)
        back = pick(backs[0], backs[2]) if step == 1 else backs[1]
        hidden, projected, values, mixed, gate_up = back
        grad_down, ffn_grads, grad_mixed, proj_rows, ffn_gain_grad = ffn_backward(
            rows, mixed, gate_up, ffn_pack, model_gains
        )
        ffn_saves.append((grad_down, ffn_grads))
        if step == 2:
            ffn_partial = weight_grad(
                turned_pair(forward_pair(2)),
                turned_pair(backward_pair(ffn_saves, 0)),
                backward_pair(ffn_saves, 1),
                forward_pair(3),
            )
            proj_rows, ffn_partial = lax.optimization_barrier((proj_rows, ffn_partial))
        grad_proj, attn_grads, grad_hidden, attn_gain_grad, head_gain_grads, *rest = attn_backward(
            proj_rows, grad_mixed, hidden, projected, values, attn_pack, model_gains, head_gains,
            tables, backward_masks[step], step < 2,
        )
        arrived = rest[0] if rest else None
        grads.append(grad_hidden)
        attn_saves.append((grad_proj, attn_grads))
        gains = (attn_gain_grad, ffn_gain_grad, head_gain_grads)
        gain_total = gains if gain_total is None else jax.tree.map(jnp.add, gain_total, gains)

    section_outputs = jnp.stack(
        [joined(pick(results[micro], results[micro + 1])) for micro in range(2)]
    )[None]
    section_input_grads = jnp.stack(
        [joined(pick(grads[micro + 1], grads[micro])) for micro in range(2)]
    )[None]

    def scattered(partial):
        return lax.psum_scatter(
            partial, "dp", scatter_dimension=0, tiled=True, axis_index_groups=chip_groups
        )

    def owned(rows):
        side = rows.shape[0] // 2
        own = jnp.where(first_core, rows[:side], rows[side:])
        other = to_core(jnp.where(first_core, rows[side:], rows[:side]))
        return (
            jnp.where(first_core, own, other).astype(f32),
            jnp.where(first_core, other, own).astype(f32),
        )

    attn_partial = weight_grad(
        turned_pair(forward_pair(0)),
        turned_pair(backward_pair(attn_saves, 0)),
        backward_pair(attn_saves, 1),
        forward_pair(1),
    )
    attn_partial, ffn_rows = lax.optimization_barrier((attn_partial, scattered(ffn_partial)))
    ffn_sides = owned(ffn_rows)
    attn_sides = owned(scattered(attn_partial))
    units = gate_weight.shape[2] // 2
    q_width = q_weight.shape[2] // 2
    kv_width = k_weight.shape[2] // 2

    def across(sides, first, width):
        return jnp.concatenate([side[:, first : first + width] for side in sides], axis=1)[None]

    def down(sides, first):
        return jnp.concatenate([side[:, first:].T for side in sides], axis=0)[None]

    packed = jnp.concatenate(
        [
            gain_total[0].reshape(-1),
            gain_total[1].reshape(-1),
            gain_total[2][0],
            gain_total[2][1],
        ]
    ).reshape(-1, head_width)
    packed = packed + to_core(packed)
    packed = packed + to_half(packed)
    reach = 2
    while reach < n_dp:
        packed = packed + lax.ppermute(packed, "dp", [(i, i ^ reach) for i in range(n_dp)])
        reach *= 2
    packed = packed.reshape(-1)
    return (
        section_outputs,
        section_input_grads,
        packed[None, :depth],
        across(attn_sides, 0, q_width),
        across(attn_sides, q_width, kv_width),
        across(attn_sides, q_width + kv_width, kv_width),
        down(attn_sides, 2 * q_width),
        packed[None, 2 * depth : 2 * depth + head_width],
        packed[None, 2 * depth + head_width :],
        packed[None, depth : 2 * depth],
        across(ffn_sides, 0, units),
        across(ffn_sides, units, units),
        down(ffn_sides, 2 * units),
    )


def solution(mesh):
    rows = P(None, ("dp", "tensor"), None)
    out_rows = P("section", None, ("dp", "tensor"), None)
    gain = P("section", None)
    wide = P("section", "dp", "tensor")
    tall = P("section", "tensor", "dp")
    return jax.shard_map(
        per_device,
        mesh=mesh,
        in_specs=(
            rows, P(None, "dp"), rows, gain, wide, wide, wide, tall, gain, gain, gain, wide, wide, tall,
        ),
        out_specs=(
            out_rows, out_rows, gain, wide, wide, wide, tall, gain, gain, gain, wide, wide, tall,
        ),
        check_vma=False,
    )
```

time: 1860 us -> 994 us (0.53)
  waiting for transfers between devices: 1000 us -> 343 us
  Pallas kernels: 216 us -> 480 us
  local copies, waits for them, and re-layouts: 264 us -> 80.8 us
  other arithmetic: 225 us -> 62.8 us
  starting transfers between devices: 127 us -> 6.04 us
    ppermute x49 -> x1, waiting for transfers between devices: 524 us -> 0.01 us  [to_half(): return lax.ppermute(values, 'tensor', swap_half)]
    pallas_call x26 -> x14, Pallas kernels: 216 us -> 480 us  [the longest x3 137 us: attn_backward(): pl.pallas_call(functools.partial(attn_backward_kernel, width, hop), in_sp...]
    ppermute x8 -> x0, waiting for transfers between devices: 146 us -> none  [the longest x4 101 us: per_device(): arrived = lax.ppermute(grads[step - 1][chunk], 'section', backward_route)]
    unnamed x738 -> x234, local copies, waits for them, and re-layouts: 138 us -> 47.1 us
    ppermute x49 -> x1, starting transfers between devices: 91 us -> 1.5 us  [to_half(): return lax.ppermute(values, 'tensor', swap_half)]
    ppermute x56 -> x6, waiting for transfers between devices: 52.7 us -> 8.79 us  [to_core(): return lax.ppermute(values, 'dp', swap_core)]
    select_n x35 -> x13, other arithmetic: 60.8 us -> 19.5 us  [pick(): return jax.tree.map(lambda a, b: jnp.where(at_first, a, b), first, second)]
    all_gather x2, waiting for transfers between devices: 152 us -> 191 us  [gathered(): lax.all_gather(chip_block, 'dp', axis=0, tiled=True, axis_index_groups=ch...]
  transfers between devices with their start and end apart: 119 -> 13, of which waited for: 94 -> 8; matrix products, arithmetic and copies ran while one was open for 9% -> 6% of each run, Pallas kernels for 2% -> 7%
where the time goes in v2:
time: 994 us; the launch traced here: 988 us
  Pallas kernels  480 us (48%)
  waiting for transfers between devices  343 us (35%)
  local copies, waits for them, and re-layouts  80.8 us (8%)
  other arithmetic  62.8 us (6%)
  between operations  15.4 us (2%)
    all_gather x2, waiting for transfers between devices, gathered(): lax.all_gather(chip_block, 'dp', axis=0, tiled=True, axis_index_groups=ch...  191 us
    reduce_scatter x2, waiting for transfers between devices, scattered(): lax.psum_scatter(partial, 'dp', scatter_dimension=0, tiled=True, axis_ind...  141 us
    pallas_call x3, Pallas kernels, attn_backward(): pl.pallas_call(functools.partial(attn_backward_kernel, width, hop), in_sp...  137 us
    pallas_call x3, Pallas kernels, ffn_forward(): pl.pallas_call(functools.partial(ffn_forward_kernel, hop), in_specs=[VMEM...  123 us
    pallas_call x3, Pallas kernels, ffn_backward(): pl.pallas_call(ffn_backward_kernel, in_specs=[VMEM_SPEC, VMEM_SPEC, ANY_S...  97.7 us
    pallas_call x3, Pallas kernels, attn_forward(): pl.pallas_call(functools.partial(attn_forward_kernel, width), in_specs=[V...  90.2 us
    unnamed x234, local copies, waits for them, and re-layouts  47.1 us
    pallas_call x2, Pallas kernels, weight_grad(): pl.pallas_call(functools.partial(weight_grad_kernel, split), grid=(split...  32.2 us
  transfers between devices with their start and end apart: 13, of which 8 were waited for; matrix products, arithmetic and copies ran while one was open for 6% of the time, Pallas kernels for 7%

profile of v2, /device:TPU:0, one launch (start us, length us, event | category | flops | bytes accessed | tf_op | source)
XLA Modules:
  0.0 988.1 jit_solution(7147790204531224969)
XLA Ops:
  18.2 4.2 collective-permute-done.2
  33.6 52.8 %all-gather.3.cloned.1.call-done.pack = bf16[2048,1536]{1,0:T(8,128)(2,1)} async-done(((bf16[512,1536]{1,0:T(8,128)(2,1)}), bf16[2048,1536]{1,0:T(8,128)(2,1)}) %all-gather.3.cloned.1.call-update) | async-done | bytes 6291472 | tf_op jit(solution)/shard_map/all_gather | solution.py:672
  86.4 2.8 copy-done
  90.2 30.2 %attn_forward.3 = (bf16[4,384,512]{2,1,0:T(8,128)(2,1)S(1)}, f32[384,1024]{1,0:T(8,128)S(1)}, bf16[384,256]{1,0:T(8,128)(2,1)S(1)}, bf16[384,512]{1,0:T(8,128)(2...) custom-call(bf16[4,96,512]{2,1,0:T(8,128)(2,1)S(1)} %bitcast.133, bf16[2048,1536]{1,0:T(8,128)(2,1)S(1)} %copy-done, ...), custom_call_target="tpu_custom_call" | custom-call | flops 2415919104 | bytes 6291456 | tf_op jit(solution)/shard_map/attn_forward/pallas_call | solution.py:486
  125.8 138.4 %all-gather.5.cloned.1.call-done.pack = bf16[2048,4608]{1,0:T(8,128)(2,1)} async-done(((bf16[512,4608]{1,0:T(8,128)(2,1)}), bf16[2048,4608]{1,0:T(8,128)(2,1)}) %all-gather.5.cloned.1.call-update) | async-done | bytes 18874384 | tf_op jit(solution)/shard_map/all_gather | solution.py:672
  266.4 46.2 %ffn_forward.3 = (bf16[4,384,512]{2,1,0:T(8,128)(2,1)}, f32[384,3072]{1,0:T(8,128)}, bf16[384,1536]{1,0:T(8,128)(2,1)}, bf16[4,96,512]{2,1,0:T(8,128)(2,1)S(1)}, bf16[4,96,512]{2,1,0:T(8,128)(2,1)S(1)}) custom-call(bf16[4,96,512]{2,1,0:T(8,128)(2,1)S(1)} %copy-done.79, f32[4,96,512]{2,1,0:T(8,128)S(1)} %copy-done.27, ...), custom_call_target="tpu_custom_call" | custom-call | flops 7247757312 | bytes 18874368 | tf_op jit(solution)/shard_map/ffn_forward/pallas_call | solution.py:511
  312.7 29.9 %attn_forward.4 = (bf16[4,384,512]{2,1,0:T(8,128)(2,1)S(1)}, f32[384,1024]{1,0:T(8,128)S(1)}, bf16[384,256]{1,0:T(8,128)(2,1)S(1)}, bf16[384,512]{1,0:T(8,128)(2...) custom-call(bf16[4,96,512]{2,1,0:T(8,128)(2,1)S(1)} %bitcast_select_fusion.1.hidden, ...), custom_call_target="tpu_custom_call" | custom-call | flops 2415919104 | bytes 6291456 | tf_op jit(solution)/shard_map/attn_forward/pallas_call | solution.py:486
  346.4 45.3 %ffn_forward.4 = (bf16[4,384,512]{2,1,0:T(8,128)(2,1)}, f32[384,3072]{1,0:T(8,128)}, bf16[384,1536]{1,0:T(8,128)(2,1)}, bf16[4,96,512]{2,1,0:T(8,128)(2,1)S(1)}, bf16[4,96,512]{2,1,0:T(8,128)(2,1)S(1)}) custom-call(bf16[4,96,512]{2,1,0:T(8,128)(2,1)S(1)} %get-tuple-element.85.rows, f32[4,96,512]{2,1,0:T(8,128)S(1)} %get-tuple-element.86.mixed, ...), custom_call_target="tpu_custom_call" | custom-call | flops 7247757312 | bytes 18874368 | tf_op jit(solution)/shard_map/ffn_forward/pallas_call | solution.py:511
  392.6 30.1 %attn_forward.5 = (bf16[4,384,512]{2,1,0:T(8,128)(2,1)S(1)}, f32[384,1024]{1,0:T(8,128)S(1)}, bf16[384,256]{1,0:T(8,128)(2,1)S(1)}, bf16[384,512]{1,0:T(8,128)(2...) custom-call(bf16[4,96,512]{2,1,0:T(8,128)(2,1)S(1)} %get-tuple-element.238.hidden, ...), custom_call_target="tpu_custom_call" | custom-call | flops 2415919104 | bytes 6291456 | tf_op jit(solution)/shard_map/attn_forward/pallas_call | solution.py:486
  426.0 31.6 %ffn_forward.5 = (bf16[4,384,512]{2,1,0:T(8,128)(2,1)}, f32[384,3072]{1,0:T(8,128)}, bf16[384,1536]{1,0:T(8,128)(2,1)}, bf16[4,96,512]{2,1,0:T(8,128)(2,1)S(1)}) custom-call(bf16[4,96,512]{2,1,0:T(8,128)(2,1)S(1)} %get-tuple-element.89.rows, f32[4,96,512]{2,1,0:T(8,128)S(1)} %get-tuple-element.90.mixed, bf16[2048,4608]{1,0:T(8,128)(2,1)} %all-gather.5.cloned.1.call-done.pack), custom_call_target="tpu_custom_call" | custom-call | flops 7247757312 | bytes 18874368 | tf_op jit(solution)/shard_map/ffn_forward/pallas_call | solution.py:511
  457.6 5.7 broadcast_select_fusion.2.gate_up
  463.3 32.8 %ffn_backward.3 = (bf16[4,384,512]{2,1,0:T(8,128)(2,1)}, bf16[384,3072]{1,0:T(8,128)(2,1)}, f32[4,96,512]{2,1,0:T(8,128)}, bf16[4,96,512]{2,1,0:T(8,128)(2,1)}, f32[4,512]{1,0:T(4,128)}) custom-call(bf16[4,96,512]{2,1,0:T(8,128)(2,1)} %bitcast.137, f32[4,96,512]{2,1,0:T(8,128)} %copy-done.77, f32[384,3072]{1,0:T(8,128)} %get-tuple-element.92.gate_up, ...), custom_call_target="tpu_custom_call" | custom-call | flops 7247757312 | bytes 18874368 | tf_op jit(solution)/shard_map/ffn_backward/pallas_call | solution.py:534
  500.6 51.7 %attn_backward.3 = (bf16[4,384,512]{2,1,0:T(8,128)(2,1)S(1)}, bf16[384,1024]{1,0:T(8,128)(2,1)S(1)}, bf16[4,96,512]{2,1,0:T(8,128)(2,1)S(1)}, f32[4,512]{1,0:T(4...) custom-call(bf16[4,96,512]{2,1,0:T(8,128)(2,1)S(1)} %copy-done.42, f32[4,96,512]{2,1,0:T(8,128)S(1)} %copy-done.30, ...), custom_call_target="tpu_custom_call" | custom-call | flops 2415919104 | bytes 6291456 | tf_op jit(solution)/shard_map/attn_backward/pallas_call | solution.py:564
  556.2 32.5 %ffn_backward.4 = (bf16[4,384,512]{2,1,0:T(8,128)(2,1)}, bf16[384,3072]{1,0:T(8,128)(2,1)}, f32[4,96,512]{2,1,0:T(8,128)}, bf16[4,96,512]{2,1,0:T(8,128)(2,1)}, f32[4,512]{1,0:T(4,128)}) custom-call(bf16[4,96,512]{2,1,0:T(8,128)(2,1)} %bitcast_select_fusion.rows, f32[4,96,512]{2,1,0:T(8,128)} %broadcast_select_fusion.24.mixed, ...), custom_call_target="tpu_custom_call" | custom-call | flops 7247757312 | bytes 18874368 | tf_op jit(solution)/shard_map/ffn_backward/pallas_call | solution.py:534
  593.1 51.8 %attn_backward.4 = (bf16[4,384,512]{2,1,0:T(8,128)(2,1)S(1)}, bf16[384,1024]{1,0:T(8,128)(2,1)S(1)}, bf16[4,96,512]{2,1,0:T(8,128)(2,1)S(1)}, f32[4,512]{1,0:T(4...) custom-call(bf16[4,96,512]{2,1,0:T(8,128)(2,1)S(1)} %copy-done.41, f32[4,96,512]{2,1,0:T(8,128)S(1)} %copy-done.29, ...), custom_call_target="tpu_custom_call" | custom-call | flops 2415919104 | bytes 6291456 | tf_op jit(solution)/shard_map/attn_backward/pallas_call | solution.py:564
  648.5 32.3 %ffn_backward.5 = (bf16[4,384,512]{2,1,0:T(8,128)(2,1)}, bf16[384,3072]{1,0:T(8,128)(2,1)}, f32[4,96,512]{2,1,0:T(8,128)}, bf16[4,96,512]{2,1,0:T(8,128)(2,1)}, f32[4,512]{1,0:T(4,128)}) custom-call(bf16[4,96,512]{2,1,0:T(8,128)(2,1)} %broadcast_select_fusion.22.rows, f32[4,96,512]{2,1,0:T(8,128)} %copy-done.77, f32[384,3072]{1,0:T(8,128)} %get-tuple-element.92.gate_up, ...), custom_call_target="tpu_custom_call" | custom-call | flops 7247757312 | bytes 18874368 | tf_op jit(solution)/shard_map/ffn_backward/pallas_call | solution.py:534
  680.9 3.3 select_bitcast_fusion.4
  686.1 2.6 copy.55
  688.7 3.8 select_bitcast_fusion.6
  695.1 2.6 copy.53
  703.8 23.3 %weight_grad.2 = bf16[2048,4608]{1,0:T(8,128)(2,1)} custom-call(bf16[2048,384]{1,0:T(8,128)(2,1)S(1)} %bitcast.131, bf16[2048,384]{1,0:T(8,128)(2,1)S(1)} %bitcast.132, bf16[2048,384]{1,0:T(8,128)(2,1)S(1)} %bitcast.127, bf16[2048,384]{1,0:T(8,128)(2,1)S(1)} %bitcast.128, bf16[384,3072]{1,0:T(8,128)(2,1)S(1)} %get-tuple-element.188.main_a, ...), custom_call_target="tpu_custom_call" | custom-call | flops 14495514624 | bytes 18874368 | tf_op jit(solution)/shard_map/weight_grad/pallas_call | solution.py:597
  728.7 2.9 copy-done.1
  732.8 33.2 %attn_backward.5 = (bf16[4,384,512]{2,1,0:T(8,128)(2,1)S(1)}, bf16[384,1024]{1,0:T(8,128)(2,1)S(1)}, bf16[4,96,512]{2,1,0:T(8,128)(2,1)S(1)}, f32[4,512]{1,0:T(4,128)S(1)}, f32[8,128]{1,0:T(8,128)S(1)}) custom-call(bf16[4,96,512]{2,1,0:T(8,128)(2,1)S(1)} %copy-done.40, f32[4,96,512]{2,1,0:T(8,128)S(1)} %copy-done.25, ...), custom_call_target="tpu_custom_call" | custom-call | flops 2415919104 | bytes 6291456 | tf_op jit(solution)/shard_map/attn_backward/pallas_call | solution.py:564
  770.3 3.8 select_bitcast_fusion.2
  776.7 2.6 copy.58
  783.1 8.9 weight_grad.3
  792.0 103.6 %reduce-scatter.3.cloned.1.call-done = bf16[512,4608]{1,0:T(8,128)(2,1)} async-done(((bf16[2048,4608]{1,0:T(8,128)(2,1)}), bf16[512,4608]{1,0:T(8,128)(2,1)}) %reduce-scatter.3.cloned.1.call-update) | async-done | bytes 4718608 | tf_op jit(solution)/shard_map/reduce_scatter | solution.py:781
  895.8 4.1 broadcast_select_fusion.3
  901.4 2.7 collective-permute-done.3
  922.3 3.0 select_convert_fusion.1
  932.1 37.3 %reduce-scatter.5.cloned.1.call-done = bf16[512,1536]{1,0:T(8,128)(2,1)} async-done(((bf16[2048,1536]{1,0:T(8,128)(2,1)}), bf16[512,1536]{1,0:T(8,128)(2,1)}) %reduce-scatter.5.cloned.1.call-update) | async-done | bytes 1572880 | tf_op jit(solution)/shard_map/reduce_scatter | solution.py:781
  971.0 3.5 maximum_bitcast_fusion.1
  (350 shorter events, 113.0 us)
Async XLA Ops:
  7.2 79.2 %all-gather.3.cloned.1.call-start = ((), (), s32[]{:S(2)}) async-start(), calls=%async_computation.2 | async-start | bytes 7864320 | tf_op jit(solution)/shard_map/all_gather | solution.py:672
  9.5 2.4 collective-permute-start
  13.5 250.8 %all-gather.5.cloned.1.call-start = ((), (), s32[]{:S(2)}) async-start(), calls=%async_computation.3 | async-start | bytes 23592960 | tf_op jit(solution)/shard_map/all_gather | solution.py:672
  17.8 4.6 collective-permute-start.2
  25.8 869.9 %reduce-scatter.3.cloned.1.call-start = ((), (), s32[]{:S(2)}) async-start(), calls=%async_computation.4 | async-start | bytes 23592960 | tf_op jit(solution)/shard_map/reduce_scatter | solution.py:781
  26.4 5.9 collective-permute-start.1
  27.9 364.6 %copy-start.61 = (f32[2,4,512]{2,1,0:T(4,128)}, f32[2,4,512]{2,1,0:T(4,128)S(1)}, u32[]{:S(2)}) copy-start(f32[2,4,512]{2,1,0:T(4,128)S(1)} %reshape.138.model_gains) | copy-start | bytes 49156
  32.7 87.7 %copy-start.6 = (f32[2,192,192]{2,1,0:T(8,128)}, f32[2,192,192]{2,1,0:T(8,128)S(1)}, u32[]{:S(2)}) copy-start(f32[2,192,192]{2,1,0:T(8,128)S(1)} %get-tuple-element.224.masks) | copy-start | bytes 884740
  90.2 222.5 %slice-start = ((s8[6291456]{0:T(1024)(128)(4,1)}), s8[2097152]{0:T(1024)(128)(4,1)S(1)}, s32[]{:S(2)}) async-start(s8[6291456]{0:T(1024)(128)(4,1)} %bitcast.123), calls=%async_computation.6 | async-start | bytes 4194304
  266.4 46.2 %copy-start.90 = (bf16[96,4,512]{2,1,0:T(4,128)(2,1)S(1)}, bf16[96,4,512]{2,1,0:T(4,128)(2,1)}, u32[]{:S(2)}) copy-start(bf16[96,4,512]{2,1,0:T(4,128)(2,1)} %reshape_squeeze.11) | copy-start | bytes 1179652
  266.4 46.3 %slice-start.1 = ((s8[6291456]{0:T(1024)(128)(4,1)}), s8[4194304]{0:T(1024)(128)(4,1)S(1)}, s32[]{:S(2)}) async-start(s8[6291456]{0:T(1024)(128)(4,1)} %bitcast.123), calls=%async_computation.7 | async-start | bytes 8388608
  266.4 46.3 %copy-start.60 = (f32[2,192,192]{2,1,0:T(8,128)S(1)}, f32[2,192,192]{2,1,0:T(8,128)}, u32[]{:S(2)}) copy-start(f32[2,192,192]{2,1,0:T(8,128)} %get-tuple-element.220.masks) | copy-start | bytes 884740
  345.6 46.0 %copy-start.77 = (f32[4,96,512]{2,1,0:T(8,128)}, f32[4,96,512]{2,1,0:T(8,128)S(1)}, u32[]{:S(2)}) copy-start(f32[4,96,512]{2,1,0:T(8,128)S(1)} %get-tuple-element.86.mixed) | copy-start | bytes 2359300
  346.4 45.3 %copy-start.85 = (bf16[96,4,512]{2,1,0:T(4,128)(2,1)S(1)}, bf16[96,4,512]{2,1,0:T(4,128)(2,1)}, u32[]{:S(2)}) copy-start(bf16[96,4,512]{2,1,0:T(4,128)(2,1)} %copy-done.84) | copy-start | bytes 1179652
  500.6 52.4 %copy-start.89 = (bf16[96,4,512]{2,1,0:T(4,128)(2,1)S(1)}, bf16[96,4,512]{2,1,0:T(4,128)(2,1)}, u32[]{:S(2)}) copy-start(bf16[96,4,512]{2,1,0:T(4,128)(2,1)} %reshape_squeeze.12) | copy-start | bytes 1179652
  500.6 53.3 %copy-start.10 = (f32[384,1024]{1,0:T(8,128)S(1)}, f32[384,1024]{1,0:T(8,128)}, u32[]{:S(2)}) copy-start(f32[384,1024]{1,0:T(8,128)} %copy-done.9) | copy-start | bytes 4718596
  500.6 53.3 %copy-start.12 = (f32[384,1024]{1,0:T(8,128)S(1)}, f32[384,1024]{1,0:T(8,128)}, u32[]{:S(2)}) copy-start(f32[384,1024]{1,0:T(8,128)} %copy-done.11) | copy-start | bytes 4718596
  647.7 33.1 %copy-start.73 = (f32[8,128]{1,0:T(8,128)}, f32[8,128]{1,0:T(8,128)S(1)}, u32[]{:S(2)}) copy-start(f32[8,128]{1,0:T(8,128)S(1)} %get-tuple-element.132) | copy-start | bytes 12292
  727.2 242.3 %reduce-scatter.5.cloned.1.call-start = ((), (), s32[]{:S(2)}) async-start(), calls=%async_computation.5 | async-start | bytes 7864320 | tf_op jit(solution)/shard_map/reduce_scatter | solution.py:781
  732.8 33.2 %copy-start.22 = (bf16[4,384,512]{2,1,0:T(8,128)(2,1)S(1)}, bf16[4,384,512]{2,1,0:T(8,128)(2,1)}, u32[]{:S(2)}) copy-start(bf16[4,384,512]{2,1,0:T(8,128)(2,1)} %copy-done.21) | copy-start | bytes 4718596
  732.8 33.2 %copy-start.24 = (bf16[4,384,512]{2,1,0:T(8,128)(2,1)S(1)}, bf16[4,384,512]{2,1,0:T(8,128)(2,1)}, u32[]{:S(2)}) copy-start(bf16[4,384,512]{2,1,0:T(8,128)(2,1)} %copy-done.23) | copy-start | bytes 4718596
  792.0 103.7 %copy-start.70 = (f32[4,512]{1,0:T(4,128)S(1)}, f32[4,512]{1,0:T(4,128)}, u32[]{:S(2)}) copy-start(f32[4,512]{1,0:T(4,128)} %copy-done.69) | copy-start | bytes 24580
  792.0 103.7 %copy-start.105 = (f32[4,512]{1,0:T(4,128)S(1)}, f32[4,512]{1,0:T(4,128)}, u32[]{:S(2)}) copy-start(f32[4,512]{1,0:T(4,128)} %get-tuple-element.128) | copy-start | bytes 24580
  792.0 103.7 %copy-start.106 = (f32[4,512]{1,0:T(4,128)S(1)}, f32[4,512]{1,0:T(4,128)}, u32[]{:S(2)}) copy-start(f32[4,512]{1,0:T(4,128)} %get-tuple-element.129) | copy-start | bytes 24580
  792.0 103.7 %copy-start.107 = (f32[4,512]{1,0:T(4,128)S(1)}, f32[4,512]{1,0:T(4,128)}, u32[]{:S(2)}) copy-start(f32[4,512]{1,0:T(4,128)} %get-tuple-element.130) | copy-start | bytes 24580
  899.9 22.3 %collective-permute-start.8 = (bf16[256,4608]{1,0:T(8,128)(2,1)}, bf16[256,4608]{1,0:T(8,128)(2,1)S(1)}, u32[]{:S(2)}, u32[]{:S(2)}) collective-permute-start(bf16[256,4608]{1,0:T(8,128)(2,1)} %broadcast_select_fusion.3), channel_id=1, source_target_pairs={{0,2},{2,0},{4,6},{6,4},{8,10},{10,8},{12,14},{14,12},{1,3},{3,1},... | collective-permute-start | bytes 7077896 | tf_op jit(solution)/shard_map/ppermute | solution.py:651
  900.1 4.1 collective-permute-start.3
  904.8 5.3 collective-permute-start.4
  911.4 4.8 collective-permute-start.5
  916.9 4.2 collective-permute-start.6
  932.1 38.9 %copy-start.81 = (f32[256,1536]{1,0:T(8,128)S(1)}, f32[256,1536]{1,0:T(8,128)}, u32[]{:S(2)}) copy-start(f32[256,1536]{1,0:T(8,128)} %get-tuple-element.178) | copy-start | bytes 4718596
  970.9 5.6 collective-permute-start.7
  (94 other events, 466.7 us)
Sparse Core Ops, SparseCore 0:
  13.6 72.7 all-gather.2
  88.3 175.9 all-gather.4
  727.3 168.3 reduce-scatter.2
  898.8 70.6 reduce-scatter.4

commit v3 on v2

--- a/solution.py
+++ b/solution.py
@@ -46,11 +46,19 @@
         self.core = {"dp": place + 1 - 2 * (place % 2)}
         self.half = {"tensor": 1 - lax.axis_index("tensor")}
         self.section = {"section": 1 - lax.axis_index("section")}
+        core, chip = place % 2, place // 2
+        across, along = chip % 2, chip // 2
+        self.chip = chip
+        numbers = (chip + 1 - 2 * across, chip + 2 - 4 * along, 3 - chip)
+        self.chips = [(number, {"dp": 2 * number + core}) for number in numbers]
         self.send_sems, self.recv_sems = send_sems, recv_sems
 
-    def greet(self, with_section):
+    def greet(self, with_section, with_chips=False):
+        others = [self.core, self.half] + ([self.section] if with_section else [])
+        self.meet(others + ([device for _, device in self.chips] if with_chips else []))
+
+    def meet(self, others):
         barrier = pltpu.get_barrier_semaphore()
-        others = [self.core, self.half] + ([self.section] if with_section else [])
         for other in others:
             pl.semaphore_signal(barrier, inc=1, device_id=other, device_id_type=MESH)
         pl.semaphore_wait(barrier, len(others))
@@ -92,7 +100,7 @@
     return first + second
 
 
-def scatter_from(exchange, make, finish, keep, send_core, recv_core, send_half, recv_half):
+def scatter_from(exchange, make, idle, finish, keep, send_core, recv_core, send_half, recv_half):
     chunks, pair, _ = keep.shape
     own = pair // 2
     first = [
@@ -118,19 +126,98 @@
             middle(c - 1)
     middle(chunks - 1)
     for c in range(chunks):
+        idle(c)
         second[c].wait_recv()
         finish(c, keep[c, :own] + recv_half[c].astype(f32))
     return first + second
 
 
-def load_pack(pack, held, sems):
-    depth = held.shape[0] // 4
+def chip_gather_kernel(block, out, local_sems, send_sems, recv_sems):
+    exchange, local = Exchange(send_sems, recv_sems), Local(local_sems)
+    (across, across_device), (along, along_device), _ = exchange.chips
+    exchange.meet([across_device, along_device])
+    half = block.shape[0] // 2
+    first, last = pl.ds(0, half), pl.ds(half, half)
+    target = out.at[exchange.chip]
+    direct = [
+        exchange.copy(block, target, across_device, 0, 0),
+        exchange.copy(block, target, along_device, 0, 1),
+    ]
+    for copy in direct:
+        copy.start()
+    local.save(block, target)
+    passed = [
+        exchange.copy(out.at[across, first], out.at[across, first], along_device, 0, 2),
+        exchange.copy(out.at[along, last], out.at[along, last], across_device, 0, 3),
+    ]
+    for copy, onward in zip(direct, passed):
+        copy.wait_recv()
+        onward.start()
+    for copy in passed:
+        copy.wait_recv()
+    for copy in direct + passed:
+        copy.wait_send()
+    local.finish()
+
+
+def chip_gather(block):
+    return pl.pallas_call(
+        chip_gather_kernel,
+        in_specs=[HBM_SPEC],
+        out_specs=HBM_SPEC,
+        out_shape=shape((4,) + block.shape, bf16),
+        scratch_shapes=[
+            pltpu.SemaphoreType.DMA((1,)),
+            pltpu.SemaphoreType.DMA((1, 4)),
+            pltpu.SemaphoreType.DMA((1, 4)),
+        ],
+        compiler_params=params(6),
+        cost_estimate=cost(0, 300 * block.size),
+        name="chip_gather",
+    )(block)
+
+
+def load_pack(pack, held, local):
+    depth = held.shape[0] // row_chunks
     return [
-        pltpu.make_async_copy(
-            pack.at[pl.ds(c * depth, depth)], held.at[pl.ds(c * depth, depth)], sems.at[c]
-        )
-        for c in range(4)
+        local.load(pack.at[pl.ds(c * depth, depth)], held.at[pl.ds(c * depth, depth)])
+        for c in range(row_chunks)
     ]
+
+
+class Local:
+    def __init__(self, sems):
+        self.sems, self.used, self.saves = sems, 0, []
+
+    def copy(self, source, target):
+        self.used += 1
+        return pltpu.make_async_copy(source, target, self.sems.at[self.used - 1])
+
+    def load(self, source, target):
+        copy = self.copy(source, target)
+        copy.start()
+        return copy
+
+    def load_either(self, at_first, first, second, target):
+        one = self.copy(first, target)
+        other = pltpu.make_async_copy(second, target, self.sems.at[self.used - 1])
+
+        @pl.when(at_first)
+        def _():
+            one.start()
+
+        @pl.when(jnp.logical_not(at_first))
+        def _():
+            other.start()
+
+        return one
+
+    def save(self, source, target):
+        self.saves.append(self.load(source, target))
+
+    def finish(self):
+        for copy in self.saves:
+            copy.wait()
 
 
 def row_mean(values):
@@ -167,16 +254,30 @@
     return exponent / jnp.sum(exponent, axis=-1, keepdims=True)
 
 
+def turn_chunk(rows, target, c):
+    cols = rows.shape[2]
+    target[pl.ds(c * cols, cols), :] = rows[c].T
+
+
 def attn_forward_kernel(
-    width, hidden, pack, model_gains, gains, cosine, signed_sine, masks,
-    normed, projected, values, attended, mixed, normed_ffn_rows,
-    held, keep, send_core, recv_core, send_half, recv_half, load_sems, send_sems, recv_sems,
+    width, carry, *refs
 ):
-    exchange = Exchange(send_sems, recv_sems)
-    exchange.greet(False)
-    loads = load_pack(pack, held, load_sems)
-    for load in loads:
-        load.start()
+    if carry:
+        carried, refs = refs[0], refs[1:]
+    (
+        hidden, pack, model_gains, gains, tables_in, masks_in,
+        turned_out, projected_out, values_out, attended_out, mixed_out, normed_ffn_rows,
+    ), refs = refs[:12], refs[12:]
+    if carry:
+        arrived, refs = refs[0], refs[1:]
+    (
+        tables, masks, normed, turned, projected, values, attended, mixed,
+        held, keep, send_core, recv_core, send_half, recv_half, local_sems, send_sems, recv_sems,
+    ) = refs
+    exchange, local = Exchange(send_sems, recv_sems), Local(local_sems)
+    exchange.greet(carry)
+    loads = load_pack(pack, held, local)
+    extra = [local.load(tables_in, tables), local.load(masks_in, masks)]
     chunks, own, cols = hidden.shape
     length = 2 * own
     q_width = attended.shape[1]
@@ -193,10 +294,18 @@
         accumulate(projected, normed[c], held, c * cols, 0, 2 * q_width, c == 0)
 
     copies = gather_then(exchange, normed, project)
-    cos, sin = cosine[...], signed_sine[...]
+    hops = []
+    if carry:
+        hops = [exchange.copy(carried, arrived, exchange.section, 4, 0)]
+        hops[0].start()
+    local.save(projected, projected_out)
+    for load in extra:
+        load.wait()
+    cos, sin = tables[0], tables[1]
     gain_q, gain_k = gains[0:1, :], gains[1:2, :]
     scale = width ** (-0.5)
     values[...] = projected[:, q_width + kv_width :].astype(bf16)
+    local.save(values, values_out)
     for seq in range(2):
         at = slice(seq * length, (seq + 1) * length)
         allowed = masks[seq] > 0.5
@@ -209,36 +318,46 @@
                 _, query_rot = rotated(projected[at, head], gain_q, cos, sin)
                 weights = softmax_rows(query_rot, key_rot, allowed, scale)
                 attended[at, head] = dot_nn(weights.astype(bf16), value).astype(bf16)
+    local.save(attended, attended_out)
 
     def make(c):
         return dot_nt(attended[...], held[c * cols : (c + 1) * cols, 2 * q_width :])
 
+    def idle(c):
+        turn_chunk(normed, turned, c)
+
     def finish(c, summed):
         mixed[c] = hidden[c].astype(f32) + summed
 
-    copies += scatter_from(exchange, make, finish, keep, send_core, recv_core, send_half, recv_half)
+    copies += scatter_from(
+        exchange, make, idle, finish, keep, send_core, recv_core, send_half, recv_half
+    )
+    local.save(turned, turned_out)
+    local.save(mixed, mixed_out)
     rows = mixed[...]
     inverse = lax.rsqrt(row_mean(rows * rows) + norm_eps)
     for c in range(chunks):
         normed_ffn_rows[c] = (rows[c] * inverse[0] * model_gains[1, c][None, :]).astype(bf16)
+    for copy in hops:
+        copy.wait()
     for copy in copies:
         copy.wait_send()
+    local.finish()
 
 
 def ffn_forward_kernel(
-    hop, rows, mixed, pack, normed, gate_up, activated, result, *rest
+    hop, rows, mixed_in, pack, turned_out, gate_up_out, activated_out, result, *rest
 ):
     if hop:
         arrived, rest = rest[0], rest[1:]
     (
-        held, total, keep, send_core, recv_core, send_half, recv_half,
-        load_sems, save_sem, send_sems, recv_sems,
+        normed, turned, mixed, activated, total,
+        held, keep, send_core, recv_core, send_half, recv_half, local_sems, send_sems, recv_sems,
     ) = rest
-    exchange = Exchange(send_sems, recv_sems)
+    exchange, local = Exchange(send_sems, recv_sems), Local(local_sems)
     exchange.greet(hop)
-    loads = load_pack(pack, held, load_sems)
-    for load in loads:
-        load.start()
+    loads = load_pack(pack, held, local)
+    mixed_load = local.load(mixed_in, mixed)
     chunks, own, cols = rows.shape
     units = activated.shape[1]
     for c in range(chunks):
@@ -249,8 +368,7 @@
         accumulate(total, normed[c], held, c * cols, 0, 2 * units, c == 0)
 
     copies = gather_then(exchange, normed, project)
-    save = pltpu.make_async_copy(total, gate_up, save_sem.at[0])
-    save.start()
+    local.save(total, gate_up_out)
     blk = 256
 
     def activate(index, _):
@@ -261,10 +379,15 @@
         return 0
 
     lax.fori_loop(0, units // blk, activate, 0)
+    local.save(activated, activated_out)
+    mixed_load.wait()
     hops = []
 
     def make(c):
         return dot_nt(activated[...], held[c * cols : (c + 1) * cols, 2 * units :])
+
+    def idle(c):
+        turn_chunk(normed, turned, c)
 
     def finish(c, summed):
         result[c] = (mixed[c] + summed).astype(bf16)
@@ -272,26 +395,36 @@
             hops.append(exchange.copy(result.at[c], arrived.at[c], exchange.section, 4, c))
             hops[-1].start()
 
-    copies += scatter_from(exchange, make, finish, keep, send_core, recv_core, send_half, recv_half)
-    save.wait()
+    copies += scatter_from(
+        exchange, make, idle, finish, keep, send_core, recv_core, send_half, recv_half
+    )
+    local.save(turned, turned_out)
     for copy in hops:
         copy.wait()
     for copy in copies:
         copy.wait_send()
-
-
-def ffn_backward_kernel(
-    rows, mixed, gate_up, pack, model_gains, grad_down, grads, grad_mixed, grad_proj_rows, gain_grad,
-    held, pre, total, keep, send_core, recv_core, send_half, recv_half,
-    load_sems, save_sem, send_sems, recv_sems,
-):
-    exchange = Exchange(send_sems, recv_sems)
-    exchange.greet(False)
-    loads = load_pack(pack, held, load_sems)
-    for load in loads:
-        load.start()
-    fetch = pltpu.make_async_copy(gate_up, pre, save_sem.at[0])
-    fetch.start()
+    local.finish()
+
+
+def ffn_backward_kernel(spread, carry, *refs):
+    if carry:
+        carried, refs = refs[0], refs[1:]
+    (
+        rows, mixed_a, mixed_b, gate_up_a, gate_up_b, pack, model_gains,
+        moved_out, grads_out, grad_mixed, grad_proj_rows, gain_grad,
+    ), refs = refs[:12], refs[12:]
+    if carry:
+        arrived, refs = refs[0], refs[1:]
+    (
+        grad_down, moved, mixed, grads, pre, total,
+        held, keep, send_core, recv_core, send_half, recv_half, local_sems, send_sems, recv_sems,
+    ) = refs
+    exchange, local = Exchange(send_sems, recv_sems), Local(local_sems)
+    exchange.greet(carry, spread)
+    at_first = lax.axis_index("section") == 0
+    loads = load_pack(pack, held, local)
+    pre_load = local.load_either(at_first, gate_up_a, gate_up_b, pre)
+    mixed_load = local.load_either(at_first, mixed_a, mixed_b, mixed)
     chunks, own, cols = rows.shape
     units = grads.shape[1] // 2
     for c in range(chunks):
@@ -302,7 +435,31 @@
         accumulate(total, grad_down[c], held, c * cols, 2 * units, units, c == 0)
 
     copies = gather_then(exchange, grad_down, project)
-    fetch.wait()
+    hops = []
+    if carry:
+        hops = [exchange.copy(carried, arrived, exchange.section, 4, 0)]
+        hops[0].start()
+    side = 2 * own
+    arrivals, onward = [], []
+    if spread:
+        for index, (number, device) in enumerate(exchange.chips):
+            arrivals.append(
+                exchange.copy(
+                    grad_down.at[number, pl.ds(0, side)],
+                    moved.at[exchange.chip, pl.ds(0, side)],
+                    device, 5, index,
+                )
+            )
+            arrivals[-1].start()
+            onward.append(
+                exchange.copy(
+                    moved.at[number, pl.ds(0, side)],
+                    moved.at[number, pl.ds(side, side)],
+                    exchange.core, 6, index,
+                )
+            )
+        moved[exchange.chip] = grad_down[exchange.chip]
+    pre_load.wait()
     blk = 256
 
     def activate(index, _):
@@ -316,19 +473,37 @@
         return 0
 
     lax.fori_loop(0, units // blk, activate, 0)
+    local.save(grads, grads_out)
 
     def make(c):
         return dot_nt(grads[...], held[c * cols : (c + 1) * cols, : 2 * units])
 
+    def idle(c):
+        if not spread:
+            turn_chunk(grad_down, moved, c)
+        elif c > 0:
+            arrivals[c - 1].wait_recv()
+            onward[c - 1].start()
+
     def finish(c, summed):
         grad_mixed[c] = summed
 
-    copies += scatter_from(exchange, make, finish, keep, send_core, recv_core, send_half, recv_half)
+    copies += scatter_from(
+        exchange, make, idle, finish, keep, send_core, recv_core, send_half, recv_half
+    )
+    for copy in onward:
+        copy.wait_recv()
+    copies += arrivals + onward
+    local.save(moved, moved_out)
+    mixed_load.wait()
     norm_step(mixed[...], grad_mixed[...], model_gains, 1, rows, grad_mixed, gain_grad)
     for c in range(chunks):
         grad_proj_rows[c] = grad_mixed[c].astype(bf16)
+    for copy in hops:
+        copy.wait()
     for copy in copies:
         copy.wait_send()
+    local.finish()
 
 
 def norm_step(values, grad_out, model_gains, which, base, out, gain_grad):
@@ -342,20 +517,24 @@
 
 
 def attn_backward_kernel(
-    width, hop, rows, grad_mixed, hidden, projected, values, pack, model_gains, gains, cosine,
-    signed_sine, masks, grad_proj, grads, grad_hidden, gain_grad, head_gain_grads, *rest
+    width, hop, rows, grad_mixed, hidden_a, hidden_b, projected_a, projected_b, values_a, values_b,
+    pack, model_gains, gains, tables_in, masks_in,
+    turned_out, grads_out, grad_hidden, gain_grad, head_gain_grads, *rest
 ):
     if hop:
         arrived, rest = rest[0], rest[1:]
     (
-        held, total, summed_rows, keep, send_core, recv_core, send_half, recv_half,
-        load_sems, send_sems, recv_sems,
+        tables, masks, grad_proj, turned, grads, hidden, projected, values, total, summed_rows,
+        held, keep, send_core, recv_core, send_half, recv_half, local_sems, send_sems, recv_sems,
     ) = rest
-    exchange = Exchange(send_sems, recv_sems)
+    exchange, local = Exchange(send_sems, recv_sems), Local(local_sems)
     exchange.greet(hop)
-    loads = load_pack(pack, held, load_sems)
-    for load in loads:
-        load.start()
+    at_first = lax.axis_index("section") == 0
+    loads = load_pack(pack, held, local)
+    extra = [local.load(tables_in, tables), local.load(masks_in, masks)]
+    projected_load = local.load_either(at_first, projected_a, projected_b, projected)
+    values_load = local.load_either(at_first, values_a, values_b, values)
+    hidden_load = local.load_either(at_first, hidden_a, hidden_b, hidden)
     chunks, own, cols = rows.shape
     length = 2 * own
     q_width = grads.shape[1] // 2
@@ -370,7 +549,11 @@
         accumulate(total, grad_proj[c], held, c * cols, 2 * q_width, q_width, c == 0)
 
     copies = gather_then(exchange, grad_proj, project)
-    cos, sin = cosine[...], signed_sine[...]
+    projected_load.wait()
+    values_load.wait()
+    for load in extra:
+        load.wait()
+    cos, sin = tables[0], tables[1]
     gain_q, gain_k = gains[0:1, :], gains[1:2, :]
     scale = width ** (-0.5)
     gain_q_sum = jnp.zeros((1, width), f32)
@@ -406,6 +589,7 @@
             grads[at, first : first + width] = norm_back(grad_key, raw_k, inverse_k, gain_k).astype(bf16)
             first += kv_width
             grads[at, first : first + width] = grad_value.astype(bf16)
+    local.save(grads, grads_out)
     head_gain_grads[...] = jnp.concatenate(
         [gain_q_sum, gain_k_sum, jnp.zeros((6, width), f32)], axis=0
     )
@@ -413,10 +597,17 @@
     def make(c):
         return dot_nt(grads[...], held[c * cols : (c + 1) * cols, : 2 * q_width])
 
+    def idle(c):
+        turn_chunk(grad_proj, turned, c)
+
     def finish(c, summed):
         summed_rows[c] = summed
 
-    copies += scatter_from(exchange, make, finish, keep, send_core, recv_core, send_half, recv_half)
+    copies += scatter_from(
+        exchange, make, idle, finish, keep, send_core, recv_core, send_half, recv_half
+    )
+    local.save(turned, turned_out)
+    hidden_load.wait()
     norm_step(
         hidden[...].astype(f32), summed_rows[...], model_gains, 0, grad_mixed, grad_hidden, gain_grad
     )
@@ -431,22 +622,56 @@
             copy.wait()
     for copy in copies:
         copy.wait_send()
-
-
-def weight_grad_kernel(split, first_a, first_b, second_a, second_b, main_a, main_b, last_a, last_b, out):
-    step = pl.program_id(0)
-
-    @pl.when(step < split)
-    def _():
-        out[...] = (dot_nn(first_a[...], main_a[...]) + dot_nn(first_b[...], main_b[...])).astype(bf16)
-
-    @pl.when(step >= split)
-    def _():
-        out[...] = (dot_nn(second_a[...], last_a[...]) + dot_nn(second_b[...], last_b[...])).astype(bf16)
+    local.finish()
+
+
+def weight_grad_kernel(blk, sides, *refs):
+    lefts, rights, refs = refs[: 3 * sides], refs[3 * sides : 6 * sides], refs[6 * sides :]
+    out, left, right = refs[0], refs[1 : 1 + sides], refs[1 + sides : 1 + 2 * sides]
+    held, local_sems = refs[1 + 2 * sides :]
+    local = Local(local_sems)
+    at_first = lax.axis_index("section") == 0
+    tokens = rights[0].shape[0]
+    loads = []
+    for side in range(sides):
+        left_steps = pairs_of(lefts[3 * side : 3 * side + 3], side == 1)
+        right_steps = pairs_of(rights[3 * side : 3 * side + 3], side == 0)
+        for micro in range(2):
+            at = pl.ds(micro * tokens, tokens)
+            loads.append(
+                [
+                    local.load_either(
+                        at_first, left_steps[0][micro], left_steps[1][micro], left[side].at[:, at]
+                    ),
+                    local.load_either(
+                        at_first, right_steps[0][micro], right_steps[1][micro], right[side].at[at]
+                    ),
+                ]
+            )
+    saves, number = [None, None], 0
+    for side in range(sides):
+        for micro in range(2):
+            for load in loads[2 * side + micro]:
+                load.wait()
+        for block in range(right[side].shape[1] // blk):
+            slot = number % 2
+            if saves[slot] is not None:
+                saves[slot].wait()
+            at = pl.ds(block * blk, blk)
+            held[slot] = dot_nn(left[side][...], right[side][:, at]).astype(bf16)
+            saves[slot] = local.load(held.at[slot], out.at[:, pl.ds(number * blk, blk)])
+            number += 1
+    for save in saves:
+        save.wait()
+
+
+def pairs_of(steps, backward):
+    early, late = (steps[0], steps[1]), (steps[1], steps[2])
+    return (late, early) if backward else (early, late)
 
 
 VMEM_SPEC = pl.BlockSpec(memory_space=pltpu.VMEM)
-ANY_SPEC = pl.BlockSpec(memory_space=pl.ANY)
+HBM_SPEC = pl.BlockSpec(memory_space=pltpu.HBM)
 
 
 def shape(dims, kind):
@@ -460,19 +685,17 @@
         pltpu.VMEM((chunks, 2 * own, cols), bf16),
         pltpu.VMEM((chunks, own, cols), bf16),
         pltpu.VMEM((chunks, own, cols), bf16),
-        pltpu.SemaphoreType.DMA((4,)),
+        pltpu.SemaphoreType.DMA((12,)),
+        pltpu.SemaphoreType.DMA((7, chunks)),
+        pltpu.SemaphoreType.DMA((7, chunks)),
     ]
 
 
-def exchange_sems(chunks):
-    return [pltpu.SemaphoreType.DMA((5, chunks)), pltpu.SemaphoreType.DMA((5, chunks))]
-
-
-def params(mib, number=None):
+def params(number=None):
     if number is None:
-        return pltpu.CompilerParams(vmem_limit_bytes=mib * MIB)
+        return pltpu.CompilerParams(vmem_limit_bytes=62 * MIB)
     return pltpu.CompilerParams(
-        vmem_limit_bytes=mib * MIB, collective_id=number, has_side_effects=True
+        vmem_limit_bytes=62 * MIB, collective_id=number, has_side_effects=True
     )
 
 
@@ -480,80 +703,103 @@
     return pl.CostEstimate(flops=int(flops), bytes_accessed=int(size), transcendentals=0)
 
 
-def attn_forward(hidden, pack, model_gains, gains, tables, masks):
+def attn_forward(hidden, pack, model_gains, gains, tables, masks, carried):
     chunks, own, cols = hidden.shape
     tokens, q_width, width = 4 * own, pack.shape[1] // 3, gains.shape[1]
+    depth = chunks * cols
+    carry = carried is not None
+    rows = shape((chunks, own, cols), bf16)
     return pl.pallas_call(
-        functools.partial(attn_forward_kernel, width),
-        in_specs=[VMEM_SPEC, ANY_SPEC] + [VMEM_SPEC] * 5,
-        out_specs=[VMEM_SPEC] * 6,
+        functools.partial(attn_forward_kernel, width, carry),
+        in_specs=[HBM_SPEC] * carry + [VMEM_SPEC, HBM_SPEC] + [VMEM_SPEC] * 2 + [HBM_SPEC] * 2,
+        out_specs=[HBM_SPEC] * 5 + [VMEM_SPEC] + [HBM_SPEC] * carry,
         out_shape=[
-            shape((chunks, tokens, cols), bf16),
+            shape((depth, tokens), bf16),
             shape((tokens, 2 * q_width), f32),
             shape((tokens, q_width // 2), bf16),
             shape((tokens, q_width), bf16),
             shape((chunks, own, cols), f32),
-            shape((chunks, own, cols), bf16),
-        ],
-        scratch_shapes=[pltpu.VMEM(pack.shape, bf16)]
-        + exchange_scratch(chunks, own, cols)
-        + exchange_sems(chunks),
-        compiler_params=params(40, 0),
+            rows,
+        ]
+        + [rows] * carry,
+        scratch_shapes=[
+            pltpu.VMEM(tables.shape, f32),
+            pltpu.VMEM(masks.shape, f32),
+            pltpu.VMEM((chunks, tokens, cols), bf16),
+            pltpu.VMEM((depth, tokens), bf16),
+            pltpu.VMEM((tokens, 2 * q_width), f32),
+            pltpu.VMEM((tokens, q_width // 2), bf16),
+            pltpu.VMEM((tokens, q_width), bf16),
+            pltpu.VMEM((chunks, own, cols), f32),
+            pltpu.VMEM(pack.shape, bf16),
+        ]
+        + exchange_scratch(chunks, own, cols),
+        compiler_params=params(8 if carry else 0),
         cost_estimate=cost(2 * tokens * pack.size, pack.size * 2),
         name="attn_forward",
-    )(hidden, pack, model_gains, gains, *tables, masks)
+    )(*([carried] if carry else []), hidden, pack, model_gains, gains, tables, masks)
 
 
 def ffn_forward(rows, mixed, pack, hop):
     chunks, own, cols = rows.shape
     tokens, units = 4 * own, pack.shape[1] // 3
-    scratch = exchange_scratch(chunks, own, cols)
+    depth = chunks * cols
     return pl.pallas_call(
         functools.partial(ffn_forward_kernel, hop),
-        in_specs=[VMEM_SPEC, VMEM_SPEC, ANY_SPEC],
-        out_specs=[VMEM_SPEC, ANY_SPEC] + [VMEM_SPEC] * (3 if hop else 2),
+        in_specs=[VMEM_SPEC, HBM_SPEC, HBM_SPEC],
+        out_specs=[HBM_SPEC] * 3 + [VMEM_SPEC] * (2 if hop else 1),
         out_shape=[
-            shape((chunks, tokens, cols), bf16),
+            shape((depth, tokens), bf16),
             shape((tokens, 2 * units), f32),
             shape((tokens, units), bf16),
         ]
         + [shape((chunks, own, cols), bf16)] * (2 if hop else 1),
-        scratch_shapes=[pltpu.VMEM(pack.shape, bf16), pltpu.VMEM((tokens, 2 * units), f32)]
-        + scratch
-        + [pltpu.SemaphoreType.DMA((1,))]
-        + exchange_sems(chunks),
-        compiler_params=params(52, 1 if hop else 2),
+        scratch_shapes=[
+            pltpu.VMEM((chunks, tokens, cols), bf16),
+            pltpu.VMEM((depth, tokens), bf16),
+            pltpu.VMEM((chunks, own, cols), f32),
+            pltpu.VMEM((tokens, units), bf16),
+            pltpu.VMEM((tokens, 2 * units), f32),
+            pltpu.VMEM(pack.shape, bf16),
+        ]
+        + exchange_scratch(chunks, own, cols),
+        compiler_params=params(1 if hop else 2),
         cost_estimate=cost(2 * tokens * pack.size, pack.size * 2),
         name="ffn_forward",
     )(rows, mixed, pack)
 
 
-def ffn_backward(rows, mixed, gate_up, pack, model_gains):
+def ffn_backward(rows, mixed, gate_up, pack, model_gains, spread, carried):
     chunks, own, cols = rows.shape
     tokens, units = 4 * own, pack.shape[1] // 3
+    moved = (chunks, tokens, cols) if spread else (chunks * cols, tokens)
+    carry = carried is not None
     return pl.pallas_call(
-        ffn_backward_kernel,
-        in_specs=[VMEM_SPEC, VMEM_SPEC, ANY_SPEC, ANY_SPEC, VMEM_SPEC],
-        out_specs=[VMEM_SPEC] * 5,
+        functools.partial(ffn_backward_kernel, spread, carry),
+        in_specs=[HBM_SPEC] * carry + [VMEM_SPEC] + [HBM_SPEC] * 5 + [VMEM_SPEC],
+        out_specs=[HBM_SPEC] * 2 + [VMEM_SPEC] * 3 + [HBM_SPEC] * carry,
         out_shape=[
-            shape((chunks, tokens, cols), bf16),
+            shape(moved, bf16),
             shape((tokens, 2 * units), bf16),
             shape((chunks, own, cols), f32),
             shape((chunks, own, cols), bf16),
             shape((chunks, cols), f32),
-        ],
+        ]
+        + [shape((chunks, own, cols), bf16)] * carry,
         scratch_shapes=[
-            pltpu.VMEM(pack.shape, bf16),
+            pltpu.VMEM((chunks, tokens, cols), bf16),
+            pltpu.VMEM(moved, bf16),
+            pltpu.VMEM((chunks, own, cols), f32),
+            pltpu.VMEM((tokens, 2 * units), bf16),
             pltpu.VMEM((tokens, 2 * units), f32),
             pltpu.VMEM((tokens, units), f32),
+            pltpu.VMEM(pack.shape, bf16),
         ]
-        + exchange_scratch(chunks, own, cols)
-        + [pltpu.SemaphoreType.DMA((1,))]
-        + exchange_sems(chunks),
-        compiler_params=params(56, 3),
+        + exchange_scratch(chunks, own, cols),
+        compiler_params=params(9 if carry else 3),
         cost_estimate=cost(2 * tokens * pack.size, pack.size * 2),
         name="ffn_backward",
-    )(rows, mixed, gate_up, pack, model_gains)
+    )(*([carried] if carry else []), rows, *mixed, *gate_up, pack, model_gains)
 
 
 def attn_backward(
@@ -561,12 +807,13 @@
 ):
     chunks, own, cols = rows.shape
     tokens, q_width, width = 4 * own, pack.shape[1] // 3, gains.shape[1]
+    depth = chunks * cols
     return pl.pallas_call(
         functools.partial(attn_backward_kernel, width, hop),
-        in_specs=[VMEM_SPEC] * 5 + [ANY_SPEC] + [VMEM_SPEC] * 5,
-        out_specs=[VMEM_SPEC] * (6 if hop else 5),
+        in_specs=[VMEM_SPEC] * 2 + [HBM_SPEC] * 7 + [VMEM_SPEC] * 2 + [HBM_SPEC] * 2,
+        out_specs=[HBM_SPEC] * 2 + [VMEM_SPEC] * (4 if hop else 3),
         out_shape=[
-            shape((chunks, tokens, cols), bf16),
+            shape((depth, tokens), bf16),
             shape((tokens, 2 * q_width), bf16),
             shape((chunks, own, cols), bf16),
             shape((chunks, cols), f32),
@@ -574,36 +821,46 @@
         ]
         + [shape((chunks, own, cols), bf16)] * (1 if hop else 0),
         scratch_shapes=[
-            pltpu.VMEM(pack.shape, bf16),
+            pltpu.VMEM(tables.shape, f32),
+            pltpu.VMEM(masks.shape, f32),
+            pltpu.VMEM((chunks, tokens, cols), bf16),
+            pltpu.VMEM((depth, tokens), bf16),
+            pltpu.VMEM((tokens, 2 * q_width), bf16),
+            pltpu.VMEM((chunks, own, cols), bf16),
+            pltpu.VMEM((tokens, 2 * q_width), f32),
+            pltpu.VMEM((tokens, q_width // 2), bf16),
             pltpu.VMEM((tokens, q_width), f32),
             pltpu.VMEM((chunks, own, cols), f32),
+            pltpu.VMEM(pack.shape, bf16),
         ]
-        + exchange_scratch(chunks, own, cols)
-        + exchange_sems(chunks),
-        compiler_params=params(40, 4 if hop else 5),
+        + exchange_scratch(chunks, own, cols),
+        compiler_params=params(4 if hop else 5),
         cost_estimate=cost(2 * tokens * pack.size, pack.size * 2),
         name="attn_backward",
-    )(rows, grad_mixed, hidden, projected, values, pack, model_gains, gains, *tables, masks)
-
-
-def weight_grad(first, second, main, last):
-    depth, tokens = first[0].shape
+    )(
+        rows, grad_mixed, *hidden, *projected, *values, pack, model_gains, gains, tables, masks
+    )
+
+
+def weight_grad(lefts, rights):
+    depth, tokens = lefts[0][0].shape
     blk = 512
-    split, rest = main[0].shape[1] // blk, last[0].shape[1] // blk
-    turned = pl.BlockSpec((depth, tokens), lambda step: (0, 0))
-    main_spec = pl.BlockSpec((tokens, blk), lambda step: (0, jnp.minimum(step, split - 1)))
-    last_spec = pl.BlockSpec((tokens, blk), lambda step: (0, jnp.maximum(step - split, 0)))
-    width = (split + rest) * blk
+    widths = [right[0].shape[1] for right in rights]
     return pl.pallas_call(
-        functools.partial(weight_grad_kernel, split),
-        grid=(split + rest,),
-        in_specs=[turned] * 4 + [main_spec] * 2 + [last_spec] * 2,
-        out_specs=pl.BlockSpec((depth, blk), lambda step: (0, step)),
-        out_shape=shape((depth, width), bf16),
-        compiler_params=params(40),
-        cost_estimate=cost(4 * depth * tokens * width, 2 * depth * width),
+        functools.partial(weight_grad_kernel, blk, len(lefts)),
+        in_specs=[HBM_SPEC] * (6 * len(lefts)),
+        out_specs=HBM_SPEC,
+        out_shape=shape((depth, sum(widths)), bf16),
+        scratch_shapes=[pltpu.VMEM((depth, 2 * tokens), bf16) for _ in lefts]
+        + [pltpu.VMEM((2 * tokens, width), bf16) for width in widths]
+        + [
+            pltpu.VMEM((2, depth, blk), bf16),
+            pltpu.SemaphoreType.DMA((4 * len(lefts) + sum(widths) // blk,)),
+        ],
+        compiler_params=params(),
+        cost_estimate=cost(4 * depth * tokens * sum(widths), 2 * depth * sum(widths)),
         name="weight_grad",
-    )(*first, *second, *main, *last)
+    )(*sum(lefts, []), *sum(rights, []))
 
 
 def rope_tables(position, head_width):
@@ -663,17 +920,18 @@
         left, right = weight[:side].T, weight[side:].T
         return jnp.where(first_core, left, right), jnp.where(first_core, right, left)
 
-    def gathered(pairs):
+    def chip_block(pairs):
         mine = jnp.concatenate([pair[0] for pair in pairs], axis=1)
         theirs = to_core(jnp.concatenate([pair[1] for pair in pairs], axis=1))
-        chip_block = jnp.concatenate(
+        return jnp.concatenate(
             [jnp.where(first_core, mine, theirs), jnp.where(first_core, theirs, mine)], axis=0
         )
-        return lax.all_gather(
-            chip_block, "dp", axis=0, tiled=True, axis_index_groups=chip_groups
-        )
-
-    attn_pack = gathered(
+
+    def gathered(block):
+        return lax.all_gather(block, "dp", axis=0, tiled=True, axis_index_groups=chip_groups)
+
+    square = n_chip == row_chunks
+    attn_block = chip_block(
         [
             split_columns(q_weight[0]),
             split_columns(k_weight[0]),
@@ -681,9 +939,15 @@
             split_rows(o_weight[0]),
         ]
     )
-    ffn_pack = gathered(
+    ffn_block = chip_block(
         [split_columns(gate_weight[0]), split_columns(up_weight[0]), split_rows(down_weight[0])]
     )
+    if square:
+        attn_block, ffn_block = lax.optimization_barrier((attn_block, ffn_block))
+        attn_pack = chip_gather(attn_block).reshape(depth, -1)
+    else:
+        attn_pack = gathered(attn_block)
+    ffn_pack = gathered(ffn_block)
 
     cols = depth // row_chunks
     model_gains = jnp.concatenate([attn_norm, ffn_norm], axis=0).reshape(2, row_chunks, cols)
@@ -694,9 +958,6 @@
 
     def joined(rows):
         return rows.transpose(1, 0, 2).reshape(rows.shape[1], depth)
-
-    def turned(rows):
-        return rows.transpose(0, 2, 1).reshape(depth, rows.shape[1])
 
     inputs = [chunked(block_input[micro]) for micro in range(2)]
     cotangents = [chunked(out_cotangent[micro]) for micro in range(2)]
@@ -708,7 +969,7 @@
         )
 
     position = arranged(jnp.arange(length, dtype=jnp.int32))
-    tables = rope_tables(position, head_width)
+    tables = jnp.stack(rope_tables(position, head_width))
     ids = arranged(jnp.stack([segment_ids, to_core(segment_ids)], axis=1))
     causal = position[:, None] >= position[None, :]
     masks = (causal & (ids[..., :, None] == ids[..., None, :])).astype(f32)
@@ -720,55 +981,72 @@
 
     zero_rows = jnp.zeros_like(inputs[0])
     forward_masks = [masks[0], pick(masks[1], masks[0]), masks[1]]
-    results, backs, saves, arrived = [], [], [], zero_rows
-    for step in range(3):
+    backward_masks = [masks[0], pick(masks[0], masks[1]), masks[1]]
+    results, backs, saves = [], [], []
+    grads, ffn_saves, attn_saves, gains = [], [], [], []
+
+    def forward_step(step, arrived, hop, carried=None):
         hidden = inputs[step] if step < 2 else zero_rows
         if step > 0:
             hidden = pick(hidden, arrived)
-        normed, projected, values, attended, mixed, rows = attn_forward(
-            hidden, attn_pack, model_gains, head_gains, tables, forward_masks[step]
+        turned_in, projected, values, attended, mixed, rows, *carried = attn_forward(
+            hidden, attn_pack, model_gains, head_gains, tables, forward_masks[step], carried
         )
-        normed_ffn, gate_up, activated, result, *rest = ffn_forward(rows, mixed, ffn_pack, step < 2)
-        arrived = rest[0] if rest else None
+        turned_mid, gate_up, activated, result, *rest = ffn_forward(rows, mixed, ffn_pack, hop)
         results.append(result)
         backs.append((hidden, projected, values, mixed, gate_up))
-        saves.append((normed, attended, normed_ffn, activated))
-    def forward_pair(item):
-        return [pick(saves[micro][item], saves[micro + 1][item]) for micro in range(2)]
-
-    def backward_pair(table, item):
-        return [pick(table[micro + 1][item], table[micro][item]) for micro in range(2)]
-
-    def turned_pair(pair):
-        return [turned(rows) for rows in pair]
-
-    backward_masks = [masks[0], pick(masks[0], masks[1]), masks[1]]
-    grads, ffn_saves, attn_saves, gain_total, arrived = [], [], [], None, zero_rows
-    for step in range(3):
+        saves.append((turned_in, attended, turned_mid, activated))
+        return (rest + carried + [None])[0]
+
+    def back_ffn(step, arrived, carried=None):
         rows = pick(arrived, cotangents[step] if step < 2 else zero_rows)
-        back = pick(backs[0], backs[2]) if step == 1 else backs[1]
-        hidden, projected, values, mixed, gate_up = back
-        grad_down, ffn_grads, grad_mixed, proj_rows, ffn_gain_grad = ffn_backward(
-            rows, mixed, gate_up, ffn_pack, model_gains
+        *_, mixed, gate_up = zip(backs[0], backs[2]) if step == 1 else zip(backs[1], backs[1])
+        turned_rows, ffn_grads, grad_mixed, proj_rows, gain_grad, *carried = ffn_backward(
+            rows, mixed, gate_up, ffn_pack, model_gains, square, carried
         )
-        ffn_saves.append((grad_down, ffn_grads))
-        if step == 2:
-            ffn_partial = weight_grad(
-                turned_pair(forward_pair(2)),
-                turned_pair(backward_pair(ffn_saves, 0)),
-                backward_pair(ffn_saves, 1),
-                forward_pair(3),
-            )
-            proj_rows, ffn_partial = lax.optimization_barrier((proj_rows, ffn_partial))
-        grad_proj, attn_grads, grad_hidden, attn_gain_grad, head_gain_grads, *rest = attn_backward(
+        ffn_saves.append((turned_rows, ffn_grads))
+        return proj_rows, grad_mixed, gain_grad, *carried
+
+    def back_attn(step, proj_rows, grad_mixed, ffn_gain_grad, hop):
+        hidden, projected, values, *_ = (
+            zip(backs[0], backs[2]) if step == 1 else zip(backs[1], backs[1])
+        )
+        turned_rows, attn_grads, grad_hidden, attn_gain_grad, head_gain_grads, *rest = attn_backward(
             proj_rows, grad_mixed, hidden, projected, values, attn_pack, model_gains, head_gains,
-            tables, backward_masks[step], step < 2,
+            tables, backward_masks[step], hop,
         )
-        arrived = rest[0] if rest else None
+        attn_saves.append((turned_rows, attn_grads))
         grads.append(grad_hidden)
-        attn_saves.append((grad_proj, attn_grads))
-        gains = (attn_gain_grad, ffn_gain_grad, head_gain_grads)
-        gain_total = gains if gain_total is None else jax.tree.map(jnp.add, gain_total, gains)
+        gains.append((attn_gain_grad, ffn_gain_grad, head_gain_grads))
+        return rest[0] if hop else None
+
+    def column(table, item):
+        return [row[item] for row in table]
+
+    arrived = forward_step(0, zero_rows, True)
+    forward_step(1, arrived, False)
+    *others, arrived = back_ffn(0, zero_rows, results[1])
+    back_attn(0, *others, False)
+    grad_arrived = forward_step(2, arrived, False, grads[0])
+    grad_arrived, results[2] = lax.optimization_barrier((grad_arrived, results[2]))
+    grad_arrived = back_attn(1, *back_ffn(1, grad_arrived), True)
+    if square:
+        active = [pick(saves[micro][3], saves[micro + 1][3]) for micro in range(2)]
+        active_all = gathered(jnp.concatenate(active, axis=0))
+    proj_rows, *others = back_ffn(2, grad_arrived)
+    if square:
+        ffn_partial = weight_grad([column(saves, 2)], [column(ffn_saves, 1)])
+        ffn_partial, active_all = lax.optimization_barrier((ffn_partial, active_all))
+    else:
+        ffn_partial = weight_grad(
+            [column(saves, 2), column(ffn_saves, 0)], [column(ffn_saves, 1), column(saves, 3)]
+        )
+    proj_rows, ffn_partial = lax.optimization_barrier((proj_rows, ffn_partial))
+    back_attn(2, proj_rows, *others, False)
+    attn_partial = weight_grad(
+        [column(saves, 0), column(attn_saves, 0)], [column(attn_saves, 1), column(saves, 1)]
+    )
+    gain_total = functools.reduce(lambda a, b: jax.tree.map(jnp.add, a, b), gains)
 
     section_outputs = jnp.stack(
         [joined(pick(results[micro], results[micro + 1])) for micro in range(2)]
@@ -791,16 +1069,18 @@
             jnp.where(first_core, other, own).astype(f32),
         )
 
-    attn_partial = weight_grad(
-        turned_pair(forward_pair(0)),
-        turned_pair(backward_pair(attn_saves, 0)),
-        backward_pair(attn_saves, 1),
-        forward_pair(1),
-    )
     attn_partial, ffn_rows = lax.optimization_barrier((attn_partial, scattered(ffn_partial)))
     ffn_sides = owned(ffn_rows)
     attn_sides = owned(scattered(attn_partial))
     units = gate_weight.shape[2] // 2
+    if square:
+        spread_rows = jnp.concatenate(
+            [pick(ffn_saves[micro + 1][0], ffn_saves[micro][0]) for micro in range(2)], axis=1
+        ).reshape(-1, cols)
+        down_sides = owned(dot_tn(spread_rows, active_all))
+    else:
+        down_sides = [side[:, 2 * units :] for side in ffn_sides]
+    attn_sides = owned(scattered(attn_partial))
     q_width = q_weight.shape[2] // 2
     kv_width = k_weight.shape[2] // 2
 
@@ -838,7 +1118,7 @@
         packed[None, depth : 2 * depth],
         across(ffn_sides, 0, units),
         across(ffn_sides, units, units),
-        down(ffn_sides, 2 * units),
+        down(down_sides, 0),
     )
 
 

time: 994 us -> 879 us (0.88)
  waiting for transfers between devices: 343 us -> 191 us
  Pallas kernels: 480 us -> 589 us
  local copies, waits for them, and re-layouts: 80.8 us -> 22.3 us
  other arithmetic: 62.8 us -> 43.5 us
    pallas_call x8 -> x9, Pallas kernels: 220 us -> 349 us  [the longest x3 113 us: ffn_backward(): pl.pallas_call(functools.partial(ffn_backward_kernel, spread, carry), in_...]
    all_gather x2, waiting for transfers between devices: 191 us -> 79.4 us  [gathered(): lax.all_gather(block, 'dp', axis=0, tiled=True, axis_index_groups=chip_gr...]
    unnamed x234 -> x84, local copies, waits for them, and re-layouts: 47.1 us -> 7.99 us
    reduce_scatter x2, waiting for transfers between devices: 141 us -> 107 us  [scattered(): lax.psum_scatter(partial, 'dp', scatter_dimension=0, tiled=True, axis_ind...]
    transpose x8 -> x0, local copies, waits for them, and re-layouts: 17.6 us -> none  [turned(): return rows.transpose(0, 2, 1).reshape(depth, rows.shape[1])]
    select_n x13 -> x7, other arithmetic: 19.5 us -> 8.78 us  [pick(): return jax.tree.map(lambda a, b: jnp.where(at_first, a, b), first, second)]
    pallas_call x3, Pallas kernels: 123 us -> 112 us  [ffn_forward(): pl.pallas_call(functools.partial(ffn_forward_kernel, hop), in_specs=[VMEM...]
    transpose x4 -> x1, other arithmetic: 12.4 us -> 1.99 us  [down(): return jnp.concatenate([side[:, first:].T for side in sides], axis=0)[None]]
  transfers between devices with their start and end apart: 13 -> 14, of which waited for: 8 -> 6; matrix products, arithmetic and copies ran while one was open for 6% -> 6% of each run, Pallas kernels for 7% -> 37%
where the time goes in v3:
time: 879 us; the launch traced here: 874 us
  Pallas kernels  589 us (67%)
  waiting for transfers between devices  191 us (22%)
  other arithmetic  43.5 us (5%)
  local copies, waits for them, and re-layouts  22.3 us (3%)
  between operations  14.8 us (2%)
    pallas_call x3, Pallas kernels, attn_backward(): pl.pallas_call(functools.partial(attn_backward_kernel, width, hop), in_sp...  128 us
    pallas_call x3, Pallas kernels, ffn_backward(): pl.pallas_call(functools.partial(ffn_backward_kernel, spread, carry), in_...  113 us
    pallas_call x3, Pallas kernels, ffn_forward(): pl.pallas_call(functools.partial(ffn_forward_kernel, hop), in_specs=[VMEM...  112 us
    reduce_scatter x2, waiting for transfers between devices, scattered(): lax.psum_scatter(partial, 'dp', scatter_dimension=0, tiled=True, axis_ind...  107 us
    pallas_call x3, Pallas kernels, attn_forward(): pl.pallas_call(functools.partial(attn_forward_kernel, width, carry), in_s...  106 us
    pallas_call x1, Pallas kernels, chip_gather(): pl.pallas_call(chip_gather_kernel, in_specs=[HBM_SPEC], out_specs=HBM_SPE...  104 us
    all_gather x2, waiting for transfers between devices, gathered(): lax.all_gather(block, 'dp', axis=0, tiled=True, axis_index_groups=chip_gr...  79.4 us
    pallas_call x2, Pallas kernels, weight_grad(): pl.pallas_call(functools.partial(weight_grad_kernel, blk, len(lefts)), in...  25.5 us
  transfers between devices with their start and end apart: 14, of which 6 were waited for; matrix products, arithmetic and copies ran while one was open for 6% of the time, Pallas kernels for 37%

profile of v3, /device:TPU:0, one launch (start us, length us, event | category | flops | bytes accessed | tf_op | source)
XLA Modules:
  0.0 873.7 jit_solution(756573044866802929)
XLA Ops:
  11.4 1.6 pad_maximum_fusion.3
  15.9 2.8 collective-permute-done
  20.2 2.1 broadcast_select_fusion.1
  22.3 2.4 pad_maximum_fusion
  33.6 104.1 %chip_gather.1 = bf16[4,512,1536]{2,1,0:T(8,128)(2,1)} custom-call(bf16[512,1536]{1,0:T(8,128)(2,1)} %pad_maximum_fusion.5.block), custom_call_target="tpu_custom_call" | custom-call | bytes 235929600 | tf_op jit(solution)/shard_map/chip_gather/pallas_call | solution.py:164
  137.8 32.3 %attn_forward.3 = (bf16[2048,384]{1,0:T(8,128)(2,1)}, f32[384,1024]{1,0:T(8,128)}, bf16[384,256]{1,0:T(8,128)(2,1)}, bf16[384,512]{1,0:T(8,128)(2,1)}, f32[4,96,...) custom-call(bf16[4,96,512]{2,1,0:T(8,128)(2,1)} %bitcast.113, bf16[2048,1536]{1,0:T(8,128)(2,1)} %bitcast.105, ...), custom_call_target="tpu_custom_call" | custom-call | flops 2415919104 | bytes 6291456 | tf_op jit(solution)/shard_map/attn_forward/pallas_call | solution.py:712
  170.1 79.3 %all-gather.3.cloned.1.call-done.pack.refs_6_.refs_5_ = bf16[2048,4608]{1,0:T(8,128)(2,1)} async-done(((bf16[512,4608]{1,0:T(8,128)(2,1)}), bf16[2048,4608]{1,0:T(8,128)(2,1)}) %all-gather.3.cloned.1.call-update) | async-done | bytes 18874384 | tf_op jit(solution)/shard_map/all_gather | solution.py:931
  249.4 46.8 %ffn_forward.3 = (bf16[2048,384]{1,0:T(8,128)(2,1)}, f32[384,3072]{1,0:T(8,128)}, bf16[384,1536]{1,0:T(8,128)(2,1)}, bf16[4,96,512]{2,1,0:T(8,128)(2,1)}, bf16[4,96,512]{2,1,0:T(8,128)(2,1)}) custom-call(bf16[4,96,512]{2,1,0:T(8,128)(2,1)} %get-tuple-element.88.rows, f32[4,96,512]{2,1,0:T(8,128)} %get-tuple-element.89.mixed_in.refs_1_, ...), custom_call_target="tpu_custom_call" | custom-call | flops 7247757312 | bytes 18874368 | tf_op jit(solution)/shard_map/ffn_forward/pallas_call | solution.py:747
  297.1 32.5 %attn_forward.4 = (bf16[2048,384]{1,0:T(8,128)(2,1)}, f32[384,1024]{1,0:T(8,128)}, bf16[384,256]{1,0:T(8,128)(2,1)}, bf16[384,512]{1,0:T(8,128)(2,1)}, f32[4,96,...) custom-call(bf16[4,96,512]{2,1,0:T(8,128)(2,1)} %bitcast_select_fusion.1.refs_0_.hidden_a.hidden_b, ...), custom_call_target="tpu_custom_call" | custom-call | flops 2415919104 | bytes 6291456 | tf_op jit(solution)/shard_map/attn_forward/pallas_call | solution.py:712
  329.6 33.1 %ffn_forward.4 = (bf16[2048,384]{1,0:T(8,128)(2,1)}, f32[384,3072]{1,0:T(8,128)}, bf16[384,1536]{1,0:T(8,128)(2,1)}, bf16[4,96,512]{2,1,0:T(8,128)(2,1)}) custom-call(bf16[4,96,512]{2,1,0:T(8,128)(2,1)} %get-tuple-element.93.rows, f32[4,96,512]{2,1,0:T(8,128)} %get-tuple-element.94.mixed_in.refs_2_.refs_3_.refs_1_, ...), custom_call_target="tpu_custom_call" | custom-call | flops 7247757312 | bytes 18874368 | tf_op jit(solution)/shard_map/ffn_forward/pallas_call | solution.py:747
  362.7 41.7 %ffn_backward.3 = (bf16[4,384,512]{2,1,0:T(8,128)(2,1)}, bf16[384,3072]{1,0:T(8,128)(2,1)}, f32[4,96,512]{2,1,0:T(8,128)}, bf16[4,96,512]{2,1,0:T(8,128)(2,1)}, ...) custom-call(bf16[4,96,512]{2,1,0:T(8,128)(2,1)} %get-tuple-element.95.refs_0_, bf16[4,96,512]{2,1,0:T(8,128)(2,1)} %bitcast.112, ...), custom_call_target="tpu_custom_call" | custom-call | flops 7247757312 | bytes 18874368 | tf_op jit(solution)/shard_map/ffn_backward/pallas_call | solution.py:777
  405.2 36.0 %attn_backward.3 = (bf16[2048,384]{1,0:T(8,128)(2,1)}, bf16[384,1024]{1,0:T(8,128)(2,1)}, bf16[4,96,512]{2,1,0:T(8,128)(2,1)}, f32[4,512]{1,0:T(4,128)}, f32[8,128]{1,0:T(8,128)}) custom-call(bf16[4,96,512]{2,1,0:T(8,128)(2,1)} %get-tuple-element.97.rows, f32[4,96,512]{2,1,0:T(8,128)} %get-tuple-element.98.grad_mixed, ...), custom_call_target="tpu_custom_call" | custom-call | flops 2415919104 | bytes 6291456 | tf_op jit(solution)/shard_map/attn_backward/pallas_call | solution.py:811
  441.2 41.4 %attn_forward.5 = (bf16[2048,384]{1,0:T(8,128)(2,1)}, f32[384,1024]{1,0:T(8,128)}, bf16[384,256]{1,0:T(8,128)(2,1)}, bf16[384,512]{1,0:T(8,128)(2,1)}, f32[4,96,...) custom-call(bf16[4,96,512]{2,1,0:T(8,128)(2,1)} %get-tuple-element.101.refs_0_, ...), custom_call_target="tpu_custom_call" | custom-call | flops 2415919104 | bytes 6291456 | tf_op jit(solution)/shard_map/attn_forward/pallas_call | solution.py:712
  482.6 32.5 %ffn_forward.5 = (bf16[2048,384]{1,0:T(8,128)(2,1)}, f32[384,3072]{1,0:T(8,128)}, bf16[384,1536]{1,0:T(8,128)(2,1)}, bf16[4,96,512]{2,1,0:T(8,128)(2,1)}) custom-call(bf16[4,96,512]{2,1,0:T(8,128)(2,1)} %get-tuple-element.104.rows, f32[4,96,512]{2,1,0:T(8,128)} %get-tuple-element.105.mixed_in.refs_2_, ...), custom_call_target="tpu_custom_call" | custom-call | flops 7247757312 | bytes 18874368 | tf_op jit(solution)/shard_map/ffn_forward/pallas_call | solution.py:747
  520.0 39.0 %ffn_backward.4 = (bf16[4,384,512]{2,1,0:T(8,128)(2,1)}, bf16[384,3072]{1,0:T(8,128)(2,1)}, f32[4,96,512]{2,1,0:T(8,128)}, bf16[4,96,512]{2,1,0:T(8,128)(2,1)}, f32[4,512]{1,0:T(4,128)}) custom-call(bf16[4,96,512]{2,1,0:T(8,128)(2,1)} %bitcast_select_fusion.refs_0_, f32[4,96,512]{2,1,0:T(8,128)} %get-tuple-element.89.mixed_in.refs_1_, ...), custom_call_target="tpu_custom_call" | custom-call | flops 7247757312 | bytes 18874368 | tf_op jit(solution)/shard_map/ffn_backward/pallas_call | solution.py:777
  559.0 55.7 %attn_backward.4 = (bf16[2048,384]{1,0:T(8,128)(2,1)}, bf16[384,1024]{1,0:T(8,128)(2,1)}, bf16[4,96,512]{2,1,0:T(8,128)(2,1)}, f32[4,512]{1,0:T(4,128)}, f32[8,128]{1,0:T(8,128)}, /*index=5*/bf16[4,96,512]{2,1,0:T(8,128)(2,1)}) custom-call(bf16[4,96,512]{2,1,0:T(8,128)(2,1)} %get-tuple-element.111.rows, f32[4,96,512]{2,1,0:T(8,128)} %get-tuple-element.112.grad_mixed, ...), custom_call_target="tpu_custom_call" | custom-call | flops 2415919104 | bytes 6291456 | tf_op jit(solution)/shard_map/attn_backward/pallas_call | solution.py:811
  614.7 1.8 broadcast_select_fusion.16.refs_0_
  616.5 32.3 %ffn_backward.5 = (bf16[4,384,512]{2,1,0:T(8,128)(2,1)}, bf16[384,3072]{1,0:T(8,128)(2,1)}, f32[4,96,512]{2,1,0:T(8,128)}, bf16[4,96,512]{2,1,0:T(8,128)(2,1)}, f32[4,512]{1,0:T(4,128)}) custom-call(bf16[4,96,512]{2,1,0:T(8,128)(2,1)} %broadcast_select_fusion.16.refs_0_, f32[4,96,512]{2,1,0:T(8,128)} %get-tuple-element.94.mixed_in.refs_2_.refs_3_.refs_1_, ...), custom_call_target="tpu_custom_call" | custom-call | flops 7247757312 | bytes 18874368 | tf_op jit(solution)/shard_map/ffn_backward/pallas_call | solution.py:777
  648.8 15.7 %weight_grad.2 = bf16[2048,3072]{1,0:T(8,128)(2,1)} custom-call(bf16[2048,384]{1,0:T(8,128)(2,1)} %get-tuple-element.120.refs_0_, bf16[2048,384]{1,0:T(8,128)(2,1)} %get-tuple-element.121.refs_1_, bf16[2048,384]{1,0:T(8,128)(2,1)} %get-tuple-element.122.refs_2_, bf16[384,3072]{1,0:T(8,128)(2,1)} %get-tuple-element.123.refs_3_, ...), custom_call_target="tpu_custom_call" | custom-call | flops 9663676416 | bytes 12582912 | tf_op jit(solution)/shard_map/weight_grad/pallas_call | solution.py:849
  664.7 35.9 %attn_backward.5 = (bf16[2048,384]{1,0:T(8,128)(2,1)}, bf16[384,1024]{1,0:T(8,128)(2,1)}, bf16[4,96,512]{2,1,0:T(8,128)(2,1)}, f32[4,512]{1,0:T(4,128)}, f32[8,128]{1,0:T(8,128)}) custom-call(bf16[4,96,512]{2,1,0:T(8,128)(2,1)} %get-tuple-element.130.rows, f32[4,96,512]{2,1,0:T(8,128)} %get-tuple-element.131.grad_mixed, ...), custom_call_target="tpu_custom_call" | custom-call | flops 2415919104 | bytes 6291456 | tf_op jit(solution)/shard_map/attn_backward/pallas_call | solution.py:811
  700.6 9.7 %weight_grad.3 = bf16[2048,1536]{1,0:T(8,128)(2,1)} custom-call(bf16[2048,384]{1,0:T(8,128)(2,1)} %get-tuple-element.142.refs_0_, bf16[2048,384]{1,0:T(8,128)(2,1)} %get-tuple-element.143.refs_1_, bf16[2048,384]{1,0:T(8,128)(2,1)} %get-tuple-element.144.refs_2_, bf16[2048,384]{1,0:T(8,128)(2,1)} %get-tuple-element.145.refs_3_, ...), custom_call_target="tpu_custom_call" | custom-call | flops 4831838208 | bytes 6291456 | tf_op jit(solution)/shard_map/weight_grad/pallas_call | solution.py:849
  710.4 72.7 %reduce-scatter.3.cloned.1.call-done = bf16[512,3072]{1,0:T(8,128)(2,1)} async-done(((bf16[2048,3072]{1,0:T(8,128)(2,1)}), bf16[512,3072]{1,0:T(8,128)(2,1)}) %reduce-scatter.3.cloned.1.call-update) | async-done | bytes 3145744 | tf_op jit(solution)/shard_map/reduce_scatter | solution.py:1059
  784.6 2.1 broadcast_select_fusion.3
  788.2 7.8 fusion.14
  812.5 2.0 select_bitcast_fusion.1
  814.8 2.4 copy.50
  817.2 2.9 select_convert_fusion.1
  820.3 1.9 fusion.5
  822.2 34.4 %reduce-scatter.5.cloned.1.call-done = bf16[512,1536]{1,0:T(8,128)(2,1)} async-done(((bf16[2048,1536]{1,0:T(8,128)(2,1)}), bf16[512,1536]{1,0:T(8,128)(2,1)}) %reduce-scatter.5.cloned.1.call-update) | async-done | bytes 1572880 | tf_op jit(solution)/shard_map/reduce_scatter | solution.py:1059
  856.6 1.6 broadcast_select_fusion.8
  858.4 1.9 maximum_bitcast_fusion.1
  860.4 1.9 maximum_bitcast_fusion
  (190 shorter events, 48.4 us)
Async XLA Ops:
  7.2 242.2 %all-gather.3.cloned.1.call-start = ((), (), s32[]{:S(2)}) async-start(), calls=%async_computation.2 | async-start | bytes 23592960 | tf_op jit(solution)/shard_map/all_gather | solution.py:931
  11.4 2.8 copy-start.16
  13.0 7.3 collective-permute-start.1
  15.6 3.1 copy-start.13
  15.8 2.9 collective-permute-start
  24.8 2.5 copy-start.24
  24.8 2.5 copy-start.25
  24.8 2.7 copy-start.14
  24.8 2.7 copy-start.15
  24.8 639.7 %all-gather.5.cloned.1.call-start = ((), (), s32[]{:S(2)}) async-start(), calls=%async_computation.3 | async-start | bytes 11796480 | tf_op jit(solution)/shard_map/all_gather | solution.py:931
  25.4 5.9 collective-permute-start.2
  482.6 32.5 %copy-start.12 = (bf16[384,1536]{1,0:T(8,128)(2,1)S(1)}, bf16[384,1536]{1,0:T(8,128)(2,1)}, u32[]{:S(2)}) copy-start(bf16[384,1536]{1,0:T(8,128)(2,1)} %get-tuple-element.126) | copy-start | bytes 3538948
  518.2 264.9 %reduce-scatter.3.cloned.1.call-start = ((), (), s32[]{:S(2)}) async-start(), calls=%async_computation.4 | async-start | bytes 15728640 | tf_op jit(solution)/shard_map/reduce_scatter | solution.py:1059
  664.6 192.0 %reduce-scatter.5.cloned.1.call-start = ((), (), s32[]{:S(2)}) async-start(), calls=%async_computation.5 | async-start | bytes 7864320 | tf_op jit(solution)/shard_map/reduce_scatter | solution.py:1059
  710.3 72.8 %copy-start.6 = (bf16[4,96,512]{2,1,0:T(8,128)(2,1)S(1)}, bf16[4,96,512]{2,1,0:T(8,128)(2,1)}, u32[]{:S(2)}) copy-start(bf16[4,96,512]{2,1,0:T(8,128)(2,1)} %get-tuple-element.95.refs_0_) | copy-start | bytes 1179652
  710.3 72.8 %copy-start.19 = (bf16[4,96,512]{2,1,0:T(8,128)(2,1)S(1)}, bf16[4,96,512]{2,1,0:T(8,128)(2,1)}, u32[]{:S(2)}) copy-start(bf16[4,96,512]{2,1,0:T(8,128)(2,1)} %get-tuple-element.91) | copy-start | bytes 1179652
  710.3 72.8 %copy-start.21 = (bf16[4,96,512]{2,1,0:T(8,128)(2,1)S(1)}, bf16[4,96,512]{2,1,0:T(8,128)(2,1)}, u32[]{:S(2)}) copy-start(bf16[4,96,512]{2,1,0:T(8,128)(2,1)} %get-tuple-element.107) | copy-start | bytes 1179652
  788.1 7.9 collective-permute-start.3
  796.0 3.0 copy-start.1
  796.0 5.8 copy-start.18
  796.1 5.8 copy-start.20
  796.1 5.8 copy-start.22
  796.1 3.8 collective-permute-start.4
  799.0 13.6 %collective-permute-start.9 = (f32[256,1536]{1,0:T(8,128)}, f32[256,1536]{1,0:T(8,128)}, u32[]{:S(2)}, u32[]{:S(2)}) collective-permute-start(f32[256,1536]{1,0:T(8,128)} %slice_select_fusion), channel_id=1, source_target_pairs={{0,2},{2,0},{4,6},{6,4},{8,10},{10,8},{12,14},{14,12},{1,3},{3,1},... | collective-permute-start | bytes 4718600 | tf_op jit(solution)/shard_map/ppermute | solution.py:908
  800.5 5.9 collective-permute-start.5
  802.7 5.2 copy-start
  807.1 2.0 copy-start.7
  807.1 2.0 copy-start.8
  807.1 4.3 collective-permute-start.6
  807.9 4.7 copy-start.2
  809.2 8.0 collective-permute-start.8
  858.1 4.2 collective-permute-start.7
  (20 other events, 26.1 us)
Sparse Core Ops, SparseCore 0:
  24.9 224.4 all-gather.2
  518.3 103.9 all-gather.4
  664.7 118.2 reduce-scatter.2
  785.9 70.6 reduce-scatter.4

commit v4 on v3

--- a/solution.py
+++ b/solution.py
@@ -11,6 +11,7 @@
 rope_base = 1000000.0
 masked_score = -1e30
 row_chunks = 4
+background_size = 4 * 384 * 960
 f32 = jnp.float32
 bf16 = jnp.bfloat16
 MIB = 1024 * 1024
@@ -53,9 +54,9 @@
         self.chips = [(number, {"dp": 2 * number + core}) for number in numbers]
         self.send_sems, self.recv_sems = send_sems, recv_sems
 
-    def greet(self, with_section, with_chips=False):
+    def greet(self, with_section, with_chips):
         others = [self.core, self.half] + ([self.section] if with_section else [])
-        self.meet(others + ([device for _, device in self.chips] if with_chips else []))
+        self.meet(others + [device for _, device in self.chips[:with_chips]])
 
     def meet(self, others):
         barrier = pltpu.get_barrier_semaphore()
@@ -132,49 +133,103 @@
     return first + second
 
 
-def chip_gather_kernel(block, out, local_sems, send_sems, recv_sems):
+class ChipGather:
+    def __init__(self, exchange, local, blocks, out, stage):
+        (across, across_device), (along, along_device), _ = exchange.chips
+        at_first = lax.axis_index("section") == 0
+        half = blocks[0].shape[0] // 2
+        first, last = pl.ds(0, half), pl.ds(half, half)
+        target = out.at[exchange.chip]
+        choices = [
+            [
+                exchange.copy(block, target, across_device, stage, 0),
+                exchange.copy(block, target, along_device, stage, 1),
+            ]
+            for block in blocks
+        ]
+        self.direct = choices[0]
+        self.passed = [
+            exchange.copy(out.at[across, first], out.at[across, first], along_device, stage, 2),
+            exchange.copy(out.at[along, last], out.at[along, last], across_device, stage, 3),
+        ]
+        for index, block in enumerate(blocks):
+            here = at_first if index == 0 else jnp.logical_not(at_first)
+
+            def start(index=index):
+                for copy in choices[index]:
+                    copy.start()
+
+            if len(blocks) > 1:
+                pl.when(here)(start)
+            else:
+                start()
+
+        if len(blocks) > 1:
+            local.saves.append(local.load_either(at_first, *blocks, target))
+        else:
+            local.save(blocks[0], target)
+
+    def pass_on(self):
+        for copy, onward in zip(self.direct, self.passed):
+            copy.wait_recv()
+            onward.start()
+
+    def finish(self):
+        for copy in self.passed:
+            copy.wait_recv()
+        return self.direct + self.passed
+
+
+class Background:
+    def __init__(self, exchange, local, spans, sources, targets):
+        self.gathers = [
+            ChipGather(
+                exchange,
+                local,
+                [source.at[pl.ds(first, count)] for source in sources[2 * index : 2 * index + 2]],
+                target,
+                7 + index,
+            )
+            for index, ((first, count), target) in enumerate(zip(spans, targets))
+        ]
+
+        self.late = sum(s.size for s in targets) > background_size
+
+    def pass_on(self, late):
+        if late == self.late:
+            for gather in self.gathers:
+                gather.pass_on()
+
+    def finish(self):
+        return sum([gather.finish() for gather in self.gathers], [])
+
+
+def chip_gather_kernel(*refs):
+    *blocks, out, local_sems, send_sems, recv_sems = refs
     exchange, local = Exchange(send_sems, recv_sems), Local(local_sems)
-    (across, across_device), (along, along_device), _ = exchange.chips
-    exchange.meet([across_device, along_device])
-    half = block.shape[0] // 2
-    first, last = pl.ds(0, half), pl.ds(half, half)
-    target = out.at[exchange.chip]
-    direct = [
-        exchange.copy(block, target, across_device, 0, 0),
-        exchange.copy(block, target, along_device, 0, 1),
-    ]
-    for copy in direct:
-        copy.start()
-    local.save(block, target)
-    passed = [
-        exchange.copy(out.at[across, first], out.at[across, first], along_device, 0, 2),
-        exchange.copy(out.at[along, last], out.at[along, last], across_device, 0, 3),
-    ]
-    for copy, onward in zip(direct, passed):
-        copy.wait_recv()
-        onward.start()
-    for copy in passed:
-        copy.wait_recv()
-    for copy in direct + passed:
+    exchange.meet([device for _, device in exchange.chips[:2]])
+    gather = ChipGather(exchange, local, blocks, out, 0)
+    gather.pass_on()
+    for copy in gather.finish():
         copy.wait_send()
     local.finish()
 
 
-def chip_gather(block):
+def chip_gather(blocks, number):
     return pl.pallas_call(
         chip_gather_kernel,
-        in_specs=[HBM_SPEC],
+        in_specs=[HBM_SPEC] * len(blocks),
         out_specs=HBM_SPEC,
-        out_shape=shape((4,) + block.shape, bf16),
+        out_shape=shape((4,) + blocks[0].shape, bf16),
         scratch_shapes=[
             pltpu.SemaphoreType.DMA((1,)),
             pltpu.SemaphoreType.DMA((1, 4)),
             pltpu.SemaphoreType.DMA((1, 4)),
         ],
-        compiler_params=params(6),
-        cost_estimate=cost(0, 300 * block.size),
+        compiler_params=params(number),
+        cost_estimate=cost(0, 300 * blocks[0].size),
         name="chip_gather",
-    )(block)
+    )(*blocks)
 
 
 def load_pack(pack, held, local):
@@ -254,29 +309,65 @@
     return exponent / jnp.sum(exponent, axis=-1, keepdims=True)
 
 
+class Spread:
+    def __init__(self, exchange, local, rows, moved):
+        side = rows.shape[1] // 2
+        self.own = local.load(rows.at[exchange.chip], moved.at[exchange.chip])
+        self.arrivals, self.onward = [], []
+        for index, (number, device) in enumerate(exchange.chips):
+            self.arrivals.append(
+                exchange.copy(
+                    rows.at[number, pl.ds(0, side)],
+                    moved.at[exchange.chip, pl.ds(0, side)],
+                    device, 5, index,
+                )
+            )
+            self.arrivals[-1].start()
+            self.onward.append(
+                exchange.copy(
+                    moved.at[number, pl.ds(0, side)],
+                    moved.at[number, pl.ds(side, side)],
+                    exchange.core, 6, index,
+                )
+            )
+
+    def pass_on(self, index):
+        self.arrivals[index].wait_recv()
+        self.onward[index].start()
+
+    def finish(self):
+        self.own.wait()
+        for copy in self.onward:
+            copy.wait_recv()
+        return self.arrivals + self.onward
+
+
 def turn_chunk(rows, target, c):
     cols = rows.shape[2]
     target[pl.ds(c * cols, cols), :] = rows[c].T
 
 
 def attn_forward_kernel(
-    width, carry, *refs
+    width, spread, hold, spans, carry, *refs
 ):
+    sources, refs = refs[: 2 * len(spans)], refs[2 * len(spans) :]
     if carry:
         carried, refs = refs[0], refs[1:]
     (
         hidden, pack, model_gains, gains, tables_in, masks_in,
-        turned_out, projected_out, values_out, attended_out, mixed_out, normed_ffn_rows,
+        moved_out, projected_out, values_out, attended_out, mixed_out, normed_ffn_rows,
     ), refs = refs[:12], refs[12:]
     if carry:
         arrived, refs = refs[0], refs[1:]
+    targets, refs = refs[: len(spans)], refs[len(spans) :]
     (
-        tables, masks, normed, turned, projected, values, attended, mixed,
+        tables, masks, normed, moved, projected, values, attended, mixed,
         held, keep, send_core, recv_core, send_half, recv_half, local_sems, send_sems, recv_sems,
     ) = refs
     exchange, local = Exchange(send_sems, recv_sems), Local(local_sems)
-    exchange.greet(carry)
+    exchange.greet(carry, (3 if spread else 2 if spans else 0))
     loads = load_pack(pack, held, local)
+    background = Background(exchange, local, spans, sources, targets)
     extra = [local.load(tables_in, tables), local.load(masks_in, masks)]
     chunks, own, cols = hidden.shape
     length = 2 * own
@@ -294,6 +385,7 @@
         accumulate(projected, normed[c], held, c * cols, 0, 2 * q_width, c == 0)
 
     copies = gather_then(exchange, normed, project)
+    moving = Spread(exchange, local, normed, moved) if spread else None
     hops = []
     if carry:
         hops = [exchange.copy(carried, arrived, exchange.section, 4, 0)]
@@ -319,12 +411,18 @@
                 weights = softmax_rows(query_rot, key_rot, allowed, scale)
                 attended[at, head] = dot_nn(weights.astype(bf16), value).astype(bf16)
     local.save(attended, attended_out)
+    background.pass_on(False)
 
     def make(c):
         return dot_nt(attended[...], held[c * cols : (c + 1) * cols, 2 * q_width :])
 
     def idle(c):
-        turn_chunk(normed, turned, c)
+        if not (spread or hold):
+            turn_chunk(normed, moved, c)
+        elif spread and c > 0:
+            moving.pass_on(c - 1)
+        if c == chunks - 2:
+            background.pass_on(True)
 
     def finish(c, summed):
         mixed[c] = hidden[c].astype(f32) + summed
@@ -332,7 +430,9 @@
     copies += scatter_from(
         exchange, make, idle, finish, keep, send_core, recv_core, send_half, recv_half
     )
-    local.save(turned, turned_out)
+    if spread:
+        copies += moving.finish()
+    local.save(normed if hold else moved, moved_out)
     local.save(mixed, mixed_out)
     rows = mixed[...]
     inverse = lax.rsqrt(row_mean(rows * rows) + norm_eps)
@@ -340,23 +440,33 @@
         normed_ffn_rows[c] = (rows[c] * inverse[0] * model_gains[1, c][None, :]).astype(bf16)
     for copy in hops:
         copy.wait()
+    copies += background.finish()
     for copy in copies:
         copy.wait_send()
     local.finish()
 
 
 def ffn_forward_kernel(
-    hop, rows, mixed_in, pack, turned_out, gate_up_out, activated_out, result, *rest
+    hop, spread, spans, *refs
 ):
+    if spread:
+        held_rows, refs = refs[0], refs[1:]
+    sources, refs = refs[: 2 * len(spans)], refs[2 * len(spans) :]
+    rows, mixed_in, pack, turned_out, gate_up_out, activated_out, result, *rest = refs
     if hop:
         arrived, rest = rest[0], rest[1:]
+    if spread:
+        moved, rest = rest[0], rest[1:]
+    targets, rest = rest[: len(spans)], rest[len(spans) :]
     (
         normed, turned, mixed, activated, total,
         held, keep, send_core, recv_core, send_half, recv_half, local_sems, send_sems, recv_sems,
     ) = rest
     exchange, local = Exchange(send_sems, recv_sems), Local(local_sems)
-    exchange.greet(hop)
+    exchange.greet(hop, 3 if spread else 2 if spans else 0)
     loads = load_pack(pack, held, local)
+    moving = Spread(exchange, local, held_rows, moved) if spread else None
+    background = Background(exchange, local, spans, sources, targets)
     mixed_load = local.load(mixed_in, mixed)
     chunks, own, cols = rows.shape
     units = activated.shape[1]
@@ -380,6 +490,7 @@
 
     lax.fori_loop(0, units // blk, activate, 0)
     local.save(activated, activated_out)
+    background.pass_on(False)
     mixed_load.wait()
     hops = []
 
@@ -388,6 +499,10 @@
 
     def idle(c):
         turn_chunk(normed, turned, c)
+        if spread and c > 0:
+            moving.pass_on(c - 1)
+        if c == chunks - 2:
+            background.pass_on(True)
 
     def finish(c, summed):
         result[c] = (mixed[c] + summed).astype(bf16)
@@ -401,12 +516,16 @@
     local.save(turned, turned_out)
     for copy in hops:
         copy.wait()
+    copies += background.finish()
+    if spread:
+        copies += moving.finish()
     for copy in copies:
         copy.wait_send()
     local.finish()
 
 
-def ffn_backward_kernel(spread, carry, *refs):
+def ffn_backward_kernel(spread, spans, carry, *refs):
+    sources, refs = refs[: 2 * len(spans)], refs[2 * len(spans) :]
     if carry:
         carried, refs = refs[0], refs[1:]
     (
@@ -415,14 +534,16 @@
     ), refs = refs[:12], refs[12:]
     if carry:
         arrived, refs = refs[0], refs[1:]
+    targets, refs = refs[: len(spans)], refs[len(spans) :]
     (
         grad_down, moved, mixed, grads, pre, total,
         held, keep, send_core, recv_core, send_half, recv_half, local_sems, send_sems, recv_sems,
     ) = refs
     exchange, local = Exchange(send_sems, recv_sems), Local(local_sems)
-    exchange.greet(carry, spread)
+    exchange.greet(carry, 3 if spread else 0)
     at_first = lax.axis_index("section") == 0
     loads = load_pack(pack, held, local)
+    background = Background(exchange, local, spans, sources, targets)
     pre_load = local.load_either(at_first, gate_up_a, gate_up_b, pre)
     mixed_load = local.load_either(at_first, mixed_a, mixed_b, mixed)
     chunks, own, cols = rows.shape
@@ -439,26 +560,7 @@
     if carry:
         hops = [exchange.copy(carried, arrived, exchange.section, 4, 0)]
         hops[0].start()
-    side = 2 * own
-    arrivals, onward = [], []
-    if spread:
-        for index, (number, device) in enumerate(exchange.chips):
-            arrivals.append(
-                exchange.copy(
-                    grad_down.at[number, pl.ds(0, side)],
-                    moved.at[exchange.chip, pl.ds(0, side)],
-                    device, 5, index,
-                )
-            )
-            arrivals[-1].start()
-            onward.append(
-                exchange.copy(
-                    moved.at[number, pl.ds(0, side)],
-                    moved.at[number, pl.ds(side, side)],
-                    exchange.core, 6, index,
-                )
-            )
-        moved[exchange.chip] = grad_down[exchange.chip]
+    moving = Spread(exchange, local, grad_down, moved) if spread else None
     pre_load.wait()
     blk = 256
 
@@ -474,6 +576,7 @@
 
     lax.fori_loop(0, units // blk, activate, 0)
     local.save(grads, grads_out)
+    background.pass_on(False)
 
     def make(c):
         return dot_nt(grads[...], held[c * cols : (c + 1) * cols, : 2 * units])
@@ -482,8 +585,9 @@
         if not spread:
             turn_chunk(grad_down, moved, c)
         elif c > 0:
-            arrivals[c - 1].wait_recv()
-            onward[c - 1].start()
+            moving.pass_on(c - 1)
+        if c == chunks - 2:
+            background.pass_on(True)
 
     def finish(c, summed):
         grad_mixed[c] = summed
@@ -491,9 +595,8 @@
     copies += scatter_from(
         exchange, make, idle, finish, keep, send_core, recv_core, send_half, recv_half
     )
-    for copy in onward:
-        copy.wait_recv()
-    copies += arrivals + onward
+    if spread:
+        copies += moving.finish()
     local.save(moved, moved_out)
     mixed_load.wait()
     norm_step(mixed[...], grad_mixed[...], model_gains, 1, rows, grad_mixed, gain_grad)
@@ -501,6 +604,7 @@
         grad_proj_rows[c] = grad_mixed[c].astype(bf16)
     for copy in hops:
         copy.wait()
+    copies += background.finish()
     for copy in copies:
         copy.wait_send()
     local.finish()
@@ -517,20 +621,26 @@
 
 
 def attn_backward_kernel(
-    width, hop, rows, grad_mixed, hidden_a, hidden_b, projected_a, projected_b, values_a, values_b,
-    pack, model_gains, gains, tables_in, masks_in,
-    turned_out, grads_out, grad_hidden, gain_grad, head_gain_grads, *rest
+    width, spread, spans, hop, *refs
 ):
+    sources, refs = refs[: 2 * len(spans)], refs[2 * len(spans) :]
+    (
+        rows, grad_mixed, hidden_a, hidden_b, projected_a, projected_b, values_a, values_b,
+        pack, model_gains, gains, tables_in, masks_in,
+        moved_out, grads_out, grad_hidden, gain_grad, head_gain_grads, *rest
+    ) = refs
     if hop:
         arrived, rest = rest[0], rest[1:]
+    targets, rest = rest[: len(spans)], rest[len(spans) :]
     (
-        tables, masks, grad_proj, turned, grads, hidden, projected, values, total, summed_rows,
+        tables, masks, grad_proj, moved, grads, hidden, projected, values, total, summed_rows,
         held, keep, send_core, recv_core, send_half, recv_half, local_sems, send_sems, recv_sems,
     ) = rest
     exchange, local = Exchange(send_sems, recv_sems), Local(local_sems)
-    exchange.greet(hop)
+    exchange.greet(hop, 3 if spread else 0)
     at_first = lax.axis_index("section") == 0
     loads = load_pack(pack, held, local)
+    background = Background(exchange, local, spans, sources, targets)
     extra = [local.load(tables_in, tables), local.load(masks_in, masks)]
     projected_load = local.load_either(at_first, projected_a, projected_b, projected)
     values_load = local.load_either(at_first, values_a, values_b, values)
@@ -549,6 +659,7 @@
         accumulate(total, grad_proj[c], held, c * cols, 2 * q_width, q_width, c == 0)
 
     copies = gather_then(exchange, grad_proj, project)
+    moving = Spread(exchange, local, grad_proj, moved) if spread else None
     projected_load.wait()
     values_load.wait()
     for load in extra:
@@ -590,6 +701,7 @@
             first += kv_width
             grads[at, first : first + width] = grad_value.astype(bf16)
     local.save(grads, grads_out)
+    background.pass_on(False)
     head_gain_grads[...] = jnp.concatenate(
         [gain_q_sum, gain_k_sum, jnp.zeros((6, width), f32)], axis=0
     )
@@ -598,7 +710,12 @@
         return dot_nt(grads[...], held[c * cols : (c + 1) * cols, : 2 * q_width])
 
     def idle(c):
-        turn_chunk(grad_proj, turned, c)
+        if not spread:
+            turn_chunk(grad_proj, moved, c)
+        elif c > 0:
+            moving.pass_on(c - 1)
+        if c == chunks - 2:
+            background.pass_on(True)
 
     def finish(c, summed):
         summed_rows[c] = summed
@@ -606,7 +723,9 @@
     copies += scatter_from(
         exchange, make, idle, finish, keep, send_core, recv_core, send_half, recv_half
     )
-    local.save(turned, turned_out)
+    if spread:
+        copies += moving.finish()
+    local.save(moved, moved_out)
     hidden_load.wait()
     norm_step(
         hidden[...].astype(f32), summed_rows[...], model_gains, 0, grad_mixed, grad_hidden, gain_grad
@@ -620,6 +739,7 @@
             copy.start()
         for copy in hops:
             copy.wait()
+    copies += background.finish()
     for copy in copies:
         copy.wait_send()
     local.finish()
@@ -685,9 +805,9 @@
         pltpu.VMEM((chunks, 2 * own, cols), bf16),
         pltpu.VMEM((chunks, own, cols), bf16),
         pltpu.VMEM((chunks, own, cols), bf16),
-        pltpu.SemaphoreType.DMA((12,)),
-        pltpu.SemaphoreType.DMA((7, chunks)),
-        pltpu.SemaphoreType.DMA((7, chunks)),
+        pltpu.SemaphoreType.DMA((16,)),
+        pltpu.SemaphoreType.DMA((9, chunks)),
+        pltpu.SemaphoreType.DMA((9, chunks)),
     ]
 
 
@@ -699,34 +819,48 @@
     )
 
 
+class Numbers(dict):
+    def of(self, *key):
+        return self.setdefault(key, len(self))
+
+
+def spans_of(background):
+    return tuple((first, count) for _, first, count in background)
+
+
+def gather_shapes(background):
+    return [shape((4, count, blocks[0].shape[1]), bf16) for blocks, _, count in background]
+
+
 def cost(flops, size):
     return pl.CostEstimate(flops=int(flops), bytes_accessed=int(size), transcendentals=0)
 
 
-def attn_forward(hidden, pack, model_gains, gains, tables, masks, carried):
+def attn_forward(hidden, pack, model_gains, gains, tables, masks, spread, hold, carried, background, numbers):
     chunks, own, cols = hidden.shape
     tokens, q_width, width = 4 * own, pack.shape[1] // 3, gains.shape[1]
-    depth = chunks * cols
-    carry = carried is not None
+    moved = (chunks, tokens, cols) if spread or hold else (chunks * cols, tokens)
+    carry, spans = carried is not None, spans_of(background)
     rows = shape((chunks, own, cols), bf16)
     return pl.pallas_call(
-        functools.partial(attn_forward_kernel, width, carry),
-        in_specs=[HBM_SPEC] * carry + [VMEM_SPEC, HBM_SPEC] + [VMEM_SPEC] * 2 + [HBM_SPEC] * 2,
-        out_specs=[HBM_SPEC] * 5 + [VMEM_SPEC] + [HBM_SPEC] * carry,
+        functools.partial(attn_forward_kernel, width, spread, hold, spans, carry),
+        in_specs=[HBM_SPEC] * (2 * len(spans) + carry) + [VMEM_SPEC, HBM_SPEC] + [VMEM_SPEC] * 2 + [HBM_SPEC] * 2,
+        out_specs=[HBM_SPEC] * 5 + [VMEM_SPEC] + [HBM_SPEC] * (carry + len(spans)),
         out_shape=[
-            shape((depth, tokens), bf16),
+            shape(moved, bf16),
             shape((tokens, 2 * q_width), f32),
             shape((tokens, q_width // 2), bf16),
             shape((tokens, q_width), bf16),
             shape((chunks, own, cols), f32),
             rows,
         ]
-        + [rows] * carry,
+        + [rows] * carry
+        + gather_shapes(background),
         scratch_shapes=[
             pltpu.VMEM(tables.shape, f32),
             pltpu.VMEM(masks.shape, f32),
             pltpu.VMEM((chunks, tokens, cols), bf16),
-            pltpu.VMEM((depth, tokens), bf16),
+            pltpu.VMEM(moved, bf16),
             pltpu.VMEM((tokens, 2 * q_width), f32),
             pltpu.VMEM((tokens, q_width // 2), bf16),
             pltpu.VMEM((tokens, q_width), bf16),
@@ -734,26 +868,29 @@
             pltpu.VMEM(pack.shape, bf16),
         ]
         + exchange_scratch(chunks, own, cols),
-        compiler_params=params(8 if carry else 0),
+        compiler_params=params(numbers.of("attn_forward", hold, carry, spans)),
         cost_estimate=cost(2 * tokens * pack.size, pack.size * 2),
         name="attn_forward",
-    )(*([carried] if carry else []), hidden, pack, model_gains, gains, tables, masks)
-
-
-def ffn_forward(rows, mixed, pack, hop):
+    )(*sum([list(blocks) for blocks, *_ in background], []), *([carried] if carry else []), hidden, pack, model_gains, gains, tables, masks)
+
+
+def ffn_forward(rows, mixed, pack, hop, held_rows, background, numbers):
     chunks, own, cols = rows.shape
     tokens, units = 4 * own, pack.shape[1] // 3
     depth = chunks * cols
+    spans, spread = spans_of(background), held_rows is not None
     return pl.pallas_call(
-        functools.partial(ffn_forward_kernel, hop),
-        in_specs=[VMEM_SPEC, HBM_SPEC, HBM_SPEC],
-        out_specs=[HBM_SPEC] * 3 + [VMEM_SPEC] * (2 if hop else 1),
+        functools.partial(ffn_forward_kernel, hop, spread, spans),
+        in_specs=[HBM_SPEC] * (spread + 2 * len(spans)) + [VMEM_SPEC, HBM_SPEC, HBM_SPEC],
+        out_specs=[HBM_SPEC] * 3 + [VMEM_SPEC] * (2 if hop else 1) + [HBM_SPEC] * (spread + len(spans)),
         out_shape=[
             shape((depth, tokens), bf16),
             shape((tokens, 2 * units), f32),
             shape((tokens, units), bf16),
         ]
-        + [shape((chunks, own, cols), bf16)] * (2 if hop else 1),
+        + [shape((chunks, own, cols), bf16)] * (2 if hop else 1)
+        + [shape((chunks, tokens, cols), bf16)] * spread
+        + gather_shapes(background),
         scratch_shapes=[
             pltpu.VMEM((chunks, tokens, cols), bf16),
             pltpu.VMEM((depth, tokens), bf16),
@@ -763,21 +900,21 @@
             pltpu.VMEM(pack.shape, bf16),
         ]
         + exchange_scratch(chunks, own, cols),
-        compiler_params=params(1 if hop else 2),
+        compiler_params=params(numbers.of("ffn_forward", hop, spread, spans)),
         cost_estimate=cost(2 * tokens * pack.size, pack.size * 2),
         name="ffn_forward",
-    )(rows, mixed, pack)
-
-
-def ffn_backward(rows, mixed, gate_up, pack, model_gains, spread, carried):
+    )(*([held_rows] if spread else []), *sum([list(blocks) for blocks, *_ in background], []), rows, mixed, pack)
+
+
+def ffn_backward(rows, mixed, gate_up, pack, model_gains, spread, carried, background, numbers):
     chunks, own, cols = rows.shape
     tokens, units = 4 * own, pack.shape[1] // 3
     moved = (chunks, tokens, cols) if spread else (chunks * cols, tokens)
-    carry = carried is not None
+    carry, spans = carried is not None, spans_of(background)
     return pl.pallas_call(
-        functools.partial(ffn_backward_kernel, spread, carry),
-        in_specs=[HBM_SPEC] * carry + [VMEM_SPEC] + [HBM_SPEC] * 5 + [VMEM_SPEC],
-        out_specs=[HBM_SPEC] * 2 + [VMEM_SPEC] * 3 + [HBM_SPEC] * carry,
+        functools.partial(ffn_backward_kernel, spread, spans, carry),
+        in_specs=[HBM_SPEC] * (2 * len(spans) + carry) + [VMEM_SPEC] + [HBM_SPEC] * 5 + [VMEM_SPEC],
+        out_specs=[HBM_SPEC] * 2 + [VMEM_SPEC] * 3 + [HBM_SPEC] * (carry + len(spans)),
         out_shape=[
             shape(moved, bf16),
             shape((tokens, 2 * units), bf16),
@@ -785,7 +922,8 @@
             shape((chunks, own, cols), bf16),
             shape((chunks, cols), f32),
         ]
-        + [shape((chunks, own, cols), bf16)] * carry,
+        + [shape((chunks, own, cols), bf16)] * carry
+        + gather_shapes(background),
         scratch_shapes=[
             pltpu.VMEM((chunks, tokens, cols), bf16),
             pltpu.VMEM(moved, bf16),
@@ -796,35 +934,38 @@
             pltpu.VMEM(pack.shape, bf16),
         ]
         + exchange_scratch(chunks, own, cols),
-        compiler_params=params(9 if carry else 3),
+        compiler_params=params(numbers.of("ffn_backward", carry, spans)),
         cost_estimate=cost(2 * tokens * pack.size, pack.size * 2),
         name="ffn_backward",
-    )(*([carried] if carry else []), rows, *mixed, *gate_up, pack, model_gains)
+    )(*sum([list(blocks) for blocks, *_ in background], []), *([carried] if carry else []), rows, *mixed, *gate_up, pack, model_gains)
 
 
 def attn_backward(
-    rows, grad_mixed, hidden, projected, values, pack, model_gains, gains, tables, masks, hop
+    rows, grad_mixed, hidden, projected, values, pack, model_gains, gains, tables, masks, spread, hop,
+    background, numbers
 ):
     chunks, own, cols = rows.shape
     tokens, q_width, width = 4 * own, pack.shape[1] // 3, gains.shape[1]
-    depth = chunks * cols
+    moved = (chunks, tokens, cols) if spread else (chunks * cols, tokens)
+    spans = spans_of(background)
     return pl.pallas_call(
-        functools.partial(attn_backward_kernel, width, hop),
-        in_specs=[VMEM_SPEC] * 2 + [HBM_SPEC] * 7 + [VMEM_SPEC] * 2 + [HBM_SPEC] * 2,
-        out_specs=[HBM_SPEC] * 2 + [VMEM_SPEC] * (4 if hop else 3),
+        functools.partial(attn_backward_kernel, width, spread, spans, hop),
+        in_specs=[HBM_SPEC] * (2 * len(spans)) + [VMEM_SPEC] * 2 + [HBM_SPEC] * 7 + [VMEM_SPEC] * 2 + [HBM_SPEC] * 2,
+        out_specs=[HBM_SPEC] * 2 + [VMEM_SPEC] * (4 if hop else 3) + [HBM_SPEC] * len(spans),
         out_shape=[
-            shape((depth, tokens), bf16),
+            shape(moved, bf16),
             shape((tokens, 2 * q_width), bf16),
             shape((chunks, own, cols), bf16),
             shape((chunks, cols), f32),
             shape((8, width), f32),
         ]
-        + [shape((chunks, own, cols), bf16)] * (1 if hop else 0),
+        + [shape((chunks, own, cols), bf16)] * (1 if hop else 0)
+        + gather_shapes(background),
         scratch_shapes=[
             pltpu.VMEM(tables.shape, f32),
             pltpu.VMEM(masks.shape, f32),
             pltpu.VMEM((chunks, tokens, cols), bf16),
-            pltpu.VMEM((depth, tokens), bf16),
+            pltpu.VMEM(moved, bf16),
             pltpu.VMEM((tokens, 2 * q_width), bf16),
             pltpu.VMEM((chunks, own, cols), bf16),
             pltpu.VMEM((tokens, 2 * q_width), f32),
@@ -834,11 +975,11 @@
             pltpu.VMEM(pack.shape, bf16),
         ]
         + exchange_scratch(chunks, own, cols),
-        compiler_params=params(4 if hop else 5),
+        compiler_params=params(numbers.of("attn_backward", hop, spans)),
         cost_estimate=cost(2 * tokens * pack.size, pack.size * 2),
         name="attn_backward",
     )(
-        rows, grad_mixed, *hidden, *projected, *values, pack, model_gains, gains, tables, masks
+        *sum([list(blocks) for blocks, *_ in background], []), rows, grad_mixed, *hidden, *projected, *values, pack, model_gains, gains, tables, masks
     )
 
 
@@ -931,6 +1072,7 @@
         return lax.all_gather(block, "dp", axis=0, tiled=True, axis_index_groups=chip_groups)
 
     square = n_chip == row_chunks
+    numbers = Numbers()
     attn_block = chip_block(
         [
             split_columns(q_weight[0]),
@@ -944,7 +1086,7 @@
     )
     if square:
         attn_block, ffn_block = lax.optimization_barrier((attn_block, ffn_block))
-        attn_pack = chip_gather(attn_block).reshape(depth, -1)
+        attn_pack = chip_gather([attn_block], numbers.of("chip_gather", 0)).reshape(depth, -1)
     else:
         attn_pack = gathered(attn_block)
     ffn_pack = gathered(ffn_block)
@@ -985,67 +1127,94 @@
     results, backs, saves = [], [], []
     grads, ffn_saves, attn_saves, gains = [], [], [], []
 
-    def forward_step(step, arrived, hop, carried=None):
+    def forward_step(step, arrived, hop, carried=None, attn_work=(), ffn_work=()):
         hidden = inputs[step] if step < 2 else zero_rows
         if step > 0:
             hidden = pick(hidden, arrived)
-        turned_in, projected, values, attended, mixed, rows, *carried = attn_forward(
-            hidden, attn_pack, model_gains, head_gains, tables, forward_masks[step], carried
-        )
-        turned_mid, gate_up, activated, result, *rest = ffn_forward(rows, mixed, ffn_pack, hop)
+        turned_in, projected, values, attended, mixed, rows, *more = attn_forward(
+            hidden, attn_pack, model_gains, head_gains, tables, forward_masks[step],
+            square and step > 0, square and step == 0, carried, attn_work, numbers,
+        )
+        turned_mid, gate_up, activated, result, *rest = ffn_forward(
+            rows, mixed, ffn_pack, hop, turned_in if square and step == 0 else None, ffn_work, numbers
+        )
+        if square and step == 0:
+            turned_in = rest.pop(1)
         results.append(result)
         backs.append((hidden, projected, values, mixed, gate_up))
         saves.append((turned_in, attended, turned_mid, activated))
-        return (rest + carried + [None])[0]
-
-    def back_ffn(step, arrived, carried=None):
+        return more + rest
+
+    def back_ffn(step, arrived, carried=None, work=()):
         rows = pick(arrived, cotangents[step] if step < 2 else zero_rows)
         *_, mixed, gate_up = zip(backs[0], backs[2]) if step == 1 else zip(backs[1], backs[1])
-        turned_rows, ffn_grads, grad_mixed, proj_rows, gain_grad, *carried = ffn_backward(
-            rows, mixed, gate_up, ffn_pack, model_gains, square, carried
+        turned_rows, ffn_grads, grad_mixed, proj_rows, gain_grad, *more = ffn_backward(
+            rows, mixed, gate_up, ffn_pack, model_gains, square, carried, work, numbers
         )
         ffn_saves.append((turned_rows, ffn_grads))
-        return proj_rows, grad_mixed, gain_grad, *carried
-
-    def back_attn(step, proj_rows, grad_mixed, ffn_gain_grad, hop):
+        return (proj_rows, grad_mixed, gain_grad), more
+
+    def back_attn(step, proj_rows, grad_mixed, ffn_gain_grad, hop, work=()):
         hidden, projected, values, *_ = (
             zip(backs[0], backs[2]) if step == 1 else zip(backs[1], backs[1])
         )
         turned_rows, attn_grads, grad_hidden, attn_gain_grad, head_gain_grads, *rest = attn_backward(
             proj_rows, grad_mixed, hidden, projected, values, attn_pack, model_gains, head_gains,
-            tables, backward_masks[step], hop,
+            tables, backward_masks[step], square, hop, work, numbers,
         )
         attn_saves.append((turned_rows, attn_grads))
         grads.append(grad_hidden)
         gains.append((attn_gain_grad, ffn_gain_grad, head_gain_grads))
-        return rest[0] if hop else None
+        return rest
 
     def column(table, item):
         return [row[item] for row in table]
 
-    arrived = forward_step(0, zero_rows, True)
+    def work(*items):
+        return items if square else ()
+
+    def of_micro(micro, item):
+        return saves[micro][item], saves[micro + 1][item]
+
+    tokens = 2 * length
+    (arrived,) = forward_step(0, zero_rows, True)
     forward_step(1, arrived, False)
-    *others, arrived = back_ffn(0, zero_rows, results[1])
-    back_attn(0, *others, False)
-    grad_arrived = forward_step(2, arrived, False, grads[0])
+    active, attended = of_micro(0, 3), of_micro(0, 1)
+    part = tokens // 4
+    others, (arrived, *pieces) = back_ffn(0, zero_rows, results[1], work((active, 0, part)))
+    active_pieces = [(0, pieces)]
+    pieces = back_attn(0, *others, False, work((active, part, part)))
+    active_pieces.append((part, pieces))
+    grad_arrived, *pieces = forward_step(
+        2, arrived, False, grads[0], work((active, 2 * part, part)),
+        work((active, 3 * part, part), (attended, 0, tokens)),
+    )
+    active_pieces += [(2 * part, pieces[:1]), (3 * part, pieces[1:2])]
+    attended_all = [pieces[2:]]
+    active, attended = of_micro(1, 3), of_micro(1, 1)
+    side = tokens // 2
     grad_arrived, results[2] = lax.optimization_barrier((grad_arrived, results[2]))
-    grad_arrived = back_attn(1, *back_ffn(1, grad_arrived), True)
-    if square:
-        active = [pick(saves[micro][3], saves[micro + 1][3]) for micro in range(2)]
-        active_all = gathered(jnp.concatenate(active, axis=0))
-    proj_rows, *others = back_ffn(2, grad_arrived)
+    others, pieces = back_ffn(1, grad_arrived, None, work((active, 0, side)))
+    late_pieces = [(0, pieces)]
+    grad_arrived, *pieces = back_attn(
+        1, *others, True, work((active, side, side), (attended, 0, tokens))
+    )
+    late_pieces.append((side, pieces[:1]))
+    attended_all.append(pieces[1:])
+    early_block = attn_saves[1][1], attn_saves[0][1]
+    (proj_rows, *others), early_grads = back_ffn(2, grad_arrived, None, work((early_block, 0, tokens)))
     if square:
         ffn_partial = weight_grad([column(saves, 2)], [column(ffn_saves, 1)])
-        ffn_partial, active_all = lax.optimization_barrier((ffn_partial, active_all))
     else:
         ffn_partial = weight_grad(
             [column(saves, 2), column(ffn_saves, 0)], [column(ffn_saves, 1), column(saves, 3)]
         )
     proj_rows, ffn_partial = lax.optimization_barrier((proj_rows, ffn_partial))
     back_attn(2, proj_rows, *others, False)
-    attn_partial = weight_grad(
-        [column(saves, 0), column(attn_saves, 0)], [column(attn_saves, 1), column(saves, 1)]
-    )
+    if not square:
+        attn_partial = weight_grad(
+            [column(saves, 0), column(attn_saves, 0)], [column(attn_saves, 1), column(saves, 1)]
+        )
     gain_total = functools.reduce(lambda a, b: jax.tree.map(jnp.add, a, b), gains)
 
     section_outputs = jnp.stack(
@@ -1069,18 +1238,43 @@
             jnp.where(first_core, other, own).astype(f32),
         )
 
-    attn_partial, ffn_rows = lax.optimization_barrier((attn_partial, scattered(ffn_partial)))
-    ffn_sides = owned(ffn_rows)
-    attn_sides = owned(scattered(attn_partial))
     units = gate_weight.shape[2] // 2
     if square:
-        spread_rows = jnp.concatenate(
-            [pick(ffn_saves[micro + 1][0], ffn_saves[micro][0]) for micro in range(2)], axis=1
-        ).reshape(-1, cols)
-        down_sides = owned(dot_tn(spread_rows, active_all))
+        late_grads = chip_gather([attn_saves[2][1], attn_saves[1][1]], numbers.of("chip_gather", 1))
+
+        def flat(rows):
+            return rows.reshape(-1, rows.shape[-1])
+
+        def summed(rows, pieces):
+            return sum(
+                dot_tn(flat(rows[:, first : first + piece.shape[1]]), flat(piece))
+                for first, (piece,) in pieces
+            )
+
+        def forward_rows(micro):
+            return pick(saves[micro][0], saves[micro + 1][0])
+
+        def backward_rows(table, micro):
+            return pick(table[micro + 1][0], table[micro][0])
+
+        down_sides = owned(
+            summed(backward_rows(ffn_saves, 0), active_pieces)
+            + summed(backward_rows(ffn_saves, 1), late_pieces)
+        )
+        o_rows = sum(
+            summed(backward_rows(attn_saves, micro), [(0, attended_all[micro])])
+            for micro in range(2)
+        )
+        qkv_rows = summed(forward_rows(0), [(0, early_grads)]) + summed(
+            forward_rows(1), [(0, [late_grads])]
+        )
+        attn_sides = owned(jnp.concatenate([qkv_rows, o_rows], axis=1))
+        ffn_sides = owned(scattered(ffn_partial))
     else:
+        attn_partial, ffn_rows = lax.optimization_barrier((attn_partial, scattered(ffn_partial)))
+        ffn_sides = owned(ffn_rows)
+        attn_sides = owned(scattered(attn_partial))
         down_sides = [side[:, 2 * units :] for side in ffn_sides]
-    attn_sides = owned(scattered(attn_partial))
     q_width = q_weight.shape[2] // 2
     kv_width = k_weight.shape[2] // 2
 

time: 879 us -> 857 us (0.975)
  waiting for transfers between devices: 191 us -> 85.9 us
  Pallas kernels: 589 us -> 644 us
  local copies, waits for them, and re-layouts: 22.3 us -> 33.7 us
    reduce_scatter x2 -> x1, waiting for transfers between devices: 107 us -> 2.04 us  [scattered(): lax.psum_scatter(partial, 'dp', scatter_dimension=0, tiled=True, axis_ind...]
    pallas_call x13 -> x14, Pallas kernels: 563 us -> 628 us  [the longest x2 157 us: chip_gather(): pl.pallas_call(chip_gather_kernel, in_specs=[HBM_SPEC] * len(blocks), out...]
    pallas_call x2 -> x1, Pallas kernels: 25.5 us -> 16 us  [weight_grad(): pl.pallas_call(functools.partial(weight_grad_kernel, blk, len(lefts)), in...]
    all_gather x2 -> x1, waiting for transfers between devices: 79.4 us -> 78.8 us  [gathered(): lax.all_gather(block, 'dp', axis=0, tiled=True, axis_index_groups=chip_gr...]
  transfers between devices with their start and end apart: 14 -> 12, of which waited for: 6 -> 4; matrix products, arithmetic and copies ran while one was open for 6% -> 8% of each run, Pallas kernels for 37% -> 27%
where the time goes in v4:
time: 857 us; the launch traced here: 851 us
  Pallas kernels  644 us (75%)
  waiting for transfers between devices  85.9 us (10%)
  other arithmetic  52.1 us (6%)
  local copies, waits for them, and re-layouts  33.7 us (4%)
  matrix products  15.2 us (2%)
  between operations  15.1 us (2%)
    pallas_call x2, Pallas kernels, chip_gather(): pl.pallas_call(chip_gather_kernel, in_specs=[HBM_SPEC] * len(blocks), out...  157 us
    pallas_call x3, Pallas kernels, attn_backward(): pl.pallas_call(functools.partial(attn_backward_kernel, width, spread, spa...  131 us
    pallas_call x3, Pallas kernels, ffn_backward(): pl.pallas_call(functools.partial(ffn_backward_kernel, spread, spans, carr...  117 us
    pallas_call x3, Pallas kernels, ffn_forward(): pl.pallas_call(functools.partial(ffn_forward_kernel, hop, spread, spans),...  115 us
    pallas_call x3, Pallas kernels, attn_forward(): pl.pallas_call(functools.partial(attn_forward_kernel, width, spread, hold...  109 us
    all_gather x1, waiting for transfers between devices, gathered(): lax.all_gather(block, 'dp', axis=0, tiled=True, axis_index_groups=chip_gr...  78.8 us
  transfers between devices with their start and end apart: 12, of which 4 were waited for; matrix products, arithmetic and copies ran while one was open for 8% of the time, Pallas kernels for 27%

profile of v4, /device:TPU:0, one launch (start us, length us, event | category | flops | bytes accessed | tf_op | source)
XLA Modules:
  0.0 851.1 jit_solution(15090108716779516051)
XLA Ops:
  15.9 2.8 collective-permute-done
  20.2 2.1 broadcast_select_fusion.1
  22.3 2.5 pad_maximum_fusion
  34.0 104.4 %chip_gather.2 = bf16[4,512,1536]{2,1,0:T(8,128)(2,1)} custom-call(bf16[512,1536]{1,0:T(8,128)(2,1)} %pad_maximum_fusion.4.refs_0_), custom_call_target="tpu_custom_call" | custom-call | bytes 235929600 | tf_op jit(solution)/shard_map/chip_gather/pallas_call | solution.py:219
  138.4 32.5 %attn_forward.3 = (bf16[4,384,512]{2,1,0:T(8,128)(2,1)}, f32[384,1024]{1,0:T(8,128)}, bf16[384,256]{1,0:T(8,128)(2,1)}, bf16[384,512]{1,0:T(8,128)(2,1)}, f32[4,...) custom-call(bf16[4,96,512]{2,1,0:T(8,128)(2,1)} %bitcast.153, bf16[2048,1536]{1,0:T(8,128)(2,1)} %bitcast.144, ...), custom_call_target="tpu_custom_call" | custom-call | flops 2415919104 | bytes 6291456 | tf_op jit(solution)/shard_map/attn_forward/pallas_call | solution.py:845
  171.0 78.8 %all-gather.2.cloned.1.call-done.refs_3_.refs_2_.refs_8_.refs_6_.refs_7_ = bf16[2048,4608]{1,0:T(8,128)(2,1)} async-done(((bf16[512,4608]{1,0:T(8,128)(2,1)}), bf16[2048,4608]{1,0:T(8,128)(2,1)}) %all-gather.2.cloned.1.call-update) | async-done | bytes 18874384 | tf_op jit(solution)/shard_map/all_gather | solution.py:1072
  249.8 47.0 %ffn_forward.3 = (bf16[2048,384]{1,0:T(8,128)(2,1)}, f32[384,3072]{1,0:T(8,128)}, bf16[384,1536]{1,0:T(8,128)(2,1)}, bf16[4,96,512]{2,1,0:T(8,128)(2,1)}, bf16[4...) custom-call(bf16[4,384,512]{2,1,0:T(8,128)(2,1)} %get-tuple-element.94.refs_0_, ...), custom_call_target="tpu_custom_call" | custom-call | flops 7247757312 | bytes 18874368 | tf_op jit(solution)/shard_map/ffn_forward/pallas_call | solution.py:882
  297.6 33.5 %attn_forward.4 = (bf16[4,384,512]{2,1,0:T(8,128)(2,1)}, f32[384,1024]{1,0:T(8,128)}, bf16[384,256]{1,0:T(8,128)(2,1)}, bf16[384,512]{1,0:T(8,128)(2,1)}, f32[4,...) custom-call(bf16[4,96,512]{2,1,0:T(8,128)(2,1)} %bitcast_select_fusion.1.refs_0_.refs_4_.refs_5_.refs_2_.refs_3_, ...), custom_call_target="tpu_custom_call" | custom-call | flops 2415919104 | bytes 6291456 | tf_op jit(solution)/shard_map/attn_forward/pallas_call | solution.py:845
  331.1 33.1 %ffn_forward.4 = (bf16[2048,384]{1,0:T(8,128)(2,1)}, f32[384,3072]{1,0:T(8,128)}, bf16[384,1536]{1,0:T(8,128)(2,1)}, bf16[4,96,512]{2,1,0:T(8,128)(2,1)}) custom-call(bf16[4,96,512]{2,1,0:T(8,128)(2,1)} %get-tuple-element.100.refs_0_, f32[4,96,512]{2,1,0:T(8,128)} %get-tuple-element.101.refs_1_.refs_4_.refs_5_.refs_3_, ...), custom_call_target="tpu_custom_call" | custom-call | flops 7247757312 | bytes 18874368 | tf_op jit(solution)/shard_map/ffn_forward/pallas_call | solution.py:882
  364.2 42.1 %ffn_backward.3 = (bf16[4,384,512]{2,1,0:T(8,128)(2,1)}, bf16[384,3072]{1,0:T(8,128)(2,1)}, f32[4,96,512]{2,1,0:T(8,128)}, bf16[4,96,512]{2,1,0:T(8,128)(2,1)}, ...) custom-call(bf16[384,1536]{1,0:T(8,128)(2,1)} %get-tuple-element.103.refs_0_, ...), custom_call_target="tpu_custom_call" | custom-call | flops 7247757312 | bytes 18874368 | tf_op jit(solution)/shard_map/ffn_backward/pallas_call | solution.py:914
  407.1 35.7 %attn_backward.3 = (bf16[4,384,512]{2,1,0:T(8,128)(2,1)}, bf16[384,1024]{1,0:T(8,128)(2,1)}, bf16[4,96,512]{2,1,0:T(8,128)(2,1)}, f32[4,512]{1,0:T(4,128)}, f32[...) custom-call(bf16[384,1536]{1,0:T(8,128)(2,1)} %get-tuple-element.103.refs_0_, ...), custom_call_target="tpu_custom_call" | custom-call | flops 2415919104 | bytes 6291456 | tf_op jit(solution)/shard_map/attn_backward/pallas_call | solution.py:951
  442.8 43.3 %attn_forward.5 = (bf16[4,384,512]{2,1,0:T(8,128)(2,1)}, f32[384,1024]{1,0:T(8,128)}, bf16[384,256]{1,0:T(8,128)(2,1)}, bf16[384,512]{1,0:T(8,128)(2,1)}, f32[4,...) custom-call(bf16[384,1536]{1,0:T(8,128)(2,1)} %get-tuple-element.103., ...), custom_call_target="tpu_custom_call" | custom-call | flops 2415919104 | bytes 6291456 | tf_op jit(solution)/shard_map/attn_forward/pallas_call | solution.py:845
  486.1 34.6 %ffn_forward.5 = (bf16[2048,384]{1,0:T(8,128)(2,1)}, f32[384,3072]{1,0:T(8,128)}, bf16[384,1536]{1,0:T(8,128)(2,1)}, bf16[4,96,512]{2,1,0:T(8,128)(2,1)}, bf16[4...) custom-call(bf16[384,1536]{1,0:T(8,128)(2,1)} %get-tuple-element.103.refs_0_, ...), custom_call_target="tpu_custom_call" | custom-call | flops 7247757312 | bytes 18874368 | tf_op jit(solution)/shard_map/ffn_forward/pallas_call | solution.py:882
  521.5 34.0 %ffn_backward.4 = (bf16[4,384,512]{2,1,0:T(8,128)(2,1)}, bf16[384,3072]{1,0:T(8,128)(2,1)}, f32[4,96,512]{2,1,0:T(8,128)}, bf16[4,96,512]{2,1,0:T(8,128)(2,1)}, ...) custom-call(bf16[384,1536]{1,0:T(8,128)(2,1)} %get-tuple-element.104.refs_1_.refs_0_, ...), custom_call_target="tpu_custom_call" | custom-call | flops 7247757312 | bytes 18874368 | tf_op jit(solution)/shard_map/ffn_backward/pallas_call | solution.py:914
  555.5 57.3 %attn_backward.4 = (bf16[4,384,512]{2,1,0:T(8,128)(2,1)}, bf16[384,1024]{1,0:T(8,128)(2,1)}, bf16[4,96,512]{2,1,0:T(8,128)(2,1)}, f32[4,512]{1,0:T(4,128)}, f32[...) custom-call(bf16[384,1536]{1,0:T(8,128)(2,1)} %get-tuple-element.104.r, ...), custom_call_target="tpu_custom_call" | custom-call | flops 2415919104 | bytes 6291456 | tf_op jit(solution)/shard_map/attn_backward/pallas_call | solution.py:951
  614.6 40.5 %ffn_backward.5 = (bf16[4,384,512]{2,1,0:T(8,128)(2,1)}, bf16[384,3072]{1,0:T(8,128)(2,1)}, f32[4,96,512]{2,1,0:T(8,128)}, bf16[4,96,512]{2,1,0:T(8,128)(2,1)}, ...) custom-call(bf16[384,1024]{1,0:T(8,128)(2,1)} %get-tuple-element.131.refs_0_.refs_1_, ...), custom_call_target="tpu_custom_call" | custom-call | flops 7247757312 | bytes 18874368 | tf_op jit(solution)/shard_map/ffn_backward/pallas_call | solution.py:914
  655.1 16.0 %weight_grad.1 = bf16[2048,3072]{1,0:T(8,128)(2,1)} custom-call(bf16[2048,384]{1,0:T(8,128)(2,1)} %get-tuple-element.135.refs_0_, bf16[2048,384]{1,0:T(8,128)(2,1)} %get-tuple-element.136.refs_1_, bf16[2048,384]{1,0:T(8,128)(2,1)} %get-tuple-element.137.refs_2_, bf16[384,3072]{1,0:T(8,128)(2,1)} %get-tuple-element.138.refs_3_, ...), custom_call_target="tpu_custom_call" | custom-call | flops 9663676416 | bytes 12582912 | tf_op jit(solution)/shard_map/weight_grad/pallas_call | solution.py:990
  686.1 38.2 %attn_backward.5 = (bf16[4,384,512]{2,1,0:T(8,128)(2,1)}, bf16[384,1024]{1,0:T(8,128)(2,1)}, bf16[4,96,512]{2,1,0:T(8,128)(2,1)}, f32[4,512]{1,0:T(4,128)}, f32[8,128]{1,0:T(8,128)}) custom-call(bf16[4,96,512]{2,1,0:T(8,128)(2,1)} %get-tuple-element.141.refs_0_, f32[4,96,512]{2,1,0:T(8,128)} %get-tuple-element.142.refs_1_, ...), custom_call_target="tpu_custom_call" | custom-call | flops 2415919104 | bytes 6291456 | tf_op jit(solution)/shard_map/attn_backward/pallas_call | solution.py:951
  726.3 52.2 %chip_gather.3 = bf16[4,384,1024]{2,1,0:T(8,128)(2,1)} custom-call(bf16[384,1024]{1,0:T(8,128)(2,1)} %get-tuple-element.157.refs_0_, bf16[384,1024]{1,0:T(8,128)(2,1)} %get-tuple-element.131.refs_0_.refs_1_), custom_call_target="tpu_custom_call" | custom-call | bytes 117964800 | tf_op jit(solution)/shard_map/chip_gather/pallas_call | solution.py:219
  778.6 3.1 fusion.17
  787.8 2.1 bitcast_add_fusion
  802.1 2.1 maximum_bitcast_fusion.5
  808.7 2.1 maximum_bitcast_fusion.6
  810.7 2.1 collective-permute-done.6
  814.0 3.8 broadcast_select_fusion.7
  817.8 3.5 select_bitcast_fusion.1
  821.3 2.0 reduce-scatter.2.cloned.1.call-done
  823.3 3.4 broadcast_select_fusion.2
  827.0 2.4 copy.62
  837.8 2.0 select_convert_fusion.1
  840.2 1.9 maximum_bitcast_fusion.1
  842.2 1.9 maximum_bitcast_fusion
  (222 shorter events, 73.1 us)
Async XLA Ops:
  7.2 242.6 %all-gather.2.cloned.1.call-start = ((), (), s32[]{:S(2)}) async-start(), calls=%async_computation.1 | async-start | bytes 23592960 | tf_op jit(solution)/shard_map/all_gather | solution.py:1072
  13.0 7.3 collective-permute-start.1
  15.8 2.9 collective-permute-start
  24.9 798.4 %reduce-scatter.2.cloned.1.call-start = ((), (), s32[]{:S(2)}) async-start(), calls=%async_computation.2 | async-start | bytes 15728640 | tf_op jit(solution)/shard_map/reduce_scatter | solution.py:1228
  25.6 6.2 collective-permute-start.2
  486.1 34.6 %copy-start.32 = (bf16[4,96,512]{2,1,0:T(8,128)(2,1)S(1)}, bf16[4,96,512]{2,1,0:T(8,128)(2,1)}, u32[]{:S(2)}) copy-start(bf16[4,96,512]{2,1,0:T(8,128)(2,1)} %get-tuple-element.121) | copy-start | bytes 1179652
  686.0 131.7 %collective-permute-start.9 = (f32[256,1536]{1,0:T(8,128)}, f32[256,1536]{1,0:T(8,128)}, u32[]{:S(2)}, u32[]{:S(2)}) collective-permute-start(f32[256,1536]{1,0:T(8,128)} %slice_select_fusion), channel_id=1, source_target_pairs={{0,2},{2,0},{4,6},{6,4},{8,10},{10,8},{12,14},{14,12},{1,3},{3,1},... | collective-permute-start | bytes 4718600 | tf_op jit(solution)/shard_map/ppermute | solution.py:1049
  686.1 38.3 %copy-start.38 = (f32[4,512]{1,0:T(4,128)S(1)}, f32[4,512]{1,0:T(4,128)}, u32[]{:S(2)}) copy-start(f32[4,512]{1,0:T(4,128)} %get-tuple-element.144) | copy-start | bytes 24580
  686.1 38.3 %copy-start.40 = (f32[4,512]{1,0:T(4,128)S(1)}, f32[4,512]{1,0:T(4,128)}, u32[]{:S(2)}) copy-start(f32[4,512]{1,0:T(4,128)} %get-tuple-element.145) | copy-start | bytes 24580
  686.1 39.0 %copy-start.43 = (f32[8,128]{1,0:T(8,128)S(1)}, f32[8,128]{1,0:T(8,128)}, u32[]{:S(2)}) copy-start(f32[8,128]{1,0:T(8,128)} %get-tuple-element.150) | copy-start | bytes 12292
  686.1 39.0 %copy-start.44 = (f32[8,128]{1,0:T(8,128)S(1)}, f32[8,128]{1,0:T(8,128)}, u32[]{:S(2)}) copy-start(f32[8,128]{1,0:T(8,128)} %get-tuple-element.151) | copy-start | bytes 12292
  725.7 66.4 %copy-start.34 = (f32[128]{0:T(128)}, f32[128]{0:T(128)S(1)}, u32[]{:S(2)}) copy-start(f32[128]{0:T(128)S(1)} %get-tuple-element.257) | copy-start | bytes 1540
  725.7 66.4 %copy-start.35 = (f32[128]{0:T(128)}, f32[128]{0:T(128)S(1)}, u32[]{:S(2)}) copy-start(f32[128]{0:T(128)S(1)} %get-tuple-element.258) | copy-start | bytes 1540
  725.8 66.4 %collective-permute-start.3 = (f32[34,128]{1,0:T(8,128)S(1)}, f32[34,128]{1,0:T(8,128)S(1)}, u32[]{:S(2)}, u32[]{:S(2)}) collective-permute-start(f32[34,128]{1,0:T(8,128)S(1)} %maximum_bitcast_fusion.11), channel_id=1, source_target_pairs={{0,2},{2,0},{4,6},{6,4},{8,10},{10,8},{12,14},{14,12},{1,3},{3,1},... | collective-permute-start | bytes 52232 | tf_op jit(solution)/shard_map/ppermute | solution.py:1049
  726.3 52.2 %copy-start.17 = (bf16[4,384,512]{2,1,0:T(8,128)(2,1)S(1)}, bf16[4,384,512]{2,1,0:T(8,128)(2,1)}, u32[]{:S(2)}) copy-start(bf16[4,384,512]{2,1,0:T(8,128)(2,1)} %get-tuple-element.159) | copy-start | bytes 4718596
  778.6 3.1 copy-start.18
  778.6 3.1 copy-start.49
  778.6 3.3 copy-start.50
  784.7 3.1 copy-start.19
  791.3 3.2 copy-start.12
  791.3 3.2 copy-start.30
  791.3 3.2 copy-start.31
  791.3 22.7 %collective-permute-start.7 = (f32[256,1536]{1,0:T(8,128)}, f32[256,1536]{1,0:T(8,128)}, u32[]{:S(2)}, u32[]{:S(2)}) collective-permute-start(f32[256,1536]{1,0:T(8,128)} %broadcast_select_fusion.8), channel_id=1, source_target_pairs={{0,2},{2,0},{4,6},{6,4},{8,10},{10,8},{12,14},{14,12},{1,3},{3,1},... | collective-permute-start | bytes 4718600 | tf_op jit(solution)/shard_map/ppermute | solution.py:1049
  792.2 3.3 copy-start.33
  792.8 6.4 collective-permute-start.4
  799.2 5.0 copy-start.14
  800.6 7.3 collective-permute-start.5
  808.7 4.2 collective-permute-start.6
  814.0 3.8 copy-start.1
  823.3 3.4 copy-start.6
  823.3 3.4 copy-start.7
  826.7 10.5 %collective-permute-start.8 = (bf16[256,3072]{1,0:T(8,128)(2,1)}, bf16[256,3072]{1,0:T(8,128)(2,1)}, u32[]{:S(2)}, u32[]{:S(2)}) collective-permute-start(bf16[256,3072]{1,0:T(8,128)(2,1)} %broadcast_select_fusion.2), channel_id=1, source_target_pairs={{0,2},{2,0},{4,6},{6,4},{8,10},{10,8},{12,14},{14,12},{1,3},{3,1},... | collective-permute-start | bytes 4718600 | tf_op jit(solution)/shard_map/ppermute | solution.py:1049
  (34 other events, 62.6 us)
Sparse Core Ops, SparseCore 0:
  25.1 224.7 all-gather.1
  671.3 151.9 reduce-scatter.1

commit v5 on v4

--- a/solution.py
+++ b/solution.py
@@ -193,11 +193,12 @@
             for index, ((first, count), target) in enumerate(zip(spans, targets))
         ]
 
-        self.late = sum(s.size for s in targets) > background_size
+        long = sum(target.size for target in targets) > background_size
+        self.late = [long and index > 0 for index in range(len(targets))]
 
     def pass_on(self, late):
-        if late == self.late:
-            for gather in self.gathers:
+        for gather, when in zip(self.gathers, self.late):
+            if when == late:
                 gather.pass_on()
 
     def finish(self):
@@ -230,6 +231,80 @@
         cost_estimate=cost(0, 300 * blocks[0].size),
         name="chip_gather",
     )(*blocks)
+
+
+def core_swap_kernel(rows, out, send_sems, recv_sems):
+    exchange = Exchange(send_sems, recv_sems)
+    exchange.meet([exchange.core])
+    side = out.shape[0]
+    theirs = pl.multiple_of((1 - lax.axis_index("dp") % 2) * side, side)
+    copy = exchange.copy(rows.at[pl.ds(theirs, side)], out, exchange.core, 0, 0)
+    copy.start()
+    copy.wait()
+
+
+def core_swap(rows, number):
+    side = rows.shape[0] // 2
+    return pl.pallas_call(
+        core_swap_kernel,
+        in_specs=[HBM_SPEC],
+        out_specs=HBM_SPEC,
+        out_shape=shape((side, rows.shape[1]), rows.dtype),
+        scratch_shapes=[pltpu.SemaphoreType.DMA((1, 1)), pltpu.SemaphoreType.DMA((1, 1))],
+        compiler_params=params(number),
+        cost_estimate=cost(0, 10 * rows.size),
+        name="core_swap",
+    )(rows)
+
+
+def place_kernel(wide, *refs):
+    rows, other, refs = refs[0], refs[1], refs[2:]
+    outs, (mine, theirs, *staged, local_sems) = refs[: len(wide)], refs[len(wide) :]
+    local = Local(local_sems)
+    core = lax.axis_index("dp") % 2
+    side = other.shape[0]
+    loads = [
+        local.load(rows.at[pl.ds(pl.multiple_of(core * side, side), side)], mine),
+        local.load(other, theirs),
+    ]
+    for load in loads:
+        load.wait()
+    for index, (source, place) in enumerate(((mine, core), (theirs, 1 - core))):
+        first = 0
+        for number, ((width, turned), out) in enumerate(zip(wide, outs)):
+            stage = staged[number].at[index]
+            block = source[:, first : first + width].astype(f32)
+            at = pl.ds(pl.multiple_of(place * width, width), width)
+            if turned:
+                staged[number][index] = block.T
+                local.save(stage, out.at[at, :])
+            else:
+                staged[number][index] = block
+                local.save(stage, out.at[:, at])
+            first += width
+    local.finish()
+
+
+def place_parts(rows, other, wide):
+    side = other.shape[0]
+    return pl.pallas_call(
+        functools.partial(place_kernel, wide),
+        in_specs=[HBM_SPEC] * 2,
+        out_specs=[HBM_SPEC] * len(wide),
+        out_shape=[
+            shape((2 * width, side) if turned else (side, 2 * width), f32)
+            for width, turned in wide
+        ],
+        scratch_shapes=[pltpu.VMEM(other.shape, other.dtype)] * 2
+        + [
+            pltpu.VMEM((2, width, side) if turned else (2, side, width), f32)
+            for width, turned in wide
+        ]
+        + [pltpu.SemaphoreType.DMA((2 + 2 * len(wide),))],
+        compiler_params=params(),
+        cost_estimate=cost(0, 12 * other.size),
+        name="place",
+    )(rows, other)
 
 
 def load_pack(pack, held, local):
@@ -354,19 +429,24 @@
     if carry:
         carried, refs = refs[0], refs[1:]
     (
-        hidden, pack, model_gains, gains, tables_in, masks_in,
+        hidden_in, pack, model_gains_in, gains_in, tables_in, masks_in,
         moved_out, projected_out, values_out, attended_out, mixed_out, normed_ffn_rows,
     ), refs = refs[:12], refs[12:]
     if carry:
         arrived, refs = refs[0], refs[1:]
     targets, refs = refs[: len(spans)], refs[len(spans) :]
     (
-        tables, masks, normed, moved, projected, values, attended, mixed,
+        hidden, model_gains, gains, tables, masks, normed, moved, projected, values, attended, mixed,
         held, keep, send_core, recv_core, send_half, recv_half, local_sems, send_sems, recv_sems,
     ) = refs
     exchange, local = Exchange(send_sems, recv_sems), Local(local_sems)
+    first = [
+        local.load(hidden_in, hidden),
+        local.load(model_gains_in, model_gains),
+        local.load(gains_in, gains),
+    ]
+    loads = load_pack(pack, held, local)
     exchange.greet(carry, (3 if spread else 2 if spans else 0))
-    loads = load_pack(pack, held, local)
     background = Background(exchange, local, spans, sources, targets)
     extra = [local.load(tables_in, tables), local.load(masks_in, masks)]
     chunks, own, cols = hidden.shape
@@ -375,6 +455,8 @@
     kv_width = q_width // 2
     kv_heads = kv_width // width
     group = q_width // kv_width
+    for load in first:
+        load.wait()
     rows = hidden[...].astype(f32)
     inverse = lax.rsqrt(row_mean(rows * rows) + norm_eps)
     for c in range(chunks):
@@ -463,15 +545,16 @@
         held, keep, send_core, recv_core, send_half, recv_half, local_sems, send_sems, recv_sems,
     ) = rest
     exchange, local = Exchange(send_sems, recv_sems), Local(local_sems)
+    own = rows.shape[1]
+    first = local.load(rows, normed.at[:, pl.ds(0, own)])
+    loads = load_pack(pack, held, local)
     exchange.greet(hop, 3 if spread else 2 if spans else 0)
-    loads = load_pack(pack, held, local)
     moving = Spread(exchange, local, held_rows, moved) if spread else None
     background = Background(exchange, local, spans, sources, targets)
     mixed_load = local.load(mixed_in, mixed)
     chunks, own, cols = rows.shape
     units = activated.shape[1]
-    for c in range(chunks):
-        normed[c, :own] = rows[c]
+    first.wait()
 
     def project(c):
         loads[c].wait()
@@ -529,27 +612,29 @@
     if carry:
         carried, refs = refs[0], refs[1:]
     (
-        rows, mixed_a, mixed_b, gate_up_a, gate_up_b, pack, model_gains,
+        rows, mixed_a, mixed_b, gate_up_a, gate_up_b, pack, model_gains_in,
         moved_out, grads_out, grad_mixed, grad_proj_rows, gain_grad,
     ), refs = refs[:12], refs[12:]
     if carry:
         arrived, refs = refs[0], refs[1:]
     targets, refs = refs[: len(spans)], refs[len(spans) :]
     (
-        grad_down, moved, mixed, grads, pre, total,
+        model_gains, grad_down, moved, mixed, grads, pre, total,
         held, keep, send_core, recv_core, send_half, recv_half, local_sems, send_sems, recv_sems,
     ) = refs
     exchange, local = Exchange(send_sems, recv_sems), Local(local_sems)
-    exchange.greet(carry, 3 if spread else 0)
+    own = rows.shape[1]
+    first = local.load(rows, grad_down.at[:, pl.ds(0, own)])
+    gains_load = local.load(model_gains_in, model_gains)
     at_first = lax.axis_index("section") == 0
     loads = load_pack(pack, held, local)
+    exchange.greet(carry, 3 if spread else 0)
     background = Background(exchange, local, spans, sources, targets)
     pre_load = local.load_either(at_first, gate_up_a, gate_up_b, pre)
     mixed_load = local.load_either(at_first, mixed_a, mixed_b, mixed)
     chunks, own, cols = rows.shape
     units = grads.shape[1] // 2
-    for c in range(chunks):
-        grad_down[c, :own] = rows[c]
+    first.wait()
 
     def project(c):
         loads[c].wait()
@@ -599,7 +684,9 @@
         copies += moving.finish()
     local.save(moved, moved_out)
     mixed_load.wait()
-    norm_step(mixed[...], grad_mixed[...], model_gains, 1, rows, grad_mixed, gain_grad)
+    gains_load.wait()
+    base = grad_down[:, :own]
+    norm_step(mixed[...], grad_mixed[...], model_gains, 1, base, grad_mixed, gain_grad)
     for c in range(chunks):
         grad_proj_rows[c] = grad_mixed[c].astype(bf16)
     for copy in hops:
@@ -625,21 +712,28 @@
 ):
     sources, refs = refs[: 2 * len(spans)], refs[2 * len(spans) :]
     (
-        rows, grad_mixed, hidden_a, hidden_b, projected_a, projected_b, values_a, values_b,
-        pack, model_gains, gains, tables_in, masks_in,
+        rows, grad_mixed_in, hidden_a, hidden_b, projected_a, projected_b, values_a, values_b,
+        pack, model_gains_in, gains_in, tables_in, masks_in,
         moved_out, grads_out, grad_hidden, gain_grad, head_gain_grads, *rest
     ) = refs
     if hop:
         arrived, rest = rest[0], rest[1:]
     targets, rest = rest[: len(spans)], rest[len(spans) :]
     (
-        tables, masks, grad_proj, moved, grads, hidden, projected, values, total, summed_rows,
+        grad_mixed, model_gains, gains, tables, masks, grad_proj, moved, grads, hidden, projected, values, total, summed_rows,
         held, keep, send_core, recv_core, send_half, recv_half, local_sems, send_sems, recv_sems,
     ) = rest
     exchange, local = Exchange(send_sems, recv_sems), Local(local_sems)
-    exchange.greet(hop, 3 if spread else 0)
+    own = rows.shape[1]
+    first = local.load(rows, grad_proj.at[:, pl.ds(0, own)])
+    gain_loads = [
+        local.load(model_gains_in, model_gains),
+        local.load(gains_in, gains),
+        local.load(grad_mixed_in, grad_mixed),
+    ]
     at_first = lax.axis_index("section") == 0
     loads = load_pack(pack, held, local)
+    exchange.greet(hop, 3 if spread else 0)
     background = Background(exchange, local, spans, sources, targets)
     extra = [local.load(tables_in, tables), local.load(masks_in, masks)]
     projected_load = local.load_either(at_first, projected_a, projected_b, projected)
@@ -651,8 +745,7 @@
     kv_width = q_width // 2
     kv_heads = kv_width // width
     group = q_width // kv_width
-    for c in range(chunks):
-        grad_proj[c, :own] = rows[c]
+    first.wait()
 
     def project(c):
         loads[c].wait()
@@ -662,7 +755,7 @@
     moving = Spread(exchange, local, grad_proj, moved) if spread else None
     projected_load.wait()
     values_load.wait()
-    for load in extra:
+    for load in extra + gain_loads:
         load.wait()
     cos, sin = tables[0], tables[1]
     gain_q, gain_k = gains[0:1, :], gains[1:2, :]
@@ -805,7 +898,7 @@
         pltpu.VMEM((chunks, 2 * own, cols), bf16),
         pltpu.VMEM((chunks, own, cols), bf16),
         pltpu.VMEM((chunks, own, cols), bf16),
-        pltpu.SemaphoreType.DMA((16,)),
+        pltpu.SemaphoreType.DMA((20,)),
         pltpu.SemaphoreType.DMA((9, chunks)),
         pltpu.SemaphoreType.DMA((9, chunks)),
     ]
@@ -844,7 +937,7 @@
     rows = shape((chunks, own, cols), bf16)
     return pl.pallas_call(
         functools.partial(attn_forward_kernel, width, spread, hold, spans, carry),
-        in_specs=[HBM_SPEC] * (2 * len(spans) + carry) + [VMEM_SPEC, HBM_SPEC] + [VMEM_SPEC] * 2 + [HBM_SPEC] * 2,
+        in_specs=[HBM_SPEC] * (2 * len(spans) + carry) + [HBM_SPEC] * 6,
         out_specs=[HBM_SPEC] * 5 + [VMEM_SPEC] + [HBM_SPEC] * (carry + len(spans)),
         out_shape=[
             shape(moved, bf16),
@@ -857,6 +950,9 @@
         + [rows] * carry
         + gather_shapes(background),
         scratch_shapes=[
+            pltpu.VMEM(hidden.shape, bf16),
+            pltpu.VMEM(model_gains.shape, f32),
+            pltpu.VMEM(gains.shape, f32),
             pltpu.VMEM(tables.shape, f32),
             pltpu.VMEM(masks.shape, f32),
             pltpu.VMEM((chunks, tokens, cols), bf16),
@@ -881,7 +977,7 @@
     spans, spread = spans_of(background), held_rows is not None
     return pl.pallas_call(
         functools.partial(ffn_forward_kernel, hop, spread, spans),
-        in_specs=[HBM_SPEC] * (spread + 2 * len(spans)) + [VMEM_SPEC, HBM_SPEC, HBM_SPEC],
+        in_specs=[HBM_SPEC] * (spread + 2 * len(spans)) + [HBM_SPEC] * 3,
         out_specs=[HBM_SPEC] * 3 + [VMEM_SPEC] * (2 if hop else 1) + [HBM_SPEC] * (spread + len(spans)),
         out_shape=[
             shape((depth, tokens), bf16),
@@ -913,7 +1009,7 @@
     carry, spans = carried is not None, spans_of(background)
     return pl.pallas_call(
         functools.partial(ffn_backward_kernel, spread, spans, carry),
-        in_specs=[HBM_SPEC] * (2 * len(spans) + carry) + [VMEM_SPEC] + [HBM_SPEC] * 5 + [VMEM_SPEC],
+        in_specs=[HBM_SPEC] * (2 * len(spans) + carry) + [HBM_SPEC] * 7,
         out_specs=[HBM_SPEC] * 2 + [VMEM_SPEC] * 3 + [HBM_SPEC] * (carry + len(spans)),
         out_shape=[
             shape(moved, bf16),
@@ -925,6 +1021,7 @@
         + [shape((chunks, own, cols), bf16)] * carry
         + gather_shapes(background),
         scratch_shapes=[
+            pltpu.VMEM(model_gains.shape, f32),
             pltpu.VMEM((chunks, tokens, cols), bf16),
             pltpu.VMEM(moved, bf16),
             pltpu.VMEM((chunks, own, cols), f32),
@@ -950,7 +1047,7 @@
     spans = spans_of(background)
     return pl.pallas_call(
         functools.partial(attn_backward_kernel, width, spread, spans, hop),
-        in_specs=[HBM_SPEC] * (2 * len(spans)) + [VMEM_SPEC] * 2 + [HBM_SPEC] * 7 + [VMEM_SPEC] * 2 + [HBM_SPEC] * 2,
+        in_specs=[HBM_SPEC] * (2 * len(spans)) + [HBM_SPEC] * 13,
         out_specs=[HBM_SPEC] * 2 + [VMEM_SPEC] * (4 if hop else 3) + [HBM_SPEC] * len(spans),
         out_shape=[
             shape(moved, bf16),
@@ -962,6 +1059,9 @@
         + [shape((chunks, own, cols), bf16)] * (1 if hop else 0)
         + gather_shapes(background),
         scratch_shapes=[
+            pltpu.VMEM(grad_mixed.shape, f32),
+            pltpu.VMEM(model_gains.shape, f32),
+            pltpu.VMEM(gains.shape, f32),
             pltpu.VMEM(tables.shape, f32),
             pltpu.VMEM(masks.shape, f32),
             pltpu.VMEM((chunks, tokens, cols), bf16),
@@ -1202,7 +1302,9 @@
     late_pieces.append((side, pieces[:1]))
     attended_all.append(pieces[1:])
     early_block = attn_saves[1][1], attn_saves[0][1]
-    (proj_rows, *others), early_grads = back_ffn(2, grad_arrived, None, work((early_block, 0, tokens)))
+    (proj_rows, *others), early_grads = back_ffn(
+        2, grad_arrived, None, work((early_block, 0, side), (early_block, side, side))
+    )
     if square:
         ffn_partial = weight_grad([column(saves, 2)], [column(ffn_saves, 1)])
     else:
@@ -1257,24 +1359,23 @@
         def backward_rows(table, micro):
             return pick(table[micro + 1][0], table[micro][0])
 
-        down_sides = owned(
-            summed(backward_rows(ffn_saves, 0), active_pieces)
-            + summed(backward_rows(ffn_saves, 1), late_pieces)
+        down_rows = summed(backward_rows(ffn_saves, 0), active_pieces) + summed(
+            backward_rows(ffn_saves, 1), late_pieces
         )
         o_rows = sum(
             summed(backward_rows(attn_saves, micro), [(0, attended_all[micro])])
             for micro in range(2)
         )
-        qkv_rows = summed(forward_rows(0), [(0, early_grads)]) + summed(
+        early_pieces = [(0, early_grads[:1]), (side, early_grads[1:])]
+        qkv_rows = summed(forward_rows(0), early_pieces) + summed(
             forward_rows(1), [(0, [late_grads])]
         )
-        attn_sides = owned(jnp.concatenate([qkv_rows, o_rows], axis=1))
-        ffn_sides = owned(scattered(ffn_partial))
+        attn_rows = jnp.concatenate([qkv_rows, o_rows], axis=1)
+        ffn_rows = scattered(ffn_partial)
     else:
         attn_partial, ffn_rows = lax.optimization_barrier((attn_partial, scattered(ffn_partial)))
         ffn_sides = owned(ffn_rows)
         attn_sides = owned(scattered(attn_partial))
-        down_sides = [side[:, 2 * units :] for side in ffn_sides]
     q_width = q_weight.shape[2] // 2
     kv_width = k_weight.shape[2] // 2
 
@@ -1299,20 +1400,40 @@
         packed = packed + lax.ppermute(packed, "dp", [(i, i ^ reach) for i in range(n_dp)])
         reach *= 2
     packed = packed.reshape(-1)
+    gain_grads = (
+        packed[None, :depth],
+        packed[None, 2 * depth : 2 * depth + head_width],
+        packed[None, 2 * depth + head_width :],
+        packed[None, depth : 2 * depth],
+    )
+    if square:
+        attn_wide = ((q_width, False), (kv_width, False), (kv_width, False), (q_width, True))
+        attn_grads = place_parts(attn_rows, core_swap(attn_rows, numbers.of("core_swap", 0)), attn_wide)
+        down_swapped = core_swap(down_rows, numbers.of("core_swap", 1))
+        down_grads = place_parts(down_rows, down_swapped, ((units, True),))
+        others = (section_outputs, section_input_grads, gain_grads, attn_grads, down_grads)
+        others, ffn_rows = lax.optimization_barrier((others, ffn_rows))
+        section_outputs, section_input_grads, gain_grads, attn_grads, down_grads = others
+        ffn_swapped = core_swap(ffn_rows, numbers.of("core_swap", 2))
+        wide_grads = place_parts(ffn_rows, ffn_swapped, ((units, False), (units, False)))
+        weight_grads = [grad[None] for grad in (*attn_grads, *wide_grads, *down_grads)]
+    else:
+        weight_grads = [
+            across(attn_sides, 0, q_width),
+            across(attn_sides, q_width, kv_width),
+            across(attn_sides, q_width + kv_width, kv_width),
+            down(attn_sides, 2 * q_width),
+            across(ffn_sides, 0, units),
+            across(ffn_sides, units, units),
+            down(ffn_sides, 2 * units),
+        ]
     return (
         section_outputs,
         section_input_grads,
-        packed[None, :depth],
-        across(attn_sides, 0, q_width),
-        across(attn_sides, q_width, kv_width),
-        across(attn_sides, q_width + kv_width, kv_width),
-        down(attn_sides, 2 * q_width),
-        packed[None, 2 * depth : 2 * depth + head_width],
-        packed[None, 2 * depth + head_width :],
-        packed[None, depth : 2 * depth],
-        across(ffn_sides, 0, units),
-        across(ffn_sides, units, units),
-        down(down_sides, 0),
+        gain_grads[0],
+        *weight_grads[:4],
+        *gain_grads[1:],
+        *weight_grads[4:],
     )
 
 

time: 857 us -> 834 us (0.973)
  other arithmetic: 52.1 us -> 25.5 us
  Pallas kernels: 644 us -> 658 us
  local copies, waits for them, and re-layouts: 33.7 us -> 20.7 us
    pallas_call x0 -> x6, Pallas kernels: none -> 24.2 us  [the longest x3 12.8 us: place_parts(): pl.pallas_call(functools.partial(place_kernel, wide), in_specs=[HBM_SPEC]...]
    select_n x4 -> x0, other arithmetic: 10 us -> none  [the longest x3 6.24 us: owned(): other = to_core(jnp.where(first_core, rows[side:], rows[:side]))]
  transfers between devices with their start and end apart: 12 -> 9, of which waited for: 4 -> 5; matrix products, arithmetic and copies ran while one was open for 8% -> 5% of each run, Pallas kernels for 27% -> 29%
where the time goes in v5:
time: 834 us; the launch traced here: 828 us
  Pallas kernels  658 us (79%)
  waiting for transfers between devices  88 us (11%)
  other arithmetic  25.5 us (3%)
  local copies, waits for them, and re-layouts  20.7 us (2%)
  between operations  15.1 us (2%)
  matrix products  14.9 us (2%)
    pallas_call x2, Pallas kernels, chip_gather(): pl.pallas_call(chip_gather_kernel, in_specs=[HBM_SPEC] * len(blocks), out...  161 us
    pallas_call x3, Pallas kernels, attn_backward(): pl.pallas_call(functools.partial(attn_backward_kernel, width, spread, spa...  126 us
    pallas_call x3, Pallas kernels, ffn_backward(): pl.pallas_call(functools.partial(ffn_backward_kernel, spread, spans, carr...  113 us
    pallas_call x3, Pallas kernels, ffn_forward(): pl.pallas_call(functools.partial(ffn_forward_kernel, hop, spread, spans),...  112 us
    pallas_call x3, Pallas kernels, attn_forward(): pl.pallas_call(functools.partial(attn_forward_kernel, width, spread, hold...  105 us
    all_gather x1, waiting for transfers between devices, gathered(): lax.all_gather(block, 'dp', axis=0, tiled=True, axis_index_groups=chip_gr...  79.9 us
  transfers between devices with their start and end apart: 9, of which 5 were waited for; matrix products, arithmetic and copies ran while one was open for 5% of the time, Pallas kernels for 29%

profile of v5, /device:TPU:0, one launch (start us, length us, event | category | flops | bytes accessed | tf_op | source)
XLA Modules:
  0.0 828.5 jit_solution(1511820530427714861)
XLA Ops:
  15.9 2.8 collective-permute-done
  20.2 2.1 broadcast_select_fusion.1
  22.3 2.5 pad_maximum_fusion
  34.0 104.4 %chip_gather.2 = bf16[4,512,1536]{2,1,0:T(8,128)(2,1)} custom-call(bf16[512,1536]{1,0:T(8,128)(2,1)} %pad_maximum_fusion.4.refs_0_), custom_call_target="tpu_custom_call" | custom-call | bytes 235929600 | tf_op jit(solution)/shard_map/chip_gather/pallas_call | solution.py:220
  138.4 31.5 %attn_forward.3 = (bf16[4,384,512]{2,1,0:T(8,128)(2,1)}, f32[384,1024]{1,0:T(8,128)}, bf16[384,256]{1,0:T(8,128)(2,1)}, bf16[384,512]{1,0:T(8,128)(2,1)}, f32[4,...) custom-call(bf16[4,96,512]{2,1,0:T(8,128)(2,1)} %bitcast.144, bf16[2048,1536]{1,0:T(8,128)(2,1)} %bitcast.134, ...), custom_call_target="tpu_custom_call" | custom-call | flops 2415919104 | bytes 6291456 | tf_op jit(solution)/shard_map/attn_forward/pallas_call | solution.py:938
  169.9 79.9 %all-gather.2.cloned.1.call-done.refs_3_.refs_2_.refs_8_.refs_6_.refs_7_.refs_9_ = bf16[2048,4608]{1,0:T(8,128)(2,1)} async-done(((bf16[512,4608]{1,0:T(8,128)(2,1)}), bf16[2048,4608]{1,0:T(8,128)(2,1)}) %all-gather.2.cloned.1.call-update) | async-done | bytes 18874384 | tf_op jit(solution)/shard_map/all_gather | solution.py:1172
  249.8 46.0 %ffn_forward.3 = (bf16[2048,384]{1,0:T(8,128)(2,1)}, f32[384,3072]{1,0:T(8,128)}, bf16[384,1536]{1,0:T(8,128)(2,1)}, bf16[4,96,512]{2,1,0:T(8,128)(2,1)}, bf16[4...) custom-call(bf16[4,384,512]{2,1,0:T(8,128)(2,1)} %get-tuple-element.113.refs_0_, ...), custom_call_target="tpu_custom_call" | custom-call | flops 7247757312 | bytes 18874368 | tf_op jit(solution)/shard_map/ffn_forward/pallas_call | solution.py:978
  296.6 32.3 %attn_forward.4 = (bf16[4,384,512]{2,1,0:T(8,128)(2,1)}, f32[384,1024]{1,0:T(8,128)}, bf16[384,256]{1,0:T(8,128)(2,1)}, bf16[384,512]{1,0:T(8,128)(2,1)}, f32[4,...) custom-call(bf16[4,96,512]{2,1,0:T(8,128)(2,1)} %bitcast_select_fusion.1.refs_0_.refs_4_.refs_5_.refs_2_.refs_3_, ...), custom_call_target="tpu_custom_call" | custom-call | flops 2415919104 | bytes 6291456 | tf_op jit(solution)/shard_map/attn_forward/pallas_call | solution.py:938
  328.9 32.5 %ffn_forward.4 = (bf16[2048,384]{1,0:T(8,128)(2,1)}, f32[384,3072]{1,0:T(8,128)}, bf16[384,1536]{1,0:T(8,128)(2,1)}, bf16[4,96,512]{2,1,0:T(8,128)(2,1)}) custom-call(bf16[4,96,512]{2,1,0:T(8,128)(2,1)} %get-tuple-element.119.refs_0_, f32[4,96,512]{2,1,0:T(8,128)} %get-tuple-element.120.refs_1_.refs_4_.refs_5_.refs_6_, ...), custom_call_target="tpu_custom_call" | custom-call | flops 7247757312 | bytes 18874368 | tf_op jit(solution)/shard_map/ffn_forward/pallas_call | solution.py:978
  361.4 41.3 %ffn_backward.3 = (bf16[4,384,512]{2,1,0:T(8,128)(2,1)}, bf16[384,3072]{1,0:T(8,128)(2,1)}, f32[4,96,512]{2,1,0:T(8,128)}, bf16[4,96,512]{2,1,0:T(8,128)(2,1)}, ...) custom-call(bf16[384,1536]{1,0:T(8,128)(2,1)} %get-tuple-element.122.refs_0_, ...), custom_call_target="tpu_custom_call" | custom-call | flops 7247757312 | bytes 18874368 | tf_op jit(solution)/shard_map/ffn_backward/pallas_call | solution.py:1010
  403.5 34.5 %attn_backward.3 = (bf16[4,384,512]{2,1,0:T(8,128)(2,1)}, bf16[384,1024]{1,0:T(8,128)(2,1)}, bf16[4,96,512]{2,1,0:T(8,128)(2,1)}, f32[4,512]{1,0:T(4,128)}, f32[...) custom-call(bf16[384,1536]{1,0:T(8,128)(2,1)} %get-tuple-element.122.refs_0_, ...), custom_call_target="tpu_custom_call" | custom-call | flops 2415919104 | bytes 6291456 | tf_op jit(solution)/shard_map/attn_backward/pallas_call | solution.py:1048
  438.0 41.8 %attn_forward.5 = (bf16[4,384,512]{2,1,0:T(8,128)(2,1)}, f32[384,1024]{1,0:T(8,128)}, bf16[384,256]{1,0:T(8,128)(2,1)}, bf16[384,512]{1,0:T(8,128)(2,1)}, f32[4,...) custom-call(bf16[384,1536]{1,0:T(8,128)(2,1)} %get-tuple-element.122., ...), custom_call_target="tpu_custom_call" | custom-call | flops 2415919104 | bytes 6291456 | tf_op jit(solution)/shard_map/attn_forward/pallas_call | solution.py:938
  479.8 33.7 %ffn_forward.5 = (bf16[2048,384]{1,0:T(8,128)(2,1)}, f32[384,3072]{1,0:T(8,128)}, bf16[384,1536]{1,0:T(8,128)(2,1)}, bf16[4,96,512]{2,1,0:T(8,128)(2,1)}, bf16[4...) custom-call(bf16[384,1536]{1,0:T(8,128)(2,1)} %get-tuple-element.122.refs_0_, ...), custom_call_target="tpu_custom_call" | custom-call | flops 7247757312 | bytes 18874368 | tf_op jit(solution)/shard_map/ffn_forward/pallas_call | solution.py:978
  514.3 32.9 %ffn_backward.4 = (bf16[4,384,512]{2,1,0:T(8,128)(2,1)}, bf16[384,3072]{1,0:T(8,128)(2,1)}, f32[4,96,512]{2,1,0:T(8,128)}, bf16[4,96,512]{2,1,0:T(8,128)(2,1)}, ...) custom-call(bf16[384,1536]{1,0:T(8,128)(2,1)} %get-tuple-element.123.refs_1_.refs_0_, ...), custom_call_target="tpu_custom_call" | custom-call | flops 7247757312 | bytes 18874368 | tf_op jit(solution)/shard_map/ffn_backward/pallas_call | solution.py:1010
  547.3 56.1 %attn_backward.4 = (bf16[4,384,512]{2,1,0:T(8,128)(2,1)}, bf16[384,1024]{1,0:T(8,128)(2,1)}, bf16[4,96,512]{2,1,0:T(8,128)(2,1)}, f32[4,512]{1,0:T(4,128)}, f32[...) custom-call(bf16[384,1536]{1,0:T(8,128)(2,1)} %get-tuple-element.123.r, ...), custom_call_target="tpu_custom_call" | custom-call | flops 2415919104 | bytes 6291456 | tf_op jit(solution)/shard_map/attn_backward/pallas_call | solution.py:1048
  603.4 1.8 broadcast_select_fusion.11.refs_4_
  605.2 39.0 %ffn_backward.5 = (bf16[4,384,512]{2,1,0:T(8,128)(2,1)}, bf16[384,3072]{1,0:T(8,128)(2,1)}, f32[4,96,512]{2,1,0:T(8,128)}, bf16[4,96,512]{2,1,0:T(8,128)(2,1)}, ...) custom-call(bf16[384,1024]{1,0:T(8,128)(2,1)} %get-tuple-element.150.refs_0_.refs_2_.refs_1_, ...), custom_call_target="tpu_custom_call" | custom-call | flops 7247757312 | bytes 18874368 | tf_op jit(solution)/shard_map/ffn_backward/pallas_call | solution.py:1010
  644.2 15.8 %weight_grad.1 = bf16[2048,3072]{1,0:T(8,128)(2,1)} custom-call(bf16[2048,384]{1,0:T(8,128)(2,1)} %get-tuple-element.154.refs_0_, bf16[2048,384]{1,0:T(8,128)(2,1)} %get-tuple-element.155.refs_1_, bf16[2048,384]{1,0:T(8,128)(2,1)} %get-tuple-element.156.refs_2_, bf16[384,3072]{1,0:T(8,128)(2,1)} %get-tuple-element.157.refs_3_, ...), custom_call_target="tpu_custom_call" | custom-call | flops 9663676416 | bytes 12582912 | tf_op jit(solution)/shard_map/weight_grad/pallas_call | solution.py:1090
  660.7 35.4 %attn_backward.5 = (bf16[4,384,512]{2,1,0:T(8,128)(2,1)}, bf16[384,1024]{1,0:T(8,128)(2,1)}, bf16[4,96,512]{2,1,0:T(8,128)(2,1)}, f32[4,512]{1,0:T(4,128)}, f32[8,128]{1,0:T(8,128)}) custom-call(bf16[4,96,512]{2,1,0:T(8,128)(2,1)} %get-tuple-element.160.refs_0_, f32[4,96,512]{2,1,0:T(8,128)} %get-tuple-element.161.refs_1_, ...), custom_call_target="tpu_custom_call" | custom-call | flops 2415919104 | bytes 6291456 | tf_op jit(solution)/shard_map/attn_backward/pallas_call | solution.py:1048
  698.0 56.6 %chip_gather.3 = bf16[4,384,1024]{2,1,0:T(8,128)(2,1)} custom-call(bf16[384,1024]{1,0:T(8,128)(2,1)} %get-tuple-element.177.refs_0_, bf16[384,1024]{1,0:T(8,128)(2,1)} %get-tuple-element.150.refs_0_.refs_2_.refs_1_), custom_call_target="tpu_custom_call" | custom-call | bytes 117964800 | tf_op jit(solution)/shard_map/chip_gather/pallas_call | solution.py:220
  754.6 2.2 broadcast_select_fusion.3
  769.3 1.9 fusion.9
  772.2 1.9 pad_maximum_fusion.1.rows.refs_0_
  778.4 3.0 fusion.4.rows.refs_0_
  781.4 1.8 collective-permute-start.4
  792.1 3.8 core_swap.4.refs_1_
  795.9 4.2 place.4
  800.1 3.8 core_swap.3.refs_1_
  803.9 3.9 place.3
  808.9 4.0 reduce-scatter.2.cloned.1.call-done.rows.refs_0_
  812.9 3.8 core_swap.5.refs_1_
  816.7 4.7 place.5
  (184 shorter events, 51.7 us)
Async XLA Ops:
  7.2 242.6 %all-gather.2.cloned.1.call-start = ((), (), s32[]{:S(2)}) async-start(), calls=%async_computation.1 | async-start | bytes 23592960 | tf_op jit(solution)/shard_map/all_gather | solution.py:1172
  11.4 2.0 copy-start.18
  11.4 2.8 copy-start.17
  13.0 7.3 collective-permute-start.1
  15.6 3.1 copy-start.14
  15.8 2.9 collective-permute-start
  24.9 2.5 copy-start.24
  24.9 2.5 copy-start.25
  24.9 2.7 copy-start.15
  24.9 2.7 copy-start.16
  24.9 787.9 %reduce-scatter.2.cloned.1.call-start = ((), (), s32[]{:S(2)}) async-start(), calls=%async_computation.2 | async-start | bytes 15728640 | tf_op jit(solution)/shard_map/reduce_scatter | solution.py:1330
  25.5 6.2 collective-permute-start.2
  479.8 33.7 %copy-start.23 = (bf16[4,96,512]{2,1,0:T(8,128)(2,1)S(1)}, bf16[4,96,512]{2,1,0:T(8,128)(2,1)}, u32[]{:S(2)}) copy-start(bf16[4,96,512]{2,1,0:T(8,128)(2,1)} %get-tuple-element.140) | copy-start | bytes 1179652
  660.7 35.4 %copy-start.26 = (f32[4,512]{1,0:T(4,128)S(1)}, f32[4,512]{1,0:T(4,128)}, u32[]{:S(2)}) copy-start(f32[4,512]{1,0:T(4,128)} %get-tuple-element.163) | copy-start | bytes 24580
  660.7 35.4 %copy-start.28 = (f32[4,512]{1,0:T(4,128)S(1)}, f32[4,512]{1,0:T(4,128)}, u32[]{:S(2)}) copy-start(f32[4,512]{1,0:T(4,128)} %get-tuple-element.164) | copy-start | bytes 24580
  660.7 36.1 %copy-start.31 = (f32[8,128]{1,0:T(8,128)S(1)}, f32[8,128]{1,0:T(8,128)}, u32[]{:S(2)}) copy-start(f32[8,128]{1,0:T(8,128)} %get-tuple-element.169) | copy-start | bytes 12292
  660.7 36.1 %copy-start.32 = (f32[8,128]{1,0:T(8,128)S(1)}, f32[8,128]{1,0:T(8,128)}, u32[]{:S(2)}) copy-start(f32[8,128]{1,0:T(8,128)} %get-tuple-element.170) | copy-start | bytes 12292
  697.6 83.9 %collective-permute-start.3 = (f32[34,128]{1,0:T(8,128)S(1)}, f32[34,128]{1,0:T(8,128)S(1)}, u32[]{:S(2)}, u32[]{:S(2)}) collective-permute-start(f32[34,128]{1,0:T(8,128)S(1)} %maximum_bitcast_fusion.4), channel_id=1, source_target_pairs={{0,2},{2,0},{4,6},{6,4},{8,10},{10,8},{12,14},{14,12},{1,3},{3,1},... | collective-permute-start | bytes 52232 | tf_op jit(solution)/shard_map/ppermute | solution.py:1149
  698.0 56.6 %copy-start.12 = (bf16[4,384,512]{2,1,0:T(8,128)(2,1)S(1)}, bf16[4,384,512]{2,1,0:T(8,128)(2,1)}, u32[]{:S(2)}) copy-start(bf16[4,384,512]{2,1,0:T(8,128)(2,1)} %get-tuple-element.188) | copy-start | bytes 4718596
  754.6 2.3 copy-start.43
  762.7 2.4 copy-start.11
  767.0 2.4 copy-start.6
  772.2 2.7 copy-start.2
  778.3 3.0 copy-start.3
  778.3 3.0 copy-start.19
  778.3 3.0 copy-start.20
  781.3 1.9 copy-start.4
  781.3 1.9 copy-start.21
  781.3 1.9 copy-start.22
  781.4 3.8 collective-permute-start.4
  785.3 4.3 collective-permute-start.5
  789.6 18.2 %collective-permute-start.6 = (f32[34,128]{1,0:T(8,128)S(1)}, f32[34,128]{1,0:T(8,128)S(1)}, u32[]{:S(2)}, u32[]{:S(2)}) collective-permute-start(f32[34,128]{1,0:T(8,128)S(1)} %add.69), channel_id=1, source_target_pairs={{0,8},{2,10},{4,12},{6,14},{8,0},{10,2},{12,4},{14,6},{1,9},{3,11}... | collective-permute-start | bytes 52232 | tf_op jit(solution)/shard_map/ppermute | solution.py:1400
  (21 other events, 30.8 us)
Sparse Core Ops, SparseCore 0:
  25.0 224.6 all-gather.1
  660.1 152.7 reduce-scatter.1

commit v6 on v5

--- a/solution.py
+++ b/solution.py
@@ -75,7 +75,7 @@
         )
 
 
-def gather_then(exchange, rows, use):
+def gather_then(exchange, rows, use, arrivals=()):
     chunks, total, _ = rows.shape
     own = total // 4
     first = [
@@ -88,14 +88,20 @@
         )
         for c in range(chunks)
     ]
-    for c in range(chunks):
-        first[c].start()
-    for c in range(chunks):
-        first[c].wait_recv()
-        second[c].start()
-        if c > 0:
-            second[c - 1].wait_recv()
-            use(c - 1)
+    if not arrivals:
+        for c in range(chunks):
+            first[c].start()
+    for c in range(chunks + 1):
+        if arrivals and c < chunks:
+            arrivals[c].wait_recv()
+            first[c].start()
+        ready = c - 1 if arrivals else c
+        if 0 <= ready < chunks:
+            first[ready].wait_recv()
+            second[ready].start()
+            if ready > 0:
+                second[ready - 1].wait_recv()
+                use(ready - 1)
     second[chunks - 1].wait_recv()
     use(chunks - 1)
     return first + second
@@ -607,7 +613,7 @@
     local.finish()
 
 
-def ffn_backward_kernel(spread, spans, carry, *refs):
+def ffn_backward_kernel(spread, spans, carry, handed, *refs):
     sources, refs = refs[: 2 * len(spans)], refs[2 * len(spans) :]
     if carry:
         carried, refs = refs[0], refs[1:]
@@ -624,23 +630,34 @@
     ) = refs
     exchange, local = Exchange(send_sems, recv_sems), Local(local_sems)
     own = rows.shape[1]
-    first = local.load(rows, grad_down.at[:, pl.ds(0, own)])
+    first = None if handed else local.load(rows, grad_down.at[:, pl.ds(0, own)])
     gains_load = local.load(model_gains_in, model_gains)
     at_first = lax.axis_index("section") == 0
     loads = load_pack(pack, held, local)
-    exchange.greet(carry, 3 if spread else 0)
+    exchange.greet(carry or handed, 3 if spread else 0)
+    arrivals = []
+    if handed:
+        arrivals = [
+            exchange.copy(rows.at[c], grad_down.at[c, pl.ds(0, own)], exchange.section, 4, c)
+            for c in range(rows.shape[0])
+        ]
+        for copy in arrivals:
+            copy.start()
     background = Background(exchange, local, spans, sources, targets)
     pre_load = local.load_either(at_first, gate_up_a, gate_up_b, pre)
     mixed_load = local.load_either(at_first, mixed_a, mixed_b, mixed)
     chunks, own, cols = rows.shape
     units = grads.shape[1] // 2
-    first.wait()
+    if first is not None:
+        first.wait()
 
     def project(c):
         loads[c].wait()
         accumulate(total, grad_down[c], held, c * cols, 2 * units, units, c == 0)
 
-    copies = gather_then(exchange, grad_down, project)
+    copies = gather_then(exchange, grad_down, project, arrivals) + arrivals
+    if handed:
+        background.late = [False] * len(background.late)
     hops = []
     if carry:
         hops = [exchange.copy(carried, arrived, exchange.section, 4, 0)]
@@ -1002,13 +1019,13 @@
     )(*([held_rows] if spread else []), *sum([list(blocks) for blocks, *_ in background], []), rows, mixed, pack)
 
 
-def ffn_backward(rows, mixed, gate_up, pack, model_gains, spread, carried, background, numbers):
+def ffn_backward(rows, mixed, gate_up, pack, model_gains, spread, carried, handed, background, numbers):
     chunks, own, cols = rows.shape
     tokens, units = 4 * own, pack.shape[1] // 3
     moved = (chunks, tokens, cols) if spread else (chunks * cols, tokens)
     carry, spans = carried is not None, spans_of(background)
     return pl.pallas_call(
-        functools.partial(ffn_backward_kernel, spread, spans, carry),
+        functools.partial(ffn_backward_kernel, spread, spans, carry, handed),
         in_specs=[HBM_SPEC] * (2 * len(spans) + carry) + [HBM_SPEC] * 7,
         out_specs=[HBM_SPEC] * 2 + [VMEM_SPEC] * 3 + [HBM_SPEC] * (carry + len(spans)),
         out_shape=[
@@ -1031,7 +1048,7 @@
             pltpu.VMEM(pack.shape, bf16),
         ]
         + exchange_scratch(chunks, own, cols),
-        compiler_params=params(numbers.of("ffn_backward", carry, spans)),
+        compiler_params=params(numbers.of("ffn_backward", carry, handed, spans)),
         cost_estimate=cost(2 * tokens * pack.size, pack.size * 2),
         name="ffn_backward",
     )(*sum([list(blocks) for blocks, *_ in background], []), *([carried] if carry else []), rows, *mixed, *gate_up, pack, model_gains)
@@ -1246,10 +1263,10 @@
         return more + rest
 
     def back_ffn(step, arrived, carried=None, work=()):
-        rows = pick(arrived, cotangents[step] if step < 2 else zero_rows)
+        rows = pick(arrived, cotangents[step]) if step < 2 else arrived
         *_, mixed, gate_up = zip(backs[0], backs[2]) if step == 1 else zip(backs[1], backs[1])
         turned_rows, ffn_grads, grad_mixed, proj_rows, gain_grad, *more = ffn_backward(
-            rows, mixed, gate_up, ffn_pack, model_gains, square, carried, work, numbers
+            rows, mixed, gate_up, ffn_pack, model_gains, square, carried, step == 2, work, numbers
         )
         ffn_saves.append((turned_rows, ffn_grads))
         return (proj_rows, grad_mixed, gain_grad), more
@@ -1264,7 +1281,8 @@
         )
         attn_saves.append((turned_rows, attn_grads))
         grads.append(grad_hidden)
-        gains.append((attn_gain_grad, ffn_gain_grad, head_gain_grads))
+        step_gains = (attn_gain_grad, ffn_gain_grad, head_gain_grads)
+        gains.append(pick(step_gains, jax.tree.map(jnp.zeros_like, step_gains)) if step == 2 else step_gains)
         return rest
 
     def column(table, item):
@@ -1294,17 +1312,19 @@
     active, attended = of_micro(1, 3), of_micro(1, 1)
     side = tokens // 2
     grad_arrived, results[2] = lax.optimization_barrier((grad_arrived, results[2]))
-    others, pieces = back_ffn(1, grad_arrived, None, work((active, 0, side)))
+    first_side = side + part // 3
+    others, pieces = back_ffn(1, grad_arrived, None, work((active, 0, first_side)))
     late_pieces = [(0, pieces)]
-    grad_arrived, *pieces = back_attn(
-        1, *others, True, work((active, side, side), (attended, 0, tokens))
-    )
-    late_pieces.append((side, pieces[:1]))
-    attended_all.append(pieces[1:])
+    pieces = back_attn(
+        1, *others, False, work((active, first_side, tokens - first_side))
+    )
+    late_pieces.append((first_side, pieces[:1]))
     early_block = attn_saves[1][1], attn_saves[0][1]
-    (proj_rows, *others), early_grads = back_ffn(
-        2, grad_arrived, None, work((early_block, 0, side), (early_block, side, side))
-    )
+    (proj_rows, *others), pieces = back_ffn(
+        2, grads[1], None, work((attended, 0, tokens), (early_block, 0, tokens))
+    )
+    attended_all.append(pieces[:1])
+    early_grads = pieces[1:]
     if square:
         ffn_partial = weight_grad([column(saves, 2)], [column(ffn_saves, 1)])
     else:
@@ -1366,7 +1386,7 @@
             summed(backward_rows(attn_saves, micro), [(0, attended_all[micro])])
             for micro in range(2)
         )
-        early_pieces = [(0, early_grads[:1]), (side, early_grads[1:])]
+        early_pieces = [(0, early_grads)]
         qkv_rows = summed(forward_rows(0), early_pieces) + summed(
             forward_rows(1), [(0, [late_grads])]
         )

time: 834 us -> 829 us (level)
    pallas_call x3, Pallas kernels: 126 us -> 104 us  [attn_backward(): pl.pallas_call(functools.partial(attn_backward_kernel, width, spread, spa...]
    pallas_call x3, Pallas kernels: 113 us -> 131 us  [ffn_backward(): pl.pallas_call(functools.partial(ffn_backward_kernel, spread, spans, carr...]
  transfers between devices with their start and end apart: 9 -> 9, of which waited for: 5 -> 5; matrix products, arithmetic and copies ran while one was open for 5% -> 5% of each run, Pallas kernels for 29% -> 30%
where the time goes in v6:
time: 829 us; the launch traced here: 823 us
  Pallas kernels  654 us (79%)
  waiting for transfers between devices  91.6 us (11%)
  other arithmetic  23.6 us (3%)
  local copies, waits for them, and re-layouts  19.1 us (2%)
  matrix products  15.2 us (2%)
  between operations  15.1 us (2%)
    pallas_call x2, Pallas kernels, chip_gather(): pl.pallas_call(chip_gather_kernel, in_specs=[HBM_SPEC] * len(blocks), out...  161 us
    pallas_call x3, Pallas kernels, ffn_backward(): pl.pallas_call(functools.partial(ffn_backward_kernel, spread, spans, carr...  131 us
    pallas_call x3, Pallas kernels, ffn_forward(): pl.pallas_call(functools.partial(ffn_forward_kernel, hop, spread, spans),...  112 us
    pallas_call x3, Pallas kernels, attn_forward(): pl.pallas_call(functools.partial(attn_forward_kernel, width, spread, hold...  106 us
    pallas_call x3, Pallas kernels, attn_backward(): pl.pallas_call(functools.partial(attn_backward_kernel, width, spread, spa...  104 us
    all_gather x1, waiting for transfers between devices, gathered(): lax.all_gather(block, 'dp', axis=0, tiled=True, axis_index_groups=chip_gr...  79.9 us
  transfers between devices with their start and end apart: 9, of which 5 were waited for; matrix products, arithmetic and copies ran while one was open for 5% of the time, Pallas kernels for 30%

profile of v6, /device:TPU:0, one launch (start us, length us, event | category | flops | bytes accessed | tf_op | source)
XLA Modules:
  0.0 823.2 jit_solution(3321363802282562793)
XLA Ops:
  15.9 2.8 collective-permute-done
  20.2 2.1 broadcast_select_fusion.1
  22.3 2.5 pad_maximum_fusion
  34.0 104.4 %chip_gather.2 = bf16[4,512,1536]{2,1,0:T(8,128)(2,1)} custom-call(bf16[512,1536]{1,0:T(8,128)(2,1)} %pad_maximum_fusion.4.refs_0_), custom_call_target="tpu_custom_call" | custom-call | bytes 235929600 | tf_op jit(solution)/shard_map/chip_gather/pallas_call | solution.py:226
  138.4 31.5 %attn_forward.3 = (bf16[4,384,512]{2,1,0:T(8,128)(2,1)}, f32[384,1024]{1,0:T(8,128)}, bf16[384,256]{1,0:T(8,128)(2,1)}, bf16[384,512]{1,0:T(8,128)(2,1)}, f32[4,...) custom-call(bf16[4,96,512]{2,1,0:T(8,128)(2,1)} %bitcast.139, bf16[2048,1536]{1,0:T(8,128)(2,1)} %bitcast.129, ...), custom_call_target="tpu_custom_call" | custom-call | flops 2415919104 | bytes 6291456 | tf_op jit(solution)/shard_map/attn_forward/pallas_call | solution.py:955
  169.9 79.9 %all-gather.2.cloned.1.call-done.refs_3_.refs_2_.refs_8_.refs_6_.refs_7_.refs_9_ = bf16[2048,4608]{1,0:T(8,128)(2,1)} async-done(((bf16[512,4608]{1,0:T(8,128)(2,1)}), bf16[2048,4608]{1,0:T(8,128)(2,1)}) %all-gather.2.cloned.1.call-update) | async-done | bytes 18874384 | tf_op jit(solution)/shard_map/all_gather | solution.py:1189
  249.8 46.0 %ffn_forward.3 = (bf16[2048,384]{1,0:T(8,128)(2,1)}, f32[384,3072]{1,0:T(8,128)}, bf16[384,1536]{1,0:T(8,128)(2,1)}, bf16[4,96,512]{2,1,0:T(8,128)(2,1)}, bf16[4...) custom-call(bf16[4,384,512]{2,1,0:T(8,128)(2,1)} %get-tuple-element.111.refs_0_, ...), custom_call_target="tpu_custom_call" | custom-call | flops 7247757312 | bytes 18874368 | tf_op jit(solution)/shard_map/ffn_forward/pallas_call | solution.py:995
  296.6 32.3 %attn_forward.4 = (bf16[4,384,512]{2,1,0:T(8,128)(2,1)}, f32[384,1024]{1,0:T(8,128)}, bf16[384,256]{1,0:T(8,128)(2,1)}, bf16[384,512]{1,0:T(8,128)(2,1)}, f32[4,...) custom-call(bf16[4,96,512]{2,1,0:T(8,128)(2,1)} %bitcast_select_fusion.1.refs_0_.refs_4_.refs_5_.refs_2_.refs_3_, ...), custom_call_target="tpu_custom_call" | custom-call | flops 2415919104 | bytes 6291456 | tf_op jit(solution)/shard_map/attn_forward/pallas_call | solution.py:955
  328.9 32.5 %ffn_forward.4 = (bf16[2048,384]{1,0:T(8,128)(2,1)}, f32[384,3072]{1,0:T(8,128)}, bf16[384,1536]{1,0:T(8,128)(2,1)}, bf16[4,96,512]{2,1,0:T(8,128)(2,1)}) custom-call(bf16[4,96,512]{2,1,0:T(8,128)(2,1)} %get-tuple-element.117.refs_0_, f32[4,96,512]{2,1,0:T(8,128)} %get-tuple-element.118.refs_1_.refs_4_.refs_5_.refs_6_, ...), custom_call_target="tpu_custom_call" | custom-call | flops 7247757312 | bytes 18874368 | tf_op jit(solution)/shard_map/ffn_forward/pallas_call | solution.py:995
  361.4 41.4 %ffn_backward.3 = (bf16[4,384,512]{2,1,0:T(8,128)(2,1)}, bf16[384,3072]{1,0:T(8,128)(2,1)}, f32[4,96,512]{2,1,0:T(8,128)}, bf16[4,96,512]{2,1,0:T(8,128)(2,1)}, ...) custom-call(bf16[384,1536]{1,0:T(8,128)(2,1)} %get-tuple-element.120.refs_0_, ...), custom_call_target="tpu_custom_call" | custom-call | flops 7247757312 | bytes 18874368 | tf_op jit(solution)/shard_map/ffn_backward/pallas_call | solution.py:1027
  403.6 34.4 %attn_backward.3 = (bf16[4,384,512]{2,1,0:T(8,128)(2,1)}, bf16[384,1024]{1,0:T(8,128)(2,1)}, bf16[4,96,512]{2,1,0:T(8,128)(2,1)}, f32[4,512]{1,0:T(4,128)}, f32[...) custom-call(bf16[384,1536]{1,0:T(8,128)(2,1)} %get-tuple-element.120.refs_0_, ...), custom_call_target="tpu_custom_call" | custom-call | flops 2415919104 | bytes 6291456 | tf_op jit(solution)/shard_map/attn_backward/pallas_call | solution.py:1065
  438.0 41.8 %attn_forward.5 = (bf16[4,384,512]{2,1,0:T(8,128)(2,1)}, f32[384,1024]{1,0:T(8,128)}, bf16[384,256]{1,0:T(8,128)(2,1)}, bf16[384,512]{1,0:T(8,128)(2,1)}, f32[4,...) custom-call(bf16[384,1536]{1,0:T(8,128)(2,1)} %get-tuple-element.120., ...), custom_call_target="tpu_custom_call" | custom-call | flops 2415919104 | bytes 6291456 | tf_op jit(solution)/shard_map/attn_forward/pallas_call | solution.py:955
  479.8 33.7 %ffn_forward.5 = (bf16[2048,384]{1,0:T(8,128)(2,1)}, f32[384,3072]{1,0:T(8,128)}, bf16[384,1536]{1,0:T(8,128)(2,1)}, bf16[4,96,512]{2,1,0:T(8,128)(2,1)}, bf16[4...) custom-call(bf16[384,1536]{1,0:T(8,128)(2,1)} %get-tuple-element.120.refs_0_, ...), custom_call_target="tpu_custom_call" | custom-call | flops 7247757312 | bytes 18874368 | tf_op jit(solution)/shard_map/ffn_forward/pallas_call | solution.py:995
  514.3 35.5 %ffn_backward.4 = (bf16[4,384,512]{2,1,0:T(8,128)(2,1)}, bf16[384,3072]{1,0:T(8,128)(2,1)}, f32[4,96,512]{2,1,0:T(8,128)}, bf16[4,96,512]{2,1,0:T(8,128)(2,1)}, ...) custom-call(bf16[384,1536]{1,0:T(8,128)(2,1)} %get-tuple-element.121.refs_1_.refs_0_, ...), custom_call_target="tpu_custom_call" | custom-call | flops 7247757312 | bytes 18874368 | tf_op jit(solution)/shard_map/ffn_backward/pallas_call | solution.py:1027
  549.9 34.5 %attn_backward.4 = (bf16[4,384,512]{2,1,0:T(8,128)(2,1)}, bf16[384,1024]{1,0:T(8,128)(2,1)}, bf16[4,96,512]{2,1,0:T(8,128)(2,1)}, f32[4,512]{1,0:T(4,128)}, f32[...) custom-call(bf16[384,1536]{1,0:T(8,128)(2,1)} %get-tuple-element.121.refs_1_.refs_0_, ...), custom_call_target="tpu_custom_call" | custom-call | flops 2415919104 | bytes 6291456 | tf_op jit(solution)/shard_map/attn_backward/pallas_call | solution.py:1065
  584.3 54.0 %ffn_backward.5 = (bf16[4,384,512]{2,1,0:T(8,128)(2,1)}, bf16[384,3072]{1,0:T(8,128)(2,1)}, f32[4,96,512]{2,1,0:T(8,128)}, bf16[4,96,512]{2,1,0:T(8,128)(2,1)}, ...) custom-call(bf16[384,512]{1,0:T(8,128)(2,1)} %get-tuple-element.131.refs_3_.refs_0_, ...), custom_call_target="tpu_custom_call" | custom-call | flops 7247757312 | bytes 18874368 | tf_op jit(solution)/shard_map/ffn_backward/pallas_call | solution.py:1027
  638.3 15.7 %weight_grad.1 = bf16[2048,3072]{1,0:T(8,128)(2,1)} custom-call(bf16[2048,384]{1,0:T(8,128)(2,1)} %get-tuple-element.151.refs_0_, bf16[2048,384]{1,0:T(8,128)(2,1)} %get-tuple-element.152.refs_1_, bf16[2048,384]{1,0:T(8,128)(2,1)} %get-tuple-element.153.refs_2_, bf16[384,3072]{1,0:T(8,128)(2,1)} %get-tuple-element.154.refs_3_, ...), custom_call_target="tpu_custom_call" | custom-call | flops 9663676416 | bytes 12582912 | tf_op jit(solution)/shard_map/weight_grad/pallas_call | solution.py:1107
  654.8 35.6 %attn_backward.5 = (bf16[4,384,512]{2,1,0:T(8,128)(2,1)}, bf16[384,1024]{1,0:T(8,128)(2,1)}, bf16[4,96,512]{2,1,0:T(8,128)(2,1)}, f32[4,512]{1,0:T(4,128)}, f32[8,128]{1,0:T(8,128)}) custom-call(bf16[4,96,512]{2,1,0:T(8,128)(2,1)} %get-tuple-element.157.refs_0_, f32[4,96,512]{2,1,0:T(8,128)} %get-tuple-element.158.refs_1_, ...), custom_call_target="tpu_custom_call" | custom-call | flops 2415919104 | bytes 6291456 | tf_op jit(solution)/shard_map/attn_backward/pallas_call | solution.py:1065
  692.3 56.5 %chip_gather.3 = bf16[4,384,1024]{2,1,0:T(8,128)(2,1)} custom-call(bf16[384,1024]{1,0:T(8,128)(2,1)} %get-tuple-element.173.refs_0_, bf16[384,1024]{1,0:T(8,128)(2,1)} %get-tuple-element.148.refs_2_.refs_1_), custom_call_target="tpu_custom_call" | custom-call | bytes 117964800 | tf_op jit(solution)/shard_map/chip_gather/pallas_call | solution.py:226
  748.8 2.2 broadcast_select_fusion.3
  760.9 2.1 fusion.10
  763.2 1.8 bitcast_add_fusion
  765.1 1.9 pad_maximum_fusion.1.rows.refs_0_
  769.2 1.9 fusion.4
  771.1 3.0 fusion.3.rows.refs_0_
  784.4 3.8 core_swap.4.refs_1_
  788.1 4.1 place.4
  792.2 3.8 core_swap.3.refs_1_
  796.0 3.8 place.3
  801.0 6.6 reduce-scatter.2.cloned.1.call-done.rows.refs_0_
  807.6 3.8 core_swap.5.refs_1_
  811.4 4.7 place.5
  (179 shorter events, 47.6 us)
Async XLA Ops:
  7.2 242.6 %all-gather.2.cloned.1.call-start = ((), (), s32[]{:S(2)}) async-start(), calls=%async_computation.1 | async-start | bytes 23592960 | tf_op jit(solution)/shard_map/all_gather | solution.py:1189
  11.4 2.0 copy-start.19
  11.4 2.8 copy-start.18
  13.0 7.3 collective-permute-start.1
  15.6 3.1 copy-start.15
  15.8 2.9 collective-permute-start
  24.9 2.5 copy-start.24
  24.9 2.5 copy-start.25
  24.9 2.7 copy-start.16
  24.9 2.7 copy-start.17
  24.9 782.7 %reduce-scatter.2.cloned.1.call-start = ((), (), s32[]{:S(2)}) async-start(), calls=%async_computation.2 | async-start | bytes 15728640 | tf_op jit(solution)/shard_map/reduce_scatter | solution.py:1350
  25.5 6.2 collective-permute-start.2
  479.8 33.7 %copy-start.23 = (bf16[4,96,512]{2,1,0:T(8,128)(2,1)S(1)}, bf16[4,96,512]{2,1,0:T(8,128)(2,1)}, u32[]{:S(2)}) copy-start(bf16[4,96,512]{2,1,0:T(8,128)(2,1)} %get-tuple-element.137) | copy-start | bytes 1179652
  654.8 35.7 %copy-start.26 = (f32[4,512]{1,0:T(4,128)S(1)}, f32[4,512]{1,0:T(4,128)}, u32[]{:S(2)}) copy-start(f32[4,512]{1,0:T(4,128)} %get-tuple-element.160) | copy-start | bytes 24580
  654.8 35.7 %copy-start.28 = (f32[4,512]{1,0:T(4,128)S(1)}, f32[4,512]{1,0:T(4,128)}, u32[]{:S(2)}) copy-start(f32[4,512]{1,0:T(4,128)} %get-tuple-element.161) | copy-start | bytes 24580
  654.8 36.4 %copy-start.31 = (f32[8,128]{1,0:T(8,128)S(1)}, f32[8,128]{1,0:T(8,128)}, u32[]{:S(2)}) copy-start(f32[8,128]{1,0:T(8,128)} %get-tuple-element.166) | copy-start | bytes 12292
  654.8 36.4 %copy-start.32 = (f32[8,128]{1,0:T(8,128)S(1)}, f32[8,128]{1,0:T(8,128)}, u32[]{:S(2)}) copy-start(f32[8,128]{1,0:T(8,128)} %get-tuple-element.167) | copy-start | bytes 12292
  691.9 82.3 %collective-permute-start.3 = (f32[34,128]{1,0:T(8,128)S(1)}, f32[34,128]{1,0:T(8,128)S(1)}, u32[]{:S(2)}, u32[]{:S(2)}) collective-permute-start(f32[34,128]{1,0:T(8,128)S(1)} %maximum_bitcast_fusion.4), channel_id=1, source_target_pairs={{0,2},{2,0},{4,6},{6,4},{8,10},{10,8},{12,14},{14,12},{1,3},{3,1},... | collective-permute-start | bytes 52232 | tf_op jit(solution)/shard_map/ppermute | solution.py:1166
  692.3 56.5 %copy-start.13 = (bf16[4,384,512]{2,1,0:T(8,128)(2,1)S(1)}, bf16[4,384,512]{2,1,0:T(8,128)(2,1)}, u32[]{:S(2)}) copy-start(bf16[4,384,512]{2,1,0:T(8,128)(2,1)} %get-tuple-element.184) | copy-start | bytes 4718596
  748.8 2.3 copy-start.42
  753.7 2.4 copy-start.11
  757.9 2.4 copy-start.2
  757.9 2.9 copy-start.6
  760.9 2.1 copy-start
  760.9 2.4 copy-start.12
  765.1 2.3 copy-start.37
  771.1 3.0 copy-start.4
  771.1 3.0 copy-start.5
  771.1 3.0 copy-start.22
  774.2 3.8 collective-permute-start.4
  778.0 4.3 collective-permute-start.5
  782.3 17.5 %collective-permute-start.6 = (f32[34,128]{1,0:T(8,128)S(1)}, f32[34,128]{1,0:T(8,128)S(1)}, u32[]{:S(2)}, u32[]{:S(2)}) collective-permute-start(f32[34,128]{1,0:T(8,128)S(1)} %add.66), channel_id=1, source_target_pairs={{0,8},{2,10},{4,12},{6,14},{8,0},{10,2},{12,4},{14,6},{1,9},{3,11}... | collective-permute-start | bytes 52232 | tf_op jit(solution)/shard_map/ppermute | solution.py:1420
  (20 other events, 28.3 us)
Sparse Core Ops, SparseCore 0:
  25.0 224.6 all-gather.1
  654.2 153.3 reduce-scatter.1
